TPU v7x, 128 devices: a whole 4x4x4 slice. The times are simulated.
128 devices in a mesh: section: 2 (over x_hi), dp: 16 (over y, z), tensor: 4 (over x_lo, core).
Axes of the slice: x: 4 (x_hi: 2, x_lo: 2; x = x_hi * 2 + x_lo), y: 4, z: 4, core: 2. Of those that a mesh axis runs over, the one named last changes fastest.
Arguments:
- inputs: bfloat16 [2, 2048, 1536], P(None, ('dp', 'tensor')), may hold values from -6 to 6
- cotangent: bfloat16 [2, 2048, 1536], P(None, ('dp', 'tensor')), may hold values from -6 to 6
- segments: int32 [2, 2048], replicated, may hold values from 0 to 7, as said below
- gain_one: bfloat16 [2, 1536], P('section', ('dp', 'tensor')), may hold values from 0.5 to 1.5
- w_query: bfloat16 [2, 1536, 1536], P('section', 'dp', 'tensor'), may hold values from -0.15625 to 0.15625
- b_query: bfloat16 [2, 1536], P('section', 'tensor'), may hold values from -3 to 3
- w_keyval: bfloat16 [2, 1536, 512], P('section', ('dp', 'tensor')), may hold values from -0.15625 to 0.15625
- b_keyval: bfloat16 [2, 512], P('section', ('dp', 'tensor')), may hold values from -3 to 3
- w_out: bfloat16 [2, 1536, 1536], P('section', 'tensor', 'dp'), may hold values from -1.25 to 1.25
- gain_two: bfloat16 [2, 1536], P('section', ('dp', 'tensor')), may hold values from 0.5 to 1.5
- w_gate: bfloat16 [2, 1536, 8960], P('section', 'dp', 'tensor'), may hold values from -0.15625 to 0.15625
- w_up: bfloat16 [2, 1536, 8960], P('section', 'dp', 'tensor'), may hold values from -0.15625 to 0.15625
- w_down: bfloat16 [2, 8960, 1536], P('section', 'tensor', 'dp'), may hold values from -0.0625 to 0.0625
Outputs:
- section_out: bfloat16 [2, 2, 2048, 1536], P('section', None, ('dp', 'tensor'))
- input_grad: bfloat16 [2, 2, 2048, 1536], P('section', None, ('dp', 'tensor'))
- grad_gain_one: float32 [2, 1536], P('section', ('dp', 'tensor'))
- grad_w_query: float32 [2, 1536, 1536], P('section', 'dp', 'tensor')
- grad_b_query: float32 [2, 1536], P('section', 'tensor')
- grad_w_keyval: float32 [2, 1536, 512], P('section', ('dp', 'tensor'))
- grad_b_keyval: float32 [2, 512], P('section', ('dp', 'tensor'))
- grad_w_out: float32 [2, 1536, 1536], P('section', 'tensor', 'dp')
- grad_gain_two: float32 [2, 1536], P('section', ('dp', 'tensor'))
- grad_w_gate: float32 [2, 1536, 8960], P('section', 'dp', 'tensor')
- grad_w_up: float32 [2, 1536, 8960], P('section', 'dp', 'tensor')
- grad_w_down: float32 [2, 8960, 1536], P('section', 'tensor', 'dp')
Inputs may be any that keep to these rules, and one draw needn't show every extreme that they name: `segments`: segment numbers start at 0 and rise by one at each new document. In one micro-batch, drawn from the seed, one document covers the whole sequence; in the others eight documents of 128 to 384 tokens follow one another.
All inputs are finite; a program needn't handle non-finite values.
Results may differ from a plain program's by a relative error of at most 0.025.
Values may be sent and summed in bfloat16 or wider, within the bound.
No kernel may reach another device: no remote copies, remote signals or barrier semaphores. Data moves between devices by JAX's collectives and lax.ppermute only.
A program may use at most 192 MiB of HBM per device.

v0:
```python
import jax
import jax.numpy as jnp
from jax import lax
from jax.sharding import PartitionSpec as P

HQ = 12
KVH = 2
HD = 128


EPS = 1e-06
NEG = -1e30
THETA = 1000000.0


def passed_along(value, axis, steps):
    count = lax.axis_size(axis)
    initial, last = (max(0, -steps), min(count, count - steps))
    return lax.ppermute(value, axis, [(source, source + steps) for source in range(initial, last)])


def rms_rows(values):
    return values * lax.rsqrt(jnp.mean(values * values, axis=-1, keepdims=True) + EPS)


def inverse_rms(values):
    return lax.rsqrt(jnp.mean(values * values, axis=-1, keepdims=True) + EPS)


def rotate(values, cosine, sine_part):
    halfway = values.shape[-1] // 2
    first_half = values[..., :halfway]
    second_half = values[..., halfway:]
    return jnp.concatenate(
        [
            first_half * cosine - second_half * sine_part,
            second_half * cosine + first_half * sine_part,
        ],
        axis=-1,
    )


def rotate_back(values, cosine, sine_part):
    halfway = values.shape[-1] // 2
    first_half = values[..., :halfway]
    second_half = values[..., halfway:]
    return jnp.concatenate(
        [
            first_half * cosine + second_half * sine_part,
            second_half * cosine - first_half * sine_part,
        ],
        axis=-1,
    )


def matmul(left_side, right_side):
    return jnp.dot(left_side, right_side, preferred_element_type=jnp.float32)


def dot_rows(left_side, right_side):
    return lax.dot_general(
        left_side, right_side, (((1,), (1,)), ((), ())), preferred_element_type=jnp.float32
    )


def dot_cols(left_side, right_side):
    return lax.dot_general(
        left_side, right_side, (((0,), (0,)), ((), ())), preferred_element_type=jnp.float32
    )


def spread(values):
    return lax.all_gather(values, "tensor", axis=0, tiled=True)


def collect(values):
    return lax.psum_scatter(
        values.astype(jnp.bfloat16), "tensor", scatter_dimension=0, tiled=True
    ).astype(jnp.float32)


def head_of_device(query_width):
    return lax.axis_index("tensor") * (query_width // HD) // (HQ // KVH)


def fetch_layer(params):
    gain_one, w_query, b_query, w_keyval, b_keyval, w_out, gain_two, w_gate, w_up, w_down = params
    full_query, full_gate, full_up = (
        lax.all_gather(w_query[0], "dp", axis=0, tiled=True),
        lax.all_gather(w_gate[0], "dp", axis=0, tiled=True),
        lax.all_gather(w_up[0], "dp", axis=0, tiled=True),
    )
    full_keyval, full_kvbias, full_gain_one, full_gain_two = (
        lax.all_gather(w_keyval[0], ("dp", "tensor"), axis=0, tiled=True),
        lax.all_gather(b_keyval[0], ("dp", "tensor"), axis=0, tiled=True),
        lax.all_gather(gain_one[0], ("dp", "tensor"), axis=0, tiled=True),
        lax.all_gather(gain_two[0], ("dp", "tensor"), axis=0, tiled=True),
    )
    full_out, full_down = (
        lax.all_gather(w_out[0], "dp", axis=1, tiled=True),
        lax.all_gather(w_down[0], "dp", axis=1, tiled=True),
    )
    head_index = head_of_device(full_query.shape[1])
    key_start = head_index * HD
    value_start = KVH * HD + head_index * HD
    key_w = lax.dynamic_slice_in_dim(full_keyval, key_start, HD, 1)
    value_w = lax.dynamic_slice_in_dim(full_keyval, value_start, HD, 1)
    key_b = lax.dynamic_slice_in_dim(full_kvbias, key_start, HD, 0)
    value_b = lax.dynamic_slice_in_dim(full_kvbias, value_start, HD, 0)
    return (
        full_query,
        b_query[0],
        key_w,
        key_b,
        value_w,
        value_b,
        full_out,
        full_gate,
        full_up,
        full_down,
        full_gain_one.astype(jnp.float32),
        full_gain_two.astype(jnp.float32),
    )


def scores_of(query_rot, key_all, allowed):
    raw_scores = jnp.einsum(
        "qhd,kd->hqk", query_rot, key_all, preferred_element_type=jnp.float32
    ) * HD ** (-0.5)
    return jnp.where(allowed[None], raw_scores, NEG)


def forward_layer(values, allowed, weights, cosine, sine_part):
    (
        full_query,
        bias_query,
        key_w,
        key_b,
        value_w,
        value_b,
        full_out,
        full_gate,
        full_up,
        full_down,
        gain_first,
        gain_second,
    ) = weights
    normed = spread((rms_rows(values) * gain_first).astype(jnp.bfloat16))
    row_count = normed.shape[0]
    heads_local = full_query.shape[1] // HD
    query_pre = matmul(normed, full_query) + bias_query.astype(jnp.float32)
    query_rot = rotate(
        query_pre.reshape(row_count, heads_local, HD), cosine[:, None, :], sine_part[:, None, :]
    ).astype(jnp.bfloat16)
    key_local = rotate(matmul(normed, key_w) + key_b.astype(jnp.float32), cosine, sine_part).astype(
        jnp.bfloat16
    )
    value_local = (matmul(normed, value_w) + value_b.astype(jnp.float32)).astype(jnp.bfloat16)
    key_all, value_all = (
        lax.all_gather(key_local, "dp", axis=0, tiled=True),
        lax.all_gather(value_local, "dp", axis=0, tiled=True),
    )
    scores = scores_of(query_rot, key_all, allowed)
    row_top = jnp.max(scores, axis=-1, keepdims=True)
    weights_exp = jnp.exp(scores - row_top)
    row_total = jnp.sum(weights_exp, axis=-1, keepdims=True)
    probabilities = weights_exp / row_total
    log_total = row_top + jnp.log(row_total)
    attended = jnp.einsum(
        "hqk,kd->qhd",
        probabilities.astype(jnp.bfloat16),
        value_all,
        preferred_element_type=jnp.float32,
    )
    attended = attended.reshape(row_count, heads_local * HD).astype(jnp.bfloat16)
    mixed_rows = values + collect(matmul(attended, full_out))
    second = spread((rms_rows(mixed_rows) * gain_second).astype(jnp.bfloat16))
    gate_proj = matmul(second, full_gate)
    up_proj = matmul(second, full_up)
    hidden = (jax.nn.silu(gate_proj) * up_proj).astype(jnp.bfloat16)
    output = mixed_rows + collect(matmul(hidden, full_down))
    kept_state = (
        values,
        mixed_rows,
        normed,
        query_rot,
        key_all,
        value_all,
        log_total,
        attended,
        second,
        gate_proj,
        up_proj,
        hidden,
    )
    return (output, kept_state)


def backward_layer(grad_out, allowed, kept_state, weights, cosine, sine_part):
    (
        full_query,
        bias_query,
        key_w,
        key_b,
        value_w,
        value_b,
        full_out,
        full_gate,
        full_up,
        full_down,
        gain_first,
        gain_second,
    ) = weights
    (
        values,
        mixed_rows,
        normed,
        query_rot,
        key_all,
        value_all,
        log_total,
        attended,
        second,
        gate_proj,
        up_proj,
        hidden,
    ) = kept_state
    row_count = normed.shape[0]
    heads_local = full_query.shape[1] // HD
    grad_low = spread(grad_out.astype(jnp.bfloat16))
    grad_hidden = dot_rows(grad_low, full_down)
    grad_w_down = dot_cols(hidden, grad_low)
    sigmoid_gate = jax.nn.sigmoid(gate_proj)
    grad_gate = (
        grad_hidden * up_proj * sigmoid_gate * (1.0 + gate_proj * (1.0 - sigmoid_gate))
    ).astype(jnp.bfloat16)
    grad_upper = (grad_hidden * gate_proj * sigmoid_gate).astype(jnp.bfloat16)
    grad_w_gate = dot_cols(second, grad_gate)
    grad_w_up = dot_cols(second, grad_upper)
    grad_second = collect(dot_rows(grad_gate, full_gate) + dot_rows(grad_upper, full_up))
    normed_mixed = rms_rows(mixed_rows)
    grad_gain_second = jnp.sum(grad_second * normed_mixed, axis=0)
    scaled = grad_second * gain_second
    grad_mixed = grad_out + inverse_rms(mixed_rows) * (
        scaled - normed_mixed * jnp.mean(scaled * normed_mixed, axis=-1, keepdims=True)
    )
    grad_att_out = spread(grad_mixed.astype(jnp.bfloat16))
    grad_w_out = dot_cols(attended, grad_att_out)
    grad_attended = (
        dot_rows(grad_att_out, full_out).astype(jnp.bfloat16).reshape(row_count, heads_local, HD)
    )
    probabilities = jnp.exp(scores_of(query_rot, key_all, allowed) - log_total)
    grad_probs = jnp.einsum(
        "qhd,kd->hqk", grad_attended, value_all, preferred_element_type=jnp.float32
    )
    grad_value_all = jnp.einsum(
        "hqk,qhd->kd",
        probabilities.astype(jnp.bfloat16),
        grad_attended,
        preferred_element_type=jnp.float32,
    )
    grad_scores = (
        probabilities * (grad_probs - jnp.sum(probabilities * grad_probs, axis=-1, keepdims=True))
    ).astype(jnp.bfloat16)
    grad_query_rot = jnp.einsum(
        "hqk,kd->qhd", grad_scores, key_all, preferred_element_type=jnp.float32
    ) * HD ** (-0.5)
    grad_key_all = jnp.einsum(
        "hqk,qhd->kd", grad_scores, query_rot, preferred_element_type=jnp.float32
    ) * HD ** (-0.5)
    grad_key_rot, grad_value_sum = (
        lax.psum_scatter(
            grad_key_all.astype(jnp.bfloat16), "dp", scatter_dimension=0, tiled=True
        ).astype(jnp.float32),
        lax.psum_scatter(
            grad_value_all.astype(jnp.bfloat16), "dp", scatter_dimension=0, tiled=True
        ).astype(jnp.float32),
    )
    grad_query = (
        rotate_back(grad_query_rot, cosine[:, None, :], sine_part[:, None, :])
        .reshape(row_count, heads_local * HD)
        .astype(jnp.bfloat16)
    )
    grad_key = rotate_back(grad_key_rot, cosine, sine_part).astype(jnp.bfloat16)
    grad_value = grad_value_sum.astype(jnp.bfloat16)
    grad_w_query = dot_cols(normed, grad_query)
    grad_b_query = jnp.sum(grad_query, axis=0, dtype=jnp.float32)
    grad_w_key = dot_cols(normed, grad_key)
    grad_b_key = jnp.sum(grad_key, axis=0, dtype=jnp.float32)
    grad_w_value = dot_cols(normed, grad_value)
    grad_b_value = jnp.sum(grad_value, axis=0, dtype=jnp.float32)
    grad_normed = collect(
        dot_rows(grad_query, full_query) + dot_rows(grad_key, key_w) + dot_rows(grad_value, value_w)
    )
    normed_values = rms_rows(values)
    grad_gain_first = jnp.sum(grad_normed * normed_values, axis=0)
    scaled_first = grad_normed * gain_first
    grad_values = grad_mixed + inverse_rms(values) * (
        scaled_first
        - normed_values * jnp.mean(scaled_first * normed_values, axis=-1, keepdims=True)
    )
    layer_grads = (
        grad_gain_first,
        grad_w_query,
        grad_b_query,
        grad_w_key,
        grad_b_key,
        grad_w_value,
        grad_b_value,
        grad_w_out,
        grad_gain_second,
        grad_w_gate,
        grad_w_up,
        grad_w_down,
    )
    return (grad_values, layer_grads)


def make_mask(segments_row, local_pos, dp_index, span_rows):
    local_seg = lax.dynamic_slice_in_dim(segments_row, dp_index * span_rows, span_rows, 0)
    key_pos = jnp.arange(segments_row.shape[0], dtype=jnp.int32)
    return (segments_row[None, :] == local_seg[:, None]) & (key_pos[None, :] <= local_pos[:, None])


def local(
    inputs,
    cotangent,
    segments,
    gain_one,
    w_query,
    b_query,
    w_keyval,
    b_keyval,
    w_out,
    gain_two,
    w_gate,
    w_up,
    w_down,
):
    params = (gain_one, w_query, b_query, w_keyval, b_keyval, w_out, gain_two, w_gate, w_up, w_down)
    batches = inputs.shape[0]
    local_rows = inputs.shape[1]
    width = inputs.shape[2]
    seq_len = segments.shape[1]
    span_rows = seq_len // lax.axis_size("dp")
    dp_index = lax.axis_index("dp")
    local_pos = dp_index * span_rows + jnp.arange(span_rows, dtype=jnp.int32)
    inverse_freq = THETA ** (-(jnp.arange(HD // 2, dtype=jnp.float32) * 2.0) / HD)
    angles = local_pos.astype(jnp.float32)[:, None] * inverse_freq[None, :]
    cosine = jnp.cos(angles)
    sine_part = jnp.sin(angles)
    mask_list = [
        make_mask(segments[member], local_pos, dp_index, span_rows) for member in range(batches)
    ]
    first_section = lax.axis_index("section") == 0

    def weights_now():
        return fetch_layer(params)

    def pick(left_side, right_side):
        return jax.tree.map(
            lambda first_one, other_one: jnp.where(first_section, first_one, other_one),
            left_side,
            right_side,
        )

    carried = jnp.zeros((local_rows, width), jnp.bfloat16)
    outs_tick = []
    kept_tick = []
    for moment in range(batches + 1):
        received = passed_along(carried, "section", 1)
        own_batch = min(moment, batches - 1)
        other_batch = max(moment - 1, 0)
        layer_in = jnp.where(first_section, inputs[own_batch], received).astype(jnp.float32)
        allowed = jnp.where(first_section, mask_list[own_batch], mask_list[other_batch])
        output, kept_state = forward_layer(layer_in, allowed, weights_now(), cosine, sine_part)
        carried = output.astype(jnp.bfloat16)
        outs_tick.append(carried)
        kept_tick.append(kept_state)
    section_rows = [pick(outs_tick[member], outs_tick[member + 1]) for member in range(batches)]
    kept_batch = [pick(kept_tick[member], kept_tick[member + 1]) for member in range(batches)]
    grad_totals = None
    carried_grad = jnp.zeros((local_rows, width), jnp.bfloat16)
    grads_tick = []
    for moment in range(batches + 1):
        received = passed_along(carried_grad, "section", -1)
        late_batch = min(moment, batches - 1)
        early_batch = max(moment - 1, 0)
        grad_in = jnp.where(first_section, received, cotangent[late_batch]).astype(jnp.float32)
        allowed = jnp.where(first_section, mask_list[early_batch], mask_list[late_batch])
        kept_state = pick(kept_batch[early_batch], kept_batch[late_batch])
        grad_values, layer_grads = backward_layer(
            grad_in, allowed, kept_state, weights_now(), cosine, sine_part
        )
        is_valid = jnp.where(first_section, moment >= 1, moment < batches)
        layer_grads = jax.tree.map(lambda term: jnp.where(is_valid, term, 0.0), layer_grads)
        if grad_totals is None:
            grad_totals = layer_grads
        else:
            grad_totals = jax.tree.map(
                lambda left_side, right_side: left_side + right_side, grad_totals, layer_grads
            )
        carried_grad = grad_values.astype(jnp.bfloat16)
        grads_tick.append(carried_grad)
    grad_rows = [pick(grads_tick[member + 1], grads_tick[member]) for member in range(batches)]
    (
        total_gain_one,
        total_w_query,
        total_b_query,
        total_w_key,
        total_b_key,
        total_w_value,
        total_b_value,
        total_w_out,
        total_gain_two,
        total_w_gate,
        total_w_up,
        total_w_down,
    ) = grad_totals
    kv_width = w_keyval.shape[2]
    head_index = head_of_device(total_w_query.shape[1])
    key_start = head_index * HD
    value_start = KVH * HD + head_index * HD
    keyval_grad = jnp.zeros((total_w_key.shape[0], kv_width), jnp.float32)
    keyval_grad = lax.dynamic_update_slice_in_dim(keyval_grad, total_w_key, key_start, 1)
    keyval_grad = lax.dynamic_update_slice_in_dim(keyval_grad, total_w_value, value_start, 1)
    kvbias_grad = jnp.zeros((kv_width,), jnp.float32)
    kvbias_grad = lax.dynamic_update_slice_in_dim(kvbias_grad, total_b_key, key_start, 0)
    kvbias_grad = lax.dynamic_update_slice_in_dim(kvbias_grad, total_b_value, value_start, 0)
    shard_query, shard_gate, shard_up = (
        lax.psum_scatter(
            total_w_query.astype(jnp.bfloat16), "dp", scatter_dimension=0, tiled=True
        ).astype(jnp.float32),
        lax.psum_scatter(
            total_w_gate.astype(jnp.bfloat16), "dp", scatter_dimension=0, tiled=True
        ).astype(jnp.float32),
        lax.psum_scatter(
            total_w_up.astype(jnp.bfloat16), "dp", scatter_dimension=0, tiled=True
        ).astype(jnp.float32),
    )
    shard_keyval, shard_kvbias, shard_gain_one, shard_gain_two = (
        lax.psum_scatter(keyval_grad, ("dp", "tensor"), scatter_dimension=0, tiled=True),
        lax.psum_scatter(kvbias_grad, ("dp", "tensor"), scatter_dimension=0, tiled=True),
        lax.psum_scatter(total_gain_one, ("dp", "tensor"), scatter_dimension=0, tiled=True),
        lax.psum_scatter(total_gain_two, ("dp", "tensor"), scatter_dimension=0, tiled=True),
    )
    shard_out, shard_down = (
        lax.psum_scatter(
            total_w_out.astype(jnp.bfloat16), "dp", scatter_dimension=1, tiled=True
        ).astype(jnp.float32),
        lax.psum_scatter(
            total_w_down.astype(jnp.bfloat16), "dp", scatter_dimension=1, tiled=True
        ).astype(jnp.float32),
    )
    summed_bias = lax.psum(total_b_query, "dp")
    section_out = jnp.stack(section_rows)[None]
    input_grad = jnp.stack(grad_rows)[None]
    return (
        section_out,
        input_grad,
        shard_gain_one[None],
        shard_query[None],
        summed_bias[None],
        shard_keyval[None],
        shard_kvbias[None],
        shard_out[None],
        shard_gain_two[None],
        shard_gate[None],
        shard_up[None],
        shard_down[None],
    )


def solution(mesh):
    placed = (
        P(None, ("dp", "tensor"), None),
        P(None, ("dp", "tensor"), None),
        P(),
        P("section", ("dp", "tensor")),
        P("section", "dp", "tensor"),
        P("section", "tensor"),
        P("section", ("dp", "tensor"), None),
        P("section", ("dp", "tensor")),
        P("section", "tensor", "dp"),
        P("section", ("dp", "tensor")),
        P("section", "dp", "tensor"),
        P("section", "dp", "tensor"),
        P("section", "tensor", "dp"),
    )
    return jax.shard_map(
        local,
        mesh=mesh,
        in_specs=placed,
        out_specs=(
            P("section", None, ("dp", "tensor"), None),
            P("section", None, ("dp", "tensor"), None),
            P("section", ("dp", "tensor")),
            P("section", "dp", "tensor"),
            P("section", "tensor"),
            P("section", ("dp", "tensor"), None),
            P("section", ("dp", "tensor")),
            P("section", "tensor", "dp"),
            P("section", ("dp", "tensor")),
            P("section", "dp", "tensor"),
            P("section", "dp", "tensor"),
            P("section", "tensor", "dp"),
        ),
        check_vma=False,
    )
```

profile of v0, /device:TPU:1, one launch (start us, length us, event | category | flops | bytes accessed | tf_op | source)
XLA Modules:
  0.0 2130.1 jit_solution(2629880951833106146)
XLA Ops:
  19.6 143.9 %all-reduce.7 = (bf16[1536]{0:T(1024)(128)(2,1)S(1)}, bf16[512]{0:T(512)(128)(2,1)S(1)}, bf16[1536]{0:T(1024)(128)(2,1)S(1)}) all-reduce(bf16[1536]{0:T(1024)(128)(2,1)S(1)} %dynamic-update-slice, bf16[512]{0:T(512)(128)(2,1)S(1)} %dynamic-update-slice.1, ...), channel_id=2, replica_groups=mesh['section'=2,'dp'=16,'tensor'=4] {'dp','tensor'}, use_global_device_ids=true, to_apply=%add | all-reduce | flops 3584 | bytes 14336
  203.2 18.0 all_gather.58
  228.0 22.1 %reduce-scatter.25.cloned.1.call-done = bf16[32,1536]{1,0:T(8,128)(2,1)} async-done(((bf16[128,1536]{1,0:T(8,128)(2,1)}), bf16[32,1536]{1,0:T(8,128)(2,1)}) %reduce-scatter.25.cloned.1.call-update) | async-done | bytes 98320 | tf_op jit(solution)/shard_map/reduce_scatter | solution.py:77
  259.0 58.8 %all-gather.22.cloned.1.call-done = bf16[1,1536,2240]{2,1,0:T(8,128)(2,1)} async-done(((bf16[1,96,2240]{2,1,0:T(8,128)(2,1)}), bf16[1,1536,2240]{2,1,0:T(8,128)(2,1)}) %all-gather.22.cloned.1.call-update) | async-done | bytes 6881296 | tf_op jit(solution)/shard_map/all_gather | solution.py:90
  323.7 61.1 %all-gather.24.cloned.1.call-done = bf16[1,1536,2240]{2,1,0:T(8,128)(2,1)} async-done(((bf16[1,96,2240]{2,1,0:T(8,128)(2,1)}), bf16[1,1536,2240]{2,1,0:T(8,128)(2,1)}) %all-gather.24.cloned.1.call-update) | async-done | bytes 6881296 | tf_op jit(solution)/shard_map/all_gather | solution.py:91
  391.6 60.2 %all-gather.26.cloned.1.call-done = bf16[1,2240,1536]{1,2,0:T(8,128)(2,1)} async-done(((bf16[1,2240,96]{1,2,0:T(8,128)(2,1)}), bf16[1,2240,1536]{1,2,0:T(8,128)(2,1)}) %all-gather.26.cloned.1.call-update) | async-done | bytes 6881296 | tf_op jit(solution)/shard_map/all_gather | solution.py:101
  493.0 19.0 all_gather.138
  513.5 18.0 all_gather.68
  542.5 18.7 all_gather.144
  594.6 18.4 reduce-scatter.31.cloned.1.call-done
  638.2 19.0 all_gather.142
  658.7 18.1 all_gather.141
  763.6 58.5 %reduce-scatter.39.cloned.1.call-done = bf16[128,128]{1,0:T(8,128)(2,1)} async-done(((bf16[2048,128]{1,0:T(8,128)(2,1)}), bf16[128,128]{1,0:T(8,128)(2,1)}) %reduce-scatter.39.cloned.1.call-update) | async-done | bytes 32784 | tf_op jit(solution)/shard_map/reduce_scatter | solution.py:272
  826.3 70.8 %reduce-scatter.41.cloned.1.call-done = bf16[128,128]{1,0:T(8,128)(2,1)} async-done(((bf16[2048,128]{1,0:T(8,128)(2,1)}), bf16[128,128]{1,0:T(8,128)(2,1)}) %reduce-scatter.41.cloned.1.call-update) | async-done | bytes 32784 | tf_op jit(solution)/shard_map/reduce_scatter | solution.py:275
  900.2 18.7 reduce-scatter.43.cloned.1.call-done
  962.3 19.3 reduce-scatter.45.cloned.1.call-done
  1008.7 64.3 %reduce-scatter.47.cloned.1.call-done = bf16[128,128]{1,0:T(8,128)(2,1)} async-done(((bf16[2048,128]{1,0:T(8,128)(2,1)}), bf16[128,128]{1,0:T(8,128)(2,1)}) %reduce-scatter.47.cloned.1.call-update) | async-done | bytes 32784 | tf_op jit(solution)/shard_map/reduce_scatter | solution.py:272
  1076.3 71.7 %reduce-scatter.49.cloned.1.call-done = bf16[128,128]{1,0:T(8,128)(2,1)} async-done(((bf16[2048,128]{1,0:T(8,128)(2,1)}), bf16[128,128]{1,0:T(8,128)(2,1)}) %reduce-scatter.49.cloned.1.call-update) | async-done | bytes 32784 | tf_op jit(solution)/shard_map/reduce_scatter | solution.py:275
  1150.5 19.0 reduce-scatter.51.cloned.1.call-done
  1245.5 64.2 %reduce-scatter.55.cloned.1.call-done = bf16[128,128]{1,0:T(8,128)(2,1)} async-done(((bf16[2048,128]{1,0:T(8,128)(2,1)}), bf16[128,128]{1,0:T(8,128)(2,1)}) %reduce-scatter.55.cloned.1.call-update) | async-done | bytes 32784 | tf_op jit(solution)/shard_map/reduce_scatter | solution.py:272
  1313.8 71.2 %reduce-scatter.57.cloned.1.call-done = bf16[128,128]{1,0:T(8,128)(2,1)} async-done(((bf16[2048,128]{1,0:T(8,128)(2,1)}), bf16[128,128]{1,0:T(8,128)(2,1)}) %reduce-scatter.57.cloned.1.call-update) | async-done | bytes 32784 | tf_op jit(solution)/shard_map/reduce_scatter | solution.py:275
  1498.7 31.4 %psum.7 = f32[1,384]{1,0:T(1,128)} all-reduce(f32[1,384]{1,0:T(1,128)S(1)} %bitcast.477), channel_id=1, replica_groups=mesh['section'=2,'dp'=16,'tensor'=4] {'dp'}, use_global_device_ids=true, to_apply=%region_53.54 | all-reduce | flops 384 | bytes 3072 | tf_op jit(solution)/shard_map/psum | solution.py:455
  1531.6 281.5 %all-reduce.6 = (f32[1536]{0:T(1024)S(1)}, f32[512]{0:T(512)S(1)}, f32[1536]{0:T(1024)S(1)}) all-reduce(f32[1536]{0:T(1024)S(1)} %select_add_fusion.1, f32[512]{0:T(512)S(1)} %fusion.335, f32[1536]{0:T(1024)S(1)} %select_add_fusion), channel_id=29, replica_groups=mesh['section'=2,'dp'=16,'tensor'=4] {'dp','tensor'}, use_global_device_ids=true, to_apply=%region_48.49.clone | all-reduce | flops 3584 | bytes 28672
  1838.8 284.3 %reduce-scatter.63.cloned.1.call-done = f32[24,512]{1,0:T(8,128)} async-done(((f32[1536,512]{1,0:T(8,128)}), f32[24,512]{1,0:T(8,128)}) %reduce-scatter.63.cloned.1.call-update) | async-done | bytes 49168 | tf_op jit(solution)/shard_map/reduce_scatter | solution.py:442
  (713 shorter events, 579.5 us)
Async XLA Ops:
  7.2 173.1 %all-gather.18.cloned.1.call-start = ((), (), s32[]{:S(2)}) async-start(), calls=%async_computation.49 | async-start | bytes 1253376 | tf_op jit(solution)/shard_map/all_gather | solution.py:89
  7.9 174.6 %all-gather.16.cloned.1.call-start = ((), (), s32[]{:S(2)}) async-start(), calls=%async_computation.48 | async-start | bytes 1597440 | tf_op jit(solution)/shard_map/all_gather | solution.py:94
  8.7 214.7 %all-gather.20.cloned.1.call-start = ((), (), s32[]{:S(2)}) async-start(), calls=%async_computation.50 | async-start | bytes 1253376 | tf_op jit(solution)/shard_map/all_gather | solution.py:100
  8.7 158.6 %collective-permute-start = (bf16[32,1536]{1,0:T(8,128)(2,1)S(1)}, bf16[32,1536]{1,0:T(8,128)(2,1)S(1)}, u32[]{:S(2)}, u32[]{:S(2)}) collective-permute-start(bf16[32,1536]{1,0:T(8,128)(2,1)S(1)} %broadcast.444), channel_id=1, source_target_pairs={{0,64},{1,65},{2,66},{3,67},{4,68},{5,69},{6,70},{7,71},{8,72},{9,... | collective-permute-start | bytes 294920 | tf_op jit(solution)/shard_map/ppermute | solution.py:19
  14.3 235.8 %reduce-scatter.25.cloned.1.call-start = ((), (), s32[]{:S(2)}) async-start(), calls=%async_computation.24 | async-start | bytes 491520 | tf_op jit(solution)/shard_map/reduce_scatter | solution.py:77
  226.6 158.1 %all-gather.24.cloned.1.call-start = ((), (), s32[]{:S(2)}) async-start(), calls=%async_computation.52 | async-start | bytes 7520256 | tf_op jit(solution)/shard_map/all_gather | solution.py:91
  227.2 224.6 %all-gather.26.cloned.1.call-start = ((), (), s32[]{:S(2)}) async-start(), calls=%async_computation.53 | async-start | bytes 7520256 | tf_op jit(solution)/shard_map/all_gather | solution.py:101
  227.9 248.1 %reduce-scatter.27.cloned.1.call-start = ((), (), s32[]{:S(2)}) async-start(), calls=%async_computation.25 | async-start | bytes 491520 | tf_op jit(solution)/shard_map/reduce_scatter | solution.py:77
  594.6 115.2 %reduce-scatter.33.cloned.1.call-start = ((), (), s32[]{:S(2)}) async-start(), calls=%async_computation.28 | async-start | bytes 491520 | tf_op jit(solution)/shard_map/reduce_scatter | solution.py:77
  694.1 128.0 %reduce-scatter.39.cloned.1.call-start = ((), (), s32[]{:S(2)}) async-start(), calls=%async_computation.31 | async-start | bytes 557056 | tf_op jit(solution)/shard_map/reduce_scatter | solution.py:272
  750.7 146.5 %reduce-scatter.41.cloned.1.call-start = ((), (), s32[]{:S(2)}) async-start(), calls=%async_computation.32 | async-start | bytes 557056 | tf_op jit(solution)/shard_map/reduce_scatter | solution.py:275
  757.1 161.8 %reduce-scatter.43.cloned.1.call-start = ((), (), s32[]{:S(2)}) async-start(), calls=%async_computation.33 | async-start | bytes 491520 | tf_op jit(solution)/shard_map/reduce_scatter | solution.py:77
  962.2 110.8 %reduce-scatter.47.cloned.1.call-start = ((), (), s32[]{:S(2)}) async-start(), calls=%async_computation.35 | async-start | bytes 557056 | tf_op jit(solution)/shard_map/reduce_scatter | solution.py:272
  1001.5 146.4 %reduce-scatter.49.cloned.1.call-start = ((), (), s32[]{:S(2)}) async-start(), calls=%async_computation.36 | async-start | bytes 557056 | tf_op jit(solution)/shard_map/reduce_scatter | solution.py:275
  1007.1 162.5 %reduce-scatter.51.cloned.1.call-start = ((), (), s32[]{:S(2)}) async-start(), calls=%async_computation.37 | async-start | bytes 491520 | tf_op jit(solution)/shard_map/reduce_scatter | solution.py:77
  1238.2 146.7 %reduce-scatter.57.cloned.1.call-start = ((), (), s32[]{:S(2)}) async-start(), calls=%async_computation.40 | async-start | bytes 557056 | tf_op jit(solution)/shard_map/reduce_scatter | solution.py:275
  1243.1 287.4 %reduce-scatter.59.cloned.1.call-start = ((), (), s32[]{:S(2)}) async-start(), calls=%async_computation.41 | async-start | bytes 491520 | tf_op jit(solution)/shard_map/reduce_scatter | solution.py:77
  1387.2 427.7 %reduce-scatter.35.cloned.1.call-start = ((), (), s32[]{:S(2)}) async-start(), calls=%async_computation.29 | async-start | bytes 491520 | tf_op jit(solution)/shard_map/reduce_scatter | solution.py:77
  1393.9 423.6 %reduce-scatter.61.cloned.1.call-start = ((), (), s32[]{:S(2)}) async-start(), calls=%async_computation.42 | async-start | bytes 1253376 | tf_op jit(solution)/shard_map/reduce_scatter | solution.py:431
  1396.8 422.2 %reduce-scatter.65.cloned.1.call-start = ((), (), s32[]{:S(2)}) async-start(), calls=%async_computation.44 | async-start | bytes 1253376 | tf_op jit(solution)/shard_map/reduce_scatter | solution.py:448
  1401.9 418.7 %reduce-scatter.67.cloned.1.call-start = ((), (), s32[]{:S(2)}) async-start(), calls=%async_computation.45 | async-start | bytes 7520256 | tf_op jit(solution)/shard_map/reduce_scatter | solution.py:434
  1430.8 391.8 %reduce-scatter.69.cloned.1.call-start = ((), (), s32[]{:S(2)}) async-start(), calls=%async_computation.46 | async-start | bytes 7520256 | tf_op jit(solution)/shard_map/reduce_scatter | solution.py:437
  1460.1 376.7 %reduce-scatter.71.cloned.1.call-start = ((), (), s32[]{:S(2)}) async-start(), calls=%async_computation.47 | async-start | bytes 7520256 | tf_op jit(solution)/shard_map/reduce_scatter | solution.py:451
  1490.0 633.1 %reduce-scatter.63.cloned.1.call-start = ((), (), s32[]{:S(2)}) async-start(), calls=%async_computation.43 | async-start | bytes 3194880 | tf_op jit(solution)/shard_map/reduce_scatter | solution.py:442
  (204 other events, 11062.8 us)
Sparse Core Ops, SparseCore 0:
  10.2 45.7 all-gather.17
  57.7 103.2 all-gather.15
  163.1 41.3 all-gather.19
  226.1 23.8 reduce-scatter.24
  252.3 65.4 all-gather.21
  320.1 64.6 all-gather.23
  387.1 64.6 all-gather.25
  535.6 28.1 reduce-scatter.28
  682.1 27.6 reduce-scatter.32
  750.8 71.2 reduce-scatter.38
  825.5 71.5 reduce-scatter.40
  900.0 18.9 reduce-scatter.42
  962.3 19.1 reduce-scatter.44
  1001.7 71.2 reduce-scatter.46
  1076.4 71.5 reduce-scatter.48
  1150.6 18.9 reduce-scatter.50
  1238.3 71.3 reduce-scatter.54
  1313.2 71.6 reduce-scatter.56
  1431.1 72.3 reduce-scatter.60
  1506.5 72.6 reduce-scatter.64
  1582.5 82.5 reduce-scatter.66
  1669.0 82.3 reduce-scatter.68
  1754.8 81.9 reduce-scatter.70
  1839.7 283.3 reduce-scatter.62
  (6 shorter events, 108.5 us)
where the time goes:
time: 2140 us; the launch traced here: 2130 us
  waiting for transfers between devices  1060 us (50%)
  blocking collectives  666 us (31%)
  matrix products  263 us (12%)
  other arithmetic  63.4 us (3%)
  local copies, waits for them, and re-layouts  37.6 us (2%)
    unnamed x2, blocking collectives  425 us
    reduce_scatter x1, waiting for transfers between devices, local(): lax.psum_scatter(keyval_grad, ('dp', 'tensor'), scatter_dimension=0, tile...  284 us
    reduce_scatter x3, waiting for transfers between devices, backward_layer(): lax.psum_scatter(grad_value_all.astype(jnp.bfloat16), 'dp', scatter_dimen...  214 us
    reduce_scatter x3, waiting for transfers between devices, backward_layer(): lax.psum_scatter(grad_key_all.astype(jnp.bfloat16), 'dp', scatter_dimensi...  187 us
    reduce_scatter x12, waiting for transfers between devices, collect(): lax.psum_scatter(values.astype(jnp.bfloat16), 'tensor', scatter_dimension...  165 us
    all_gather x12, blocking collectives, spread(): return lax.all_gather(values, 'tensor', axis=0, tiled=True)  99.4 us
    dot_general x21, matrix products, dot_cols(): lax.dot_general(left_side, right_side, (((0,), (0,)), ((), ())), preferre...  96.1 us
    dot_general x21, matrix products, matmul(): return jnp.dot(left_side, right_side, preferred_element_type=jnp.float32)  68.7 us
  transfers between devices with their start and end apart: 36, of which 25 were waited for; matrix products, arithmetic and copies ran while one was open for 10% of the time, Pallas kernels for 0%

commit v1 on v0

v1 whole, which is shorter than its diff:
```python
import jax
import jax.numpy as jnp
import numpy as np
from jax import lax
from jax.sharding import Mesh
from jax.sharding import PartitionSpec as P

HEAD = 128
EPS = 1e-06
NEG = -1e30
THETA = 1000000.0
WIDTH = 1536
QCOLS = 384
LOCAL_FF = 560
PAD_FF = 640
AXES = ("s", "y", "z", "x", "c")
BLOCK_ORDER = (0, 2, 1, 3)
BF = jnp.bfloat16
F32 = jnp.float32


def swap(value, axis):
    return lax.ppermute(value, axis, [(0, 1), (1, 0)])


def exchange(value, axes):
    return lax.all_to_all(value, axes, split_axis=0, concat_axis=0, tiled=True)


def nn(left, right):
    return jnp.dot(left, right, preferred_element_type=F32)


def nt(left, right):
    return lax.dot_general(left, right, (((1,), (1,)), ((), ())), preferred_element_type=F32)


def tn(left, right):
    return lax.dot_general(left, right, (((0,), (0,)), ((), ())), preferred_element_type=F32)


def inverse_rms(values):
    return lax.rsqrt(jnp.mean(values * values, axis=-1, keepdims=True) + EPS)


def halves_swapped(values):
    half = HEAD // 2
    return jnp.concatenate([values[..., half:], values[..., :half]], axis=-1)


def rotate(values, cosine, sine):
    return values * cosine + halves_swapped(values) * sine


def rotate_back(values, cosine, sine):
    return values * cosine - halves_swapped(values) * sine


def gather_block(rows):
    count = 8
    mine = exchange(jnp.broadcast_to(rows[None], (count,) + rows.shape), ("z", "x"))
    mine = mine.reshape(count * rows.shape[0], rows.shape[1])
    return jnp.concatenate([mine, swap(mine, "c")], axis=0)


def scatter_block(part):
    half = part.shape[0] // 2
    given = swap(part[half:].astype(BF), "c")
    joined = (part[:half] + given.astype(F32)).astype(BF)
    pieces = exchange(joined.reshape(8, half // 8, part.shape[1]), ("z", "x"))
    return jnp.sum(pieces.astype(F32), axis=0)


def scatter_heads(part):
    pieces = exchange(part.astype(BF).reshape(4, part.shape[0] // 4, part.shape[1]), ("x", "c"))
    return jnp.sum(pieces.astype(F32), axis=0)


def forward_layer(xin, weights, allowed, cosine, sine, is_key):
    attn, ffn, gain_one, gain_two, bias = weights
    normed_local = (xin * inverse_rms(xin) * gain_one).astype(BF)
    normed = lax.all_gather(normed_local, ("x", "c"), axis=0, tiled=True)
    qkv = nn(normed, attn[:, :512]) + bias
    rows = normed.shape[0]
    query = rotate(qkv[:, :QCOLS].reshape(rows, 3, HEAD), cosine[:, None], sine[:, None]).astype(BF)
    query = query.transpose(1, 0, 2).reshape(3 * rows, HEAD)
    kv = qkv[:, QCOLS:]
    kv = jnp.where(is_key, rotate(kv, cosine, sine), kv).astype(BF)
    kv_mine = exchange(jnp.broadcast_to(kv[None], (16, rows, HEAD)), ("y", "z")).reshape(16 * rows, HEAD)
    kv_other = swap(kv_mine, "c")
    key = jnp.where(is_key, kv_mine, kv_other)
    value = jnp.where(is_key, kv_other, kv_mine)
    scores = nt(query, key).reshape(3, rows, -1) * HEAD**-0.5
    scores = jnp.where(allowed[None], scores, NEG)
    top = jnp.max(scores, axis=-1, keepdims=True)
    raised = jnp.exp(scores - top)
    total = jnp.sum(raised, axis=-1, keepdims=True)
    probs = (raised / total).astype(BF).reshape(3 * rows, -1)
    lse = top + jnp.log(total)
    attended = nn(probs, value).astype(BF)
    attended = attended.reshape(3, rows, HEAD).transpose(1, 0, 2).reshape(rows, QCOLS)
    mixed = xin + scatter_heads(nt(attended, attn[:, 512:]))
    second_local = (mixed * inverse_rms(mixed) * gain_two).astype(BF)
    second = gather_block(second_local)
    gate = nn(second, ffn[:, :PAD_FF])
    up = nn(second, ffn[:, PAD_FF : 2 * PAD_FF])
    hidden = (jax.nn.silu(gate) * up).astype(BF)
    output = mixed + scatter_block(nt(hidden, ffn[:, 2 * PAD_FF :]))
    kept = (xin, mixed, normed, query, key, value, lse, attended, second, gate, up, hidden)
    return output, kept


def backward_layer(grad_out, weights, kept, allowed, cosine, sine, is_key):
    attn, ffn, gain_one, gain_two, bias = weights
    xin, mixed, normed, query, key, value, lse, attended, second, gate, up, hidden = kept
    rows = normed.shape[0]
    grad_low = gather_block(grad_out)
    grad_hidden = nn(grad_low, ffn[:, 2 * PAD_FF :])
    sig = jax.nn.sigmoid(gate)
    grad_gate = (grad_hidden * up * sig * (1.0 + gate * (1.0 - sig))).astype(BF)
    grad_up = (grad_hidden * gate * sig).astype(BF)
    grad_second = scatter_block(nt(grad_gate, ffn[:, :PAD_FF]) + nt(grad_up, ffn[:, PAD_FF : 2 * PAD_FF]))
    grad_ffn = jnp.concatenate(
        [tn(second, grad_gate).astype(BF), tn(second, grad_up).astype(BF), tn(grad_low, hidden).astype(BF)], axis=1
    )
    inv = inverse_rms(mixed)
    norm_mixed = mixed * inv
    grad_gain_two = jnp.sum(grad_second * norm_mixed, axis=0)
    scaled = grad_second * gain_two
    grad_mixed = grad_out.astype(F32) + inv * (
        scaled - norm_mixed * jnp.mean(scaled * norm_mixed, axis=-1, keepdims=True)
    )
    grad_att = lax.all_gather(grad_mixed.astype(BF), ("x", "c"), axis=0, tiled=True)
    grad_out_t = tn(grad_att, attended)
    grad_attended = nn(grad_att, attn[:, 512:]).astype(BF)
    grad_attended = grad_attended.reshape(rows, 3, HEAD).transpose(1, 0, 2).reshape(3 * rows, HEAD)
    scores = nt(query, key).reshape(3, rows, -1) * HEAD**-0.5
    probs = jnp.exp(jnp.where(allowed[None], scores, NEG) - lse).reshape(3 * rows, -1)
    grad_probs = nt(grad_attended, value)
    grad_value = tn(probs.astype(BF), grad_attended)
    grad_scores = (probs * (grad_probs - jnp.sum(probs * grad_probs, axis=-1, keepdims=True))).astype(BF)
    grad_query = nn(grad_scores, key) * HEAD**-0.5
    grad_key = tn(grad_scores, query) * HEAD**-0.5
    kept_half = jnp.where(is_key, grad_key, grad_value)
    sent_half = jnp.where(is_key, grad_value, grad_key).astype(BF)
    grad_kv = (kept_half + swap(sent_half, "c").astype(F32)).astype(BF)
    grad_kv = jnp.sum(exchange(grad_kv.reshape(16, rows, HEAD), ("y", "z")).astype(F32), axis=0)
    grad_kv = jnp.where(is_key, rotate_back(grad_kv, cosine, sine), grad_kv).astype(BF)
    grad_query = rotate_back(grad_query.reshape(3, rows, HEAD), cosine[None], sine[None]).astype(BF)
    grad_query = grad_query.transpose(1, 0, 2).reshape(rows, QCOLS)
    grad_qkv = jnp.concatenate([grad_query, grad_kv], axis=1)
    grad_w_qkv = tn(normed, grad_qkv)
    grad_bias = jnp.sum(grad_qkv, axis=0, dtype=F32)
    grad_normed = scatter_heads(nt(grad_qkv, attn[:, :512]))
    inv_one = inverse_rms(xin)
    norm_one = xin * inv_one
    grad_gain_one = jnp.sum(grad_normed * norm_one, axis=0)
    scaled_one = grad_normed * gain_one
    grad_in = grad_mixed + inv_one * (
        scaled_one - norm_one * jnp.mean(scaled_one * norm_one, axis=-1, keepdims=True)
    )
    grad_attn = jnp.concatenate([grad_w_qkv, grad_out_t], axis=1).astype(BF).reshape(16, 96, 896)
    small = jnp.concatenate(
        [
            jnp.broadcast_to(grad_bias[None], (16, 512)),
            grad_gain_one.reshape(16, 96),
            grad_gain_two.reshape(16, 96),
            jnp.zeros((16, 192), F32),
        ],
        axis=1,
    ).astype(BF)
    grad_attn = jnp.concatenate([grad_attn, small[:, None], jnp.zeros((16, 15, 896), BF)], axis=1)
    return grad_in, grad_attn.reshape(16 * 112, 896), grad_ffn


def local(
    inputs, cotangent, segments, gain_one, w_query, b_query, w_keyval, b_keyval, w_out, gain_two, w_gate, w_up, w_down
):
    on_first = lax.axis_index("s") == 0
    is_key = lax.axis_index("c") == 0
    block = lax.axis_index("y") * 4 + lax.axis_index("z")
    member = lax.axis_index("x") * 2 + lax.axis_index("c")

    def pick(first, second):
        return jnp.where(on_first, first, second)

    small = jnp.concatenate([gain_one[0], gain_two[0], b_keyval[0], jnp.zeros((72,), BF)])
    kv_blocks = w_keyval[0].reshape(24, 4, HEAD).transpose(1, 0, 2)
    kv_blocks = jnp.stack([kv_blocks[b] for b in BLOCK_ORDER])
    payload = jnp.concatenate(
        [kv_blocks, jnp.broadcast_to(small[None, None], (4, 1, HEAD)), jnp.zeros((4, 7, HEAD), BF)], axis=1
    )
    payload = exchange(payload, ("x", "c"))
    kv_rows = payload[:, :24].reshape(96, HEAD)
    small_row = jnp.concatenate([payload[:, 24, :56].reshape(224), jnp.zeros((288,), BF), b_query[0]])
    attn_own = jnp.concatenate(
        [
            jnp.concatenate([w_query[0], kv_rows, w_out[0].T], axis=1),
            small_row[None],
            jnp.zeros((15, 896), BF),
        ],
        axis=0,
    )
    attn_other = swap(attn_own, "s")

    stacked = jnp.stack([w_gate[0], w_up[0], w_down[0].T], axis=1).reshape(96, 3, 4, LOCAL_FF)
    stacked = jnp.pad(stacked, ((0, 0), (0, 0), (0, 0), (0, PAD_FF - LOCAL_FF)))
    ffn_own = exchange(stacked.transpose(2, 0, 1, 3).reshape(4, 96, 3 * PAD_FF), "z").reshape(384, 3 * PAD_FF)
    ffn_other = swap(ffn_own, "s")

    def attn_weights(piece):
        whole = lax.all_gather(piece, ("y", "z"), axis=0, tiled=True).reshape(16, 112, 896)
        matrix = whole[:, :96].reshape(WIDTH, 896)
        row = whole[:, 96]
        bits = row[:, :224].reshape(64, 56)
        gain_a = bits[:, :24].reshape(WIDTH).astype(F32)
        gain_b = bits[:, 24:48].reshape(WIDTH).astype(F32)
        kv_bias = lax.dynamic_slice_in_dim(
            bits[:, 48:].reshape(512), (lax.axis_index("c") * 2 + lax.axis_index("x")) * HEAD, HEAD, 0
        )
        bias = jnp.concatenate([row[0, 512:], kv_bias]).astype(F32)
        return matrix, gain_a, gain_b, bias

    def ffn_weights(piece):
        return lax.all_gather(piece, "y", axis=0, tiled=True)

    layers = []
    for layer in range(2):
        a_piece = pick(attn_own, attn_other) if layer == 0 else pick(attn_other, attn_own)
        f_piece = pick(ffn_own, ffn_other) if layer == 0 else pick(ffn_other, ffn_own)
        matrix, gain_a, gain_b, bias = attn_weights(a_piece)
        layers.append((matrix, ffn_weights(f_piece), gain_a, gain_b, bias))

    rows = 128
    seq = segments.shape[1]
    seg = pick(segments[0], segments[1])
    local_pos = block * rows + jnp.arange(rows, dtype=jnp.int32)
    inverse_freq = THETA ** (-(jnp.arange(HEAD // 2, dtype=F32) * 2.0) / HEAD)
    angles = local_pos.astype(F32)[:, None] * inverse_freq[None, :]
    cosine = jnp.cos(angles)
    sine = jnp.sin(angles)
    cosine = jnp.concatenate([cosine, cosine], axis=1)
    sine = jnp.concatenate([-sine, sine], axis=1)
    local_seg = lax.dynamic_slice_in_dim(seg, block * rows, rows, 0)
    key_pos = jnp.arange(seq, dtype=jnp.int32)
    allowed = (seg[None, :] == local_seg[:, None]) & (key_pos[None, :] <= local_pos[:, None])

    xin = pick(inputs[0], inputs[1]).astype(F32)
    out_one, kept_one = forward_layer(xin, layers[0], allowed, cosine, sine, is_key)
    out_one = out_one.astype(BF)
    out_two, kept_two = forward_layer(out_one.astype(F32), layers[1], allowed, cosine, sine, is_key)
    out_two = out_two.astype(BF)
    cot = pick(cotangent[0], cotangent[1])
    grad_two, attn_two, ffn_two = backward_layer(cot, layers[1], kept_two, allowed, cosine, sine, is_key)
    grad_two = grad_two.astype(BF)
    attn_two = lax.psum_scatter(attn_two, ("y", "z"), scatter_dimension=0, tiled=True)
    ffn_two = lax.psum_scatter(ffn_two, "y", scatter_dimension=0, tiled=True)
    grad_one, attn_one, ffn_one = backward_layer(grad_two, layers[0], kept_one, allowed, cosine, sine, is_key)
    grad_one = grad_one.astype(BF)
    attn_one = lax.psum_scatter(attn_one, ("y", "z"), scatter_dimension=0, tiled=True)
    ffn_one = lax.psum_scatter(ffn_one, "y", scatter_dimension=0, tiled=True)

    def across(first, second):
        return pick(first, second).astype(F32) + (
            lax.ppermute(second, "s", [(0, 1)]).astype(F32) + lax.ppermute(first, "s", [(1, 0)]).astype(F32)
        )

    attn_sum = across(attn_one, attn_two)
    ffn_sum = across(ffn_one, ffn_two)

    pieces = exchange(ffn_sum.astype(BF).reshape(4, 96, 3 * PAD_FF), "z").astype(F32)
    pieces = pieces.reshape(4, 96, 3, PAD_FF)[..., :LOCAL_FF]
    grad_gate = pieces[:, :, 0].transpose(1, 0, 2).reshape(96, 4 * LOCAL_FF)
    grad_up = pieces[:, :, 1].transpose(1, 0, 2).reshape(96, 4 * LOCAL_FF)
    grad_down = pieces[:, :, 2].transpose(0, 2, 1).reshape(4 * LOCAL_FF, 96)

    grad_query = attn_sum[:96, :QCOLS]
    grad_w_out = attn_sum[:96, 512:].T
    grad_row = attn_sum[96]
    grad_b_query = grad_row[:QCOLS]
    kv_bias_row = grad_row[QCOLS:512]
    gains = jnp.concatenate([grad_row[512:608].reshape(4, 24), grad_row[608:704].reshape(4, 24)], axis=1)
    payload = jnp.concatenate(
        [
            attn_sum[:96, QCOLS:512].reshape(4, 24, HEAD),
            jnp.pad(gains, ((0, 0), (0, HEAD - 48)))[:, None],
            jnp.broadcast_to(kv_bias_row[None, None], (4, 1, HEAD)),
            jnp.zeros((4, 6, HEAD), F32),
        ],
        axis=1,
    )
    payload = exchange(payload, ("x", "c"))
    payload = jnp.stack([payload[b] for b in BLOCK_ORDER])
    grad_keyval = payload[:, :24].transpose(1, 0, 2).reshape(24, 512)
    gains = jnp.sum(payload[:, 24], axis=0)
    kv_bias_row = lax.dynamic_index_in_dim(payload[:, 25], lax.axis_index("y"), 0, keepdims=False)
    grad_b_keyval = lax.dynamic_slice_in_dim(kv_bias_row, (lax.axis_index("z") * 4 + member) * 8, 8, 0)

    def both(first, second):
        given = swap(pick(second, first), "s")
        return jnp.stack([pick(first, given), pick(given, second)])[None]

    return (
        both(out_one, out_two),
        both(grad_one, grad_two),
        gains[None, :24],
        grad_query[None],
        grad_b_query[None],
        grad_keyval[None],
        grad_b_keyval[None],
        grad_w_out[None],
        gains[None, 24:48],
        grad_gate[None],
        grad_up[None],
        grad_down[None],
    )


def solution(mesh):
    fine = Mesh(np.asarray(mesh.devices).reshape(2, 4, 4, 2, 2), AXES)
    block, member = ("y", "z"), ("x", "c")
    every = block + member
    tokens = P(None, every, None)
    split = P("s", every)
    columns = P("s", block, member)
    rows = P("s", member, block)
    keyval = P("s", every, None)
    outs = P("s", None, every, None)
    return jax.shard_map(
        local,
        mesh=fine,
        in_specs=(
            tokens, tokens, P(), split, columns, P("s", member), keyval, split, rows, split, columns, columns, rows,
        ),
        out_specs=(
            outs, outs, split, columns, P("s", member), keyval, split, rows, split, columns, columns, rows,
        ),
        check_vma=False,
    )
```

time: 2140 us -> 825 us (0.39)
  waiting for transfers between devices: 1060 us -> 293 us
  blocking collectives: 666 us -> 132 us
  matrix products: 263 us -> 92.1 us
  starting transfers between devices: 20.1 us -> 97.8 us
  local copies, waits for them, and re-layouts: 37.6 us -> 105 us
    reduce_scatter x24 -> x2, waiting for transfers between devices: 862 us -> 0.02 us  [the longest x1 0.02 us: local(): ffn_one = lax.psum_scatter(ffn_one, 'y', scatter_dimension=0, tiled=True)]
    unnamed x2 -> x0, blocking collectives: 425 us -> none
    all_gather x18 -> x4, blocking collectives: 209 us -> 30.4 us  [the longest x2 15.9 us: forward_layer(): normed = lax.all_gather(normed_local, ('x', 'c'), axis=0, tiled=True)]
    dot_general x84 -> x42, matrix products: 263 us -> 92.1 us  [the longest x14 36.9 us: nn(): return jnp.dot(left, right, preferred_element_type=F32)]
    all_gather x6 -> x4, waiting for transfers between devices: 180 us -> 25.8 us  [the longest x2 25.8 us: attn_weights(): lax.all_gather(piece, ('y', 'z'), axis=0, tiled=True).reshape(16, 112, 896)]
    unnamed x30 -> x10, waiting for transfers between devices: 3.54 us -> 123 us
    all_to_all x0 -> x6, blocking collectives: none -> 101 us  [exchange(): return lax.all_to_all(value, axes, split_axis=0, concat_axis=0, tiled=True)]
    all_to_all x0 -> x14, waiting for transfers between devices: none -> 92.6 us  [exchange(): return lax.all_to_all(value, axes, split_axis=0, concat_axis=0, tiled=True)]
  transfers between devices with their start and end apart: 36 -> 42, of which waited for: 25 -> 25; matrix products, arithmetic and copies ran while one was open for 10% -> 28% of each run, Pallas kernels for 0% -> 0%
where the time goes in v1:
time: 825 us; the launch traced here: 812 us
  waiting for transfers between devices  293 us (36%)
  blocking collectives  132 us (16%)
  local copies, waits for them, and re-layouts  105 us (13%)
  starting transfers between devices  97.8 us (12%)
  matrix products  92.1 us (11%)
  other arithmetic  75.2 us (9%)
  between operations  16.4 us (2%)
    unnamed x10, waiting for transfers between devices  123 us
    all_to_all x6, blocking collectives, exchange(): return lax.all_to_all(value, axes, split_axis=0, concat_axis=0, tiled=True)  101 us
    all_to_all x14, waiting for transfers between devices, exchange(): return lax.all_to_all(value, axes, split_axis=0, concat_axis=0, tiled=True)  92.6 us
    all_to_all x14, starting transfers between devices, exchange(): return lax.all_to_all(value, axes, split_axis=0, concat_axis=0, tiled=True)  62.4 us
    ppermute x16, waiting for transfers between devices, swap(): return lax.ppermute(value, axis, [(0, 1), (1, 0)])  50 us
    dot_general x14, matrix products, nn(): return jnp.dot(left, right, preferred_element_type=F32)  36.9 us
    dot_general x14, matrix products, nt(): lax.dot_general(left, right, (((1,), (1,)), ((), ())), preferred_element_...  31.1 us
    unnamed x207, local copies, waits for them, and re-layouts  28.2 us
  transfers between devices with their start and end apart: 42, of which 25 were waited for; matrix products, arithmetic and copies ran while one was open for 28% of the time, Pallas kernels for 0%

profile of v1, /device:TPU:1, one launch (start us, length us, event | category | flops | bytes accessed | tf_op | source)
XLA Modules:
  0.0 811.7 jit_solution(3150137863121430646)
XLA Ops:
  41.1 25.6 %all_to_all.100 = bf16[4,96,1920]{2,1,0:T(8,128)(2,1)S(1)} all-to-all(bf16[4,96,1920]{2,1,0:T(8,128)(2,1)} %reshape.706), channel_id=1, replica_groups=mesh['s'=2,'y'=4,'z'=4,'x'=2,'c'=2] {'z'}, dimensions={0} | all-to-all | bytes 2949120 | tf_op jit(solution)/shard_map/all_to_all | solution.py:27
  69.4 30.5 %collective-permute-done.3 = bf16[384,1920]{1,0:T(8,128)(2,1)S(1)} collective-permute-done((bf16[384,1920]{1,0:T(8,128)(2,1)S(1)}, bf16[384,1920]{1,0:T(8,128)(2,1)S(1)}, u32[]{:S(2)}, u32[]{:S(2)}) %collective-permute-start.3) | collective-permute-done | bytes 1474592 | tf_op jit(solution)/shard_map/ppermute | solution.py:23
  106.8 9.2 %all_gather.25 = bf16[128,1536]{1,0:T(8,128)(2,1)S(1)} all-gather(bf16[32,1536]{1,0:T(8,128)(2,1)S(1)} %fusion.78), channel_id=1, replica_groups=mesh['s'=2,'y'=4,'z'=4,'x'=2,'c'=2] {'x','c'}, dimensions={0}, use_global_device_ids=true | all-gather | bytes 491520 | tf_op jit(solution)/shard_map/all_gather | solution.py:82
  123.6 14.7 %all-to-all-done.1 = bf16[16,128,128]{2,1,0:T(8,128)(2,1)} async-done(((bf16[16,128,128]{2,1,0:T(8,128)(2,1)}), bf16[16,128,128]{2,1,0:T(8,128)(2,1)}, u32[]{:S(2)}, u32[]{:S(2)}) %all-to-all-start.1) | async-done | bytes 524320 | tf_op jit(solution)/shard_map/all_to_all | solution.py:27
  161.5 15.9 %all_to_all.101 = bf16[8,32,1536]{2,1,0:T(8,128)(2,1)S(1)} all-to-all(bf16[8,32,1536]{2,1,0:T(8,128)(2,1)S(1)} %broadcast_in_dim.90), channel_id=1, replica_groups=mesh['s'=2,'y'=4,'z'=4,'x'=2,'c'=2] {'z','x'}, dimensions={0} | all-to-all | bytes 1572864 | tf_op jit(solution)/shard_map/all_to_all | solution.py:27
  204.3 25.8 %all-gather.9.cloned.1.call-done = bf16[1792,896]{1,0:T(8,128)(2,1)} async-done(((bf16[112,896]{1,0:T(8,128)(2,1)}), bf16[1792,896]{1,0:T(8,128)(2,1)}) %all-gather.9.cloned.1.call-update) | async-done | bytes 3211280 | tf_op jit(solution)/shard_map/all_gather | solution.py:212
  240.1 6.7 all_gather.28
  249.1 18.2 %all_to_all.102 = bf16[16,128,128]{2,1,0:T(8,128)(2,1)} all-to-all(bf16[16,128,128]{2,1,0:T(8,128)(2,1)S(1)} %broadcast_in_dim.91), channel_id=1, replica_groups=mesh['s'=2,'y'=4,'z'=4,'x'=2,'c'=2] {'y','z'}, dimensions={0} | all-to-all | bytes 1048576 | tf_op jit(solution)/shard_map/all_to_all | solution.py:27
  305.4 7.3 all-to-all-done.10
  321.2 8.3 %all-to-all-done.8 = bf16[8,32,1536]{2,1,0:T(8,128)(2,1)} async-done(((bf16[8,32,1536]{2,1,0:T(8,128)(2,1)}), bf16[8,32,1536]{2,1,0:T(8,128)(2,1)}, u32[]{:S(2)}, u32[]{:S(2)}) %all-to-all-start.8) | async-done | bytes 786464 | tf_op jit(solution)/shard_map/all_to_all | solution.py:27
  357.6 8.6 %copy.295 = bf16[1536,1920]{1,0:T(8,128)(2,1)} copy(bf16[1536,1920]{0,1:T(8,128)(2,1)} %pad_maximum_fusion.1) | data formatting | bytes 11796480
  374.7 10.9 %all-to-all-done.11 = bf16[8,32,1536]{2,1,0:T(8,128)(2,1)} async-done(((bf16[8,32,1536]{2,1,0:T(8,128)(2,1)}), bf16[8,32,1536]{2,1,0:T(8,128)(2,1)}, u32[]{:S(2)}, u32[]{:S(2)}) %all-to-all-start.11) | async-done | bytes 786464 | tf_op jit(solution)/shard_map/all_to_all | solution.py:27
  390.3 7.4 all_gather.30
  424.2 7.2 all-to-all-done.12
  438.1 10.1 %all_to_all.103 = bf16[4,32,1536]{2,1,0:T(8,128)(2,1)S(1)} all-to-all(bf16[4,32,1536]{2,1,0:T(8,128)(2,1)S(1)} %bitcast.373), channel_id=1, replica_groups=mesh['s'=2,'y'=4,'z'=4,'x'=2,'c'=2] {'x','c'}, dimensions={0} | all-to-all | bytes 786432 | tf_op jit(solution)/shard_map/all_to_all | solution.py:27
  449.2 15.1 %all_to_all.104 = bf16[8,32,1536]{2,1,0:T(8,128)(2,1)S(1)} all-to-all(bf16[8,32,1536]{2,1,0:T(8,128)(2,1)S(1)} %broadcast_in_dim.97), channel_id=1, replica_groups=mesh['s'=2,'y'=4,'z'=4,'x'=2,'c'=2] {'z','x'}, dimensions={0} | all-to-all | bytes 1572864 | tf_op jit(solution)/shard_map/all_to_all | solution.py:27
  481.2 8.6 %copy.293 = bf16[1536,1920]{1,0:T(8,128)(2,1)} copy(bf16[1536,1920]{0,1:T(8,128)(2,1)} %pad_maximum_fusion) | data formatting | bytes 11796480
  509.5 7.0 all-to-all-done.15
  521.7 7.2 all_gather.31
  590.5 16.5 %all_to_all.105 = bf16[8,32,1536]{2,1,0:T(8,128)(2,1)S(1)} all-to-all(bf16[8,32,1536]{2,1,0:T(8,128)(2,1)S(1)} %bitcast.328), channel_id=1, replica_groups=mesh['s'=2,'y'=4,'z'=4,'x'=2,'c'=2] {'z','x'}, dimensions={0} | all-to-all | bytes 1572864 | tf_op jit(solution)/shard_map/all_to_all | solution.py:27
  619.7 42.5 %reduce-scatter.17.cloned.1.call-done = bf16[112,896]{1,0:T(8,128)(2,1)} async-done(((bf16[1792,896]{1,0:T(8,128)(2,1)}), bf16[112,896]{1,0:T(8,128)(2,1)}) %reduce-scatter.17.cloned.1.call-update) | async-done | bytes 200720
  663.5 79.6 %reduce-scatter.19.cloned.1.call-done = bf16[112,896]{1,0:T(8,128)(2,1)} async-done(((bf16[1792,896]{1,0:T(8,128)(2,1)}), bf16[112,896]{1,0:T(8,128)(2,1)}) %reduce-scatter.19.cloned.1.call-update) | async-done | bytes 200720
  770.6 16.4 %all-to-all-done.19 = bf16[4,96,1920]{2,1,0:T(8,128)(2,1)S(1)} async-done(((bf16[4,96,1920]{2,1,0:T(8,128)(2,1)}), bf16[4,96,1920]{2,1,0:T(8,128)(2,1)S(1)}, u32[]{:S(2)}, u32[]{:S(2)}) %all-to-all-start.19) | async-done | bytes 1474592 | tf_op jit(solution)/shard_map/all_to_all | solution.py:27
  789.8 7.4 fusion.142
  (533 shorter events, 388.6 us)
Async XLA Ops:
  14.3 88.9 %all-gather.5.cloned.1.call-start = ((), (), s32[]{:S(2)}) async-start(), calls=%async_computation.24 | async-start | bytes 3411968 | tf_op jit(solution)/shard_map/all_gather | solution.py:212
  27.9 154.5 %all-gather.7.cloned.1.call-start = ((), (), s32[]{:S(2)}) async-start(), calls=%async_computation.25 | async-start | bytes 7372800 | tf_op jit(solution)/shard_map/all_gather | solution.py:225
  66.7 33.2 %collective-permute-start.3 = (bf16[384,1920]{1,0:T(8,128)(2,1)S(1)}, bf16[384,1920]{1,0:T(8,128)(2,1)S(1)}, u32[]{:S(2)}, u32[]{:S(2)}) collective-permute-start(bf16[384,1920]{1,0:T(8,128)(2,1)S(1)} %bitcast.315), channel_id=1, source_target_pairs={{0,64},{64,0},{1,65},{65,1},{2,66},{66,2},{3,67},{67,3},{4,68},{68... | collective-permute-start | bytes 4423688 | tf_op jit(solution)/shard_map/ppermute | solution.py:23
  119.0 19.3 %all-to-all-start.1 = ((bf16[16,128,128]{2,1,0:T(8,128)(2,1)}), bf16[16,128,128]{2,1,0:T(8,128)(2,1)}, u32[]{:S(2)}, u32[]{:S(2)}) async-start(bf16[16,128,128]{2,1,0:T(8,128)(2,1)} %broadcast_in_dim.87), calls=%async_computation.1 | async-start | bytes 1048576 | tf_op jit(solution)/shard_map/all_to_all | solution.py:27
  123.5 106.6 %all-gather.9.cloned.1.call-start = ((), (), s32[]{:S(2)}) async-start(), calls=%async_computation.26 | async-start | bytes 3411968 | tf_op jit(solution)/shard_map/all_gather | solution.py:212
  153.4 179.3 %all-gather.11.cloned.1.call-start = ((), (), s32[]{:S(2)}) async-start(), calls=%async_computation.27 | async-start | bytes 7372800 | tf_op jit(solution)/shard_map/all_gather | solution.py:225
  200.0 37.8 %all-to-all-start.5 = ((bf16[8,32,1536]{2,1,0:T(8,128)(2,1)}), bf16[8,32,1536]{2,1,0:T(8,128)(2,1)}, u32[]{:S(2)}, u32[]{:S(2)}) async-start(bf16[8,32,1536]{2,1,0:T(8,128)(2,1)} %bitcast.325), calls=%async_computation.5 | async-start | bytes 1572864 | tf_op jit(solution)/shard_map/all_to_all | solution.py:27
  296.8 15.9 %all-to-all-start.10 = ((bf16[8,32,1536]{2,1,0:T(8,128)(2,1)}), bf16[8,32,1536]{2,1,0:T(8,128)(2,1)}, u32[]{:S(2)}, u32[]{:S(2)}) async-start(bf16[8,32,1536]{2,1,0:T(8,128)(2,1)} %broadcast_in_dim.95), calls=%async_computation.10 | async-start | bytes 1572864 | tf_op jit(solution)/shard_map/all_to_all | solution.py:27
  314.5 14.9 %all-to-all-start.8 = ((bf16[8,32,1536]{2,1,0:T(8,128)(2,1)}), bf16[8,32,1536]{2,1,0:T(8,128)(2,1)}, u32[]{:S(2)}, u32[]{:S(2)}) async-start(bf16[8,32,1536]{2,1,0:T(8,128)(2,1)} %broadcast_in_dim.93), calls=%async_computation.8 | async-start | bytes 1572864 | tf_op jit(solution)/shard_map/all_to_all | solution.py:27
  318.7 295.6 %reduce-scatter.15.cloned.1.call-start = ((), (), s32[]{:S(2)}) async-start(), calls=%async_computation.29 | async-start | bytes 7372800 | tf_op jit(solution)/shard_map/reduce_scatter | solution.py:257
  318.8 13.9 %collective-permute-start.9 = (bf16[256,1536]{1,0:T(8,128)(2,1)}, bf16[256,1536]{1,0:T(8,128)(2,1)}, u32[]{:S(2)}, u32[]{:S(2)}) collective-permute-start(bf16[256,1536]{1,0:T(8,128)(2,1)} %bitcast.50), channel_id=1, source_target_pairs={{0,1},{1,0},{2,3},{3,2},{4,5},{5,4},{6,7},{7,6},{8,9},{9,8},{10,11... | collective-permute-start | bytes 2359304 | tf_op jit(solution)/shard_map/ppermute | solution.py:23
  346.3 19.9 %collective-permute-start.10 = (bf16[256,1536]{1,0:T(8,128)(2,1)}, bf16[256,1536]{1,0:T(8,128)(2,1)}, u32[]{:S(2)}, u32[]{:S(2)}) collective-permute-start(bf16[256,1536]{1,0:T(8,128)(2,1)} %slice.528), channel_id=1, source_target_pairs={{0,1},{1,0},{2,3},{3,2},{4,5},{5,4},{6,7},{7,6},{8,9},{9,8},{10,11... | collective-permute-start | bytes 2359304 | tf_op jit(solution)/shard_map/ppermute | solution.py:23
  368.9 16.8 %all-to-all-start.11 = ((bf16[8,32,1536]{2,1,0:T(8,128)(2,1)}), bf16[8,32,1536]{2,1,0:T(8,128)(2,1)}, u32[]{:S(2)}, u32[]{:S(2)}) async-start(bf16[8,32,1536]{2,1,0:T(8,128)(2,1)} %bitcast.327), calls=%async_computation.11 | async-start | bytes 1572864 | tf_op jit(solution)/shard_map/all_to_all | solution.py:27
  412.2 19.2 %all-to-all-start.12 = ((bf16[16,128,128]{2,1,0:T(8,128)(2,1)}), bf16[16,128,128]{2,1,0:T(8,128)(2,1)}, u32[]{:S(2)}, u32[]{:S(2)}) async-start(bf16[16,128,128]{2,1,0:T(8,128)(2,1)} %bitcast.334), calls=%async_computation.12 | async-start | bytes 1048576 | tf_op jit(solution)/shard_map/all_to_all | solution.py:27
  416.9 201.4 %reduce-scatter.13.cloned.1.call-start = ((), (), s32[]{:S(2)}) async-start(), calls=%async_computation.28 | async-start | bytes 7372800 | tf_op jit(solution)/shard_map/reduce_scatter | solution.py:261
  499.6 16.9 %all-to-all-start.15 = ((bf16[8,32,1536]{2,1,0:T(8,128)(2,1)}), bf16[8,32,1536]{2,1,0:T(8,128)(2,1)}, u32[]{:S(2)}, u32[]{:S(2)}) async-start(bf16[8,32,1536]{2,1,0:T(8,128)(2,1)} %bitcast.326), calls=%async_computation.15 | async-start | bytes 1572864 | tf_op jit(solution)/shard_map/all_to_all | solution.py:27
  546.7 14.7 %all-to-all-start.16 = ((bf16[16,128,128]{2,1,0:T(8,128)(2,1)}), bf16[16,128,128]{2,1,0:T(8,128)(2,1)S(1)}, u32[]{:S(2)}, u32[]{:S(2)}) async-start(bf16[16,128,128]{2,1,0:T(8,128)(2,1)} %bitcast.333), calls=%async_computation.16 | async-start | bytes 1048576 | tf_op jit(solution)/shard_map/all_to_all | solution.py:27
  564.7 11.6 %all-to-all-start.17 = ((bf16[4,32,1536]{2,1,0:T(8,128)(2,1)}), bf16[4,32,1536]{2,1,0:T(8,128)(2,1)S(1)}, u32[]{:S(2)}, u32[]{:S(2)}) async-start(bf16[4,32,1536]{2,1,0:T(8,128)(2,1)} %bitcast.372), calls=%async_computation.17 | async-start | bytes 786432 | tf_op jit(solution)/shard_map/all_to_all | solution.py:27
  569.7 92.5 %reduce-scatter.17.cloned.1.call-start = ((), (), s32[]{:S(2)}) async-start(), calls=%async_computation.30 | async-start | bytes 3411968
  583.3 159.9 %reduce-scatter.19.cloned.1.call-start = ((), (), s32[]{:S(2)}) async-start(), calls=%async_computation.31 | async-start | bytes 3411968
  614.4 146.1 %collective-permute-start.18 = (bf16[384,1920]{1,0:T(8,128)(2,1)}, bf16[384,1920]{1,0:T(8,128)(2,1)S(1)}, u32[]{:S(2)}, u32[]{:S(2)}) collective-permute-start(bf16[384,1920]{1,0:T(8,128)(2,1)} %reduce-scatter.15.cloned.1.call-done), channel_id=1, source_target_pairs={{0,64},{1,65},{2,66},{3,67},{4,68},{5,69},{6,70},{7,71},{8,72},{9,... | collective-permute-start | bytes 4423688 | tf_op jit(solution)/shard_map/ppermute | solution.py:265
  618.4 142.1 %collective-permute-start.19 = (bf16[384,1920]{1,0:T(8,128)(2,1)}, bf16[384,1920]{1,0:T(8,128)(2,1)}, u32[]{:S(2)}, u32[]{:S(2)}) collective-permute-start(bf16[384,1920]{1,0:T(8,128)(2,1)} %reduce-scatter.13.cloned.1.call-done), channel_id=1, source_target_pairs={{64,0},{65,1},{66,2},{67,3},{68,4},{69,5},{70,6},{71,7},{72,8},{73... | collective-permute-start | bytes 4423688 | tf_op jit(solution)/shard_map/ppermute | solution.py:265
  662.2 86.2 %collective-permute-start.17 = (bf16[112,896]{1,0:T(8,128)(2,1)}, bf16[112,896]{1,0:T(8,128)(2,1)S(1)}, u32[]{:S(2)}, u32[]{:S(2)}) collective-permute-start(bf16[112,896]{1,0:T(8,128)(2,1)} %reduce-scatter.17.cloned.1.call-done), channel_id=1, source_target_pairs={{64,0},{65,1},{66,2},{67,3},{68,4},{69,5},{70,6},{71,7},{72,8},{73... | collective-permute-start | bytes 602120 | tf_op jit(solution)/shard_map/ppermute | solution.py:265
  764.1 22.8 %all-to-all-start.19 = ((bf16[4,96,1920]{2,1,0:T(8,128)(2,1)}), bf16[4,96,1920]{2,1,0:T(8,128)(2,1)S(1)}, u32[]{:S(2)}, u32[]{:S(2)}) async-start(bf16[4,96,1920]{2,1,0:T(8,128)(2,1)} %bitcast.107), calls=%async_computation.19 | async-start | bytes 2949120 | tf_op jit(solution)/shard_map/all_to_all | solution.py:27
  (119 other events, 1392.3 us)
Sparse Core Ops, SparseCore 0:
  28.0 53.8 all-gather.4
  102.1 69.2 all-gather.6
  173.6 56.4 all-gather.8
  231.6 65.8 all-gather.10
  366.3 63.9 reduce-scatter.14
  489.9 58.1 reduce-scatter.12
  583.4 78.8 reduce-scatter.16
  665.7 77.3 reduce-scatter.18

commit v2 on v1

v2 whole, which is shorter than its diff:
```python
import jax
import jax.numpy as jnp
import numpy as np
from jax import lax
from jax.experimental import pallas as pl
from jax.experimental.pallas import tpu as pltpu
from jax.sharding import Mesh
from jax.sharding import PartitionSpec as P

HEAD = 128
EPS = 1e-06
NEG = -1e30
THETA = 1000000.0
WIDTH = 1536
QCOLS = 384
SEQ = 2048
CHUNK = 512
LOCAL_FF = 560
PAD_FF = 640
GU = 2 * PAD_FF
FW = 3 * PAD_FF
SCALE = HEAD**-0.5
AXES = ("s", "y", "z", "x", "c")
BLOCK_ORDER = (0, 2, 1, 3)
BF = jnp.bfloat16
F32 = jnp.float32
VMEM = pl.BlockSpec(memory_space=pltpu.VMEM)
SMEM = pl.BlockSpec(memory_space=pltpu.SMEM)
ANY = pl.BlockSpec(memory_space=pl.ANY)


def swap(value, axis):
    return lax.ppermute(value, axis, [(0, 1), (1, 0)])


def exchange(value, axes):
    return lax.all_to_all(value, axes, split_axis=0, concat_axis=0, tiled=True)


def nn(left, right):
    return jnp.dot(left, right, preferred_element_type=F32)


def nt(left, right):
    return lax.dot_general(left, right, (((1,), (1,)), ((), ())), preferred_element_type=F32)


def tn(left, right):
    return lax.dot_general(left, right, (((0,), (0,)), ((), ())), preferred_element_type=F32)


def after(value, done):
    return lax.optimization_barrier((value, done))[0]


def inverse_rms(values):
    return lax.rsqrt(jnp.mean(values * values, axis=-1, keepdims=True) + EPS)


def call(kernel, out_shape, in_specs, args, scratch=(), flops=0, size=0, exps=0, **more):
    return pl.pallas_call(
        kernel,
        out_shape=out_shape,
        in_specs=in_specs,
        scratch_shapes=list(scratch),
        compiler_params=pltpu.CompilerParams(vmem_limit_bytes=52 * 1024 * 1024),
        cost_estimate=pl.CostEstimate(flops=flops, bytes_accessed=size, transcendentals=exps),
        **more,
    )(*args)


def arr(shape, dtype=BF):
    return jax.ShapeDtypeStruct(shape, dtype)


def turned(values, cosine, sine):
    return values * cosine + pltpu.roll(values, HEAD // 2, 1) * sine


def whole_weight(ref, scratch, first, size):
    if len(ref.shape) == 2:
        return ref[...]
    for b in range(16):
        scratch[pl.ds(b * 96, 96), :] = ref[b, pl.ds(0, 96), pl.ds(first, size)]
    return scratch[...]


def qkv_kernel(flag, xin, gain, weight, bias, cosine, sine, normed, query, kv, scratch):
    whole = whole_weight(weight, scratch, 0, 512)
    cos, sin = cosine[...], sine[...]
    rows = xin[...].astype(F32)
    low = (rows * inverse_rms(rows) * gain[...]).astype(BF)
    normed[...] = low
    out = nn(low, whole) + bias[...]
    for h in range(3):
        query[h] = turned(out[:, h * HEAD : (h + 1) * HEAD], cos, sin).astype(BF)
    last = out[:, QCOLS:]
    last = jnp.where(flag[0] == 1, turned(last, cos, sin), last).astype(BF)
    for b in range(16):
        kv[b] = last


def qkv_columns(flag, xin, gain, weight, bias, cosine, sine):
    return call(
        qkv_kernel,
        (arr((HEAD, WIDTH)), arr((3, HEAD, HEAD)), arr((16, HEAD, HEAD))),
        [SMEM] + [VMEM] * 6,
        (flag, xin, gain, weight, bias, cosine, sine),
        [pltpu.VMEM((WIDTH, 512), BF)],
        flops=2 * 128 * 1536 * 512,
        size=3_000_000,
    )


def key_scores(query_all, keys, key_seg, query_seg, first_key, first_query):
    scores = nt(keys, query_all) * SCALE
    key_pos = first_key + lax.broadcasted_iota(jnp.int32, (CHUNK, HEAD), 0)
    query_pos = first_query + lax.broadcasted_iota(jnp.int32, (CHUNK, HEAD), 1)
    allowed = (key_seg == query_seg) & (key_pos <= query_pos)
    return [jnp.where(allowed, scores[:, h * HEAD : (h + 1) * HEAD], NEG) for h in range(3)]


def attend_kernel(flag, query, kv_mine, kv_other, seg_col, seg_row, out_t, attended, lse, part, top, total, acc, scratch):
    query_all = query[...].reshape(3 * HEAD, HEAD)
    is_key = flag[0] == 1
    first_query = flag[1] * HEAD
    top[...] = jnp.full(top.shape, -3e38, F32)
    total[...] = jnp.zeros(total.shape, F32)
    acc[...] = jnp.zeros(acc.shape, F32)

    @pl.loop(0, SEQ // CHUNK)
    def _(step):
        at = pl.ds(pl.multiple_of(step * CHUNK, CHUNK), CHUNK)
        mine, other = kv_mine[at, :], kv_other[at, :]
        keys = jnp.where(is_key, mine, other)
        values = jnp.where(is_key, other, mine)
        scores = key_scores(query_all, keys, seg_col[at, :], seg_row[...], step * CHUNK, first_query)
        for h in range(3):
            columns = pl.ds(h * HEAD, HEAD)
            old = top[:, columns]
            new = jnp.maximum(old, jnp.max(scores[h], axis=0, keepdims=True))
            shrink = jnp.exp(old - new)
            raised = jnp.exp(scores[h] - new)
            top[:, columns] = new
            total[:, columns] = total[:, columns] * shrink + jnp.sum(raised, axis=0, keepdims=True)
            acc[:, columns] = acc[:, columns] * shrink + tn(values, raised.astype(BF))

    lse[...] = top[...] + jnp.log(total[...])
    done = acc[...] / total[...]
    for h in range(3):
        attended[:, pl.ds(h * HEAD, HEAD)] = done[:, h * HEAD : (h + 1) * HEAD].T.astype(BF)
    out = nt(attended[...], whole_weight(out_t, scratch, 512, QCOLS)).astype(BF)
    for t in range(4):
        part[t] = out[t * 32 : (t + 1) * 32]


def attend(flag, query, kv_mine, kv_other, seg_col, seg_row, out_t):
    return call(
        attend_kernel,
        (arr((HEAD, QCOLS)), arr((1, QCOLS), F32), arr((4, 32, WIDTH))),
        [SMEM] + [VMEM] * 6,
        (flag, query, kv_mine, kv_other, seg_col, seg_row, out_t),
        [
            pltpu.VMEM((1, QCOLS), F32),
            pltpu.VMEM((1, QCOLS), F32),
            pltpu.VMEM((HEAD, QCOLS), F32),
            pltpu.VMEM((WIDTH, QCOLS), BF),
        ],
        flops=4 * 384 * 2048 * 128 + 2 * 128 * 384 * 1536,
        size=3_000_000,
        exps=384 * 2048,
    )


def attend_back_kernel(
    flag, query, kv_mine, kv_other, seg_col, seg_row, lse, grad_att, out_t, cosine, sine,
    grad_query, kept, sent, low, acc, scratch
):
    query_all = query[...].reshape(3 * HEAD, HEAD)
    is_key = flag[0] == 1
    first_query = flag[1] * HEAD
    grad_attended = nn(grad_att[...], whole_weight(out_t, scratch, 512, QCOLS)).astype(BF)
    for h in range(3):
        low[pl.ds(h * HEAD, HEAD), :] = grad_attended[:, h * HEAD : (h + 1) * HEAD]
    grad_rows = low[...]
    lse_row = lse[...]

    def chunk(step):
        at = pl.ds(pl.multiple_of(step * CHUNK, CHUNK), CHUNK)
        mine, other = kv_mine[at, :], kv_other[at, :]
        keys = jnp.where(is_key, mine, other)
        values = jnp.where(is_key, other, mine)
        scores = key_scores(query_all, keys, seg_col[at, :], seg_row[...], step * CHUNK, first_query)
        probs = [jnp.exp(scores[h] - lse_row[:, h * HEAD : (h + 1) * HEAD]) for h in range(3)]
        grad_probs = nt(values, grad_rows)
        return at, keys, probs, grad_probs

    acc[...] = jnp.zeros(acc.shape, F32)

    def row_sums(step, sums):
        _, _, probs, grad_probs = chunk(step)
        return tuple(
            sums[h] + jnp.sum(probs[h] * grad_probs[:, h * HEAD : (h + 1) * HEAD], axis=0, keepdims=True)
            for h in range(3)
        )

    zero = jnp.zeros((1, HEAD), F32)
    sums = lax.fori_loop(0, SEQ // CHUNK, row_sums, (zero, zero, zero))

    @pl.loop(0, SEQ // CHUNK)
    def _(step):
        at, keys, probs, grad_probs = chunk(step)
        low_probs = jnp.concatenate([p.astype(BF) for p in probs], axis=1)
        low_scores = jnp.concatenate(
            [
                (probs[h] * (grad_probs[:, h * HEAD : (h + 1) * HEAD] - sums[h])).astype(BF)
                for h in range(3)
            ],
            axis=1,
        )
        grad_value = nn(low_probs, grad_rows)
        grad_key = nn(low_scores, query_all) * SCALE
        acc[...] += tn(keys, low_scores)
        kept[at, :] = jnp.where(is_key, grad_key, grad_value)
        sent[at, :] = jnp.where(is_key, grad_value, grad_key).astype(BF)

    cos, sin = cosine[...], sine[...]
    for h in range(3):
        rows = acc[:, pl.ds(h * HEAD, HEAD)].T * SCALE
        grad_query[:, pl.ds(h * HEAD, HEAD)] = turned(rows, cos, -sin).astype(BF)


def attend_back(flag, query, kv_mine, kv_other, seg_col, seg_row, lse, grad_att, out_t, cosine, sine):
    return call(
        attend_back_kernel,
        (arr((HEAD, QCOLS)), arr((SEQ, HEAD), F32), arr((SEQ, HEAD))),
        [SMEM] + [VMEM] * 10,
        (flag, query, kv_mine, kv_other, seg_col, seg_row, lse, grad_att, out_t, cosine, sine),
        [pltpu.VMEM((3 * HEAD, HEAD), BF), pltpu.VMEM((HEAD, QCOLS), F32), pltpu.VMEM((WIDTH, QCOLS), BF)],
        flops=14 * 384 * 2048 * 128 + 2 * 128 * 384 * 1536,
        size=5_000_000,
        exps=2 * 384 * 2048,
    )


def qkv_back_kernel(
    flag, pieces, grad_query, weight, xin, cosine, sine, grad_qkv, grad_bias, grad_gain, part, scratch
):
    whole = whole_weight(weight, scratch, 0, 512)
    total = jnp.sum(pieces[...].astype(F32), axis=0)
    total = jnp.where(flag[0] == 1, turned(total, cosine[...], -sine[...]), total).astype(BF)
    grad_qkv[:, pl.ds(0, QCOLS)] = grad_query[...]
    grad_qkv[:, pl.ds(QCOLS, HEAD)] = total
    grads = grad_qkv[...]
    grad_bias[...] = jnp.sum(grads.astype(F32), axis=0, keepdims=True)
    out = nt(grads, whole)
    rows = xin[...].astype(F32)
    grad_gain[...] = jnp.sum(out * rows * inverse_rms(rows), axis=0, keepdims=True)
    low = out.astype(BF)
    for t in range(4):
        part[t] = low[t * 32 : (t + 1) * 32]


def qkv_back(flag, pieces, grad_query, weight, xin, cosine, sine):
    return call(
        qkv_back_kernel,
        (arr((HEAD, 512)), arr((1, 512), F32), arr((1, WIDTH), F32), arr((4, 32, WIDTH))),
        [SMEM] + [VMEM] * 6,
        (flag, pieces, grad_query, weight, xin, cosine, sine),
        [pltpu.VMEM((WIDTH, 512), BF)],
        flops=2 * 128 * 1536 * 512,
        size=3_000_000,
    )


def weight_copies(own, other, gate_up, down, sems, order):
    copies = {}
    for i, ref in enumerate((own, other)):
        for name in order:
            start, size, buffer = (0, GU, gate_up) if name == "gate_up" else (GU, PAD_FF, down)
            copies[i, name] = pltpu.make_async_copy(
                ref.at[:, pl.ds(start, size)], buffer.at[i], sems.at[2 * i + (name == "down")]
            )
    for i in range(2):
        for name in order:
            copies[i, name].start()
    return copies


def feed_kernel(tokens, own, other, part, gate_up_out, gate_up, down, acc, sems):
    copies = weight_copies(own, other, gate_up, down, sems, ("gate_up", "down"))
    rows = tokens[...]
    for i in range(2):
        copies[i, "gate_up"].wait()
        both = nn(rows, gate_up[i])
        gate_up_out[i] = both.astype(BF)
        gate, up = both[:, :PAD_FF], both[:, PAD_FF:]
        hidden = (gate * jax.nn.sigmoid(gate) * up).astype(BF)
        copies[i, "down"].wait()
        out = nt(hidden, down[i])
        if i == 0:
            acc[...] = out
        else:
            part[...] = (acc[...] + out).astype(BF)


FEED_SCRATCH = [
    pltpu.VMEM((2, WIDTH, GU), BF),
    pltpu.VMEM((2, WIDTH, PAD_FF), BF),
    pltpu.VMEM((256, WIDTH), F32),
    pltpu.SemaphoreType.DMA((4,)),
]


def feed(tokens, own, other):
    return call(
        feed_kernel,
        (arr((256, WIDTH)), arr((2, 256, GU))),
        [VMEM, ANY, ANY],
        (tokens, own, other),
        FEED_SCRATCH,
        flops=2 * 256 * 1536 * 3840,
        size=15_000_000,
        exps=256 * 1280,
    )


def feed_back_kernel(grads, own, other, gate_up_in, part, for_own, for_other, gate_up, down, acc, sems):
    copies = weight_copies(own, other, gate_up, down, sems, ("down", "gate_up"))
    rows = grads[...]
    for i, result in enumerate((for_own, for_other)):
        copies[i, "down"].wait()
        grad_hidden = nn(rows, down[i])
        gate = gate_up_in[i, :, pl.ds(0, PAD_FF)].astype(F32)
        up = gate_up_in[i, :, pl.ds(PAD_FF, PAD_FF)].astype(F32)
        sig = jax.nn.sigmoid(gate)
        silu = gate * sig
        result[:, pl.ds(0, PAD_FF)] = (grad_hidden * up * sig * (1.0 + gate * (1.0 - sig))).astype(BF)
        result[:, pl.ds(PAD_FF, PAD_FF)] = (grad_hidden * silu).astype(BF)
        result[:, pl.ds(GU, PAD_FF)] = (silu * up).astype(BF)
        copies[i, "gate_up"].wait()
        out = nt(result[:, pl.ds(0, GU)], gate_up[i])
        if i == 0:
            acc[...] = out
        else:
            part[...] = (acc[...] + out).astype(BF)


def feed_back(grads, own, other, gate_up):
    return call(
        feed_back_kernel,
        (arr((256, WIDTH)), arr((256, FW)), arr((256, FW))),
        [VMEM, ANY, ANY, VMEM],
        (grads, own, other, gate_up),
        FEED_SCRATCH,
        flops=2 * 256 * 1536 * 3840,
        size=17_000_000,
        exps=256 * 1280,
    )


def feed_grad_kernel(tokens, tokens_other, grads, grads_other, own, given, out):
    gate_up, hidden = pl.ds(0, GU), pl.ds(GU, PAD_FF)
    out[:, gate_up] = (tn(tokens[...], own[:, gate_up]) + tn(tokens_other[...], given[:, gate_up])).astype(BF)
    out[:, hidden] = (tn(grads[...], own[:, hidden]) + tn(grads_other[...], given[:, hidden])).astype(BF)


def feed_grad(tokens, tokens_other, grads, grads_other, own, given):
    rows = 256
    columns = pl.BlockSpec((256, rows), lambda i: (0, i))
    fixed = pl.BlockSpec((256, FW), lambda i: (0, 0))
    return call(
        feed_grad_kernel,
        arr((WIDTH, FW)),
        [columns] * 4 + [fixed] * 2,
        (tokens, tokens_other, grads, grads_other, own, given),
        flops=2 * 512 * 1536 * 1920,
        size=12_000_000,
        grid=(WIDTH // rows,),
        out_specs=pl.BlockSpec((rows, FW), lambda i: (i, 0)),
    )


def shifted(value, axis, steps):
    return lax.ppermute(value, axis, [(i, (i + steps) % 4) for i in range(4)])


def ring_gather(piece, first, second, done):
    some = after(jnp.stack([piece] + [shifted(piece, first, j) for j in (1, 2, 3)]), done)
    return [some] + [shifted(some, second, k) for k in (1, 2, 3)]


def ring_block(place, j, k):
    return lax.rem(place[0] + 4 - j, 4) * place[1] + lax.rem(place[2] + 4 - k, 4) * place[3]


def assemble_kernel(columns, place, *refs):
    pieces, outs, tail = refs[:4], refs[4:-1], refs[-1]
    for k in range(4):
        for j in range(4):
            block = ring_block(place, j, k)
            first = 0
            for out, size in zip(outs, columns, strict=True):
                at = pl.ds(pl.multiple_of(block * 96, 32), 96)
                out[at, :] = pieces[k][j, pl.ds(0, 96), pl.ds(first, size)]
                first += size
            tail[block] = pieces[k][j, pl.ds(96, 16), pl.ds(0, 512)]


def assemble(place, pieces, columns):
    return call(
        lambda *refs: assemble_kernel(columns, *refs),
        tuple(arr((WIDTH, size)) for size in columns) + (arr((16, 16, 512)),),
        [SMEM] + [VMEM] * 4,
        (place, *pieces),
        size=7_000_000,
    )


def weight_grad_kernel(place, normed, grad_qkv, grad_att, attended, bias, gain_a, gain_b, *rest):
    outs, scratch = rest[:-1], rest[-1]
    scratch[:, pl.ds(0, 512)] = tn(normed[...], grad_qkv[...]).astype(BF)
    scratch[:, pl.ds(512, QCOLS)] = tn(grad_att[...], attended[...]).astype(BF)
    gains = [gain_a[...], gain_b[...]]
    first_row = lax.broadcasted_iota(jnp.int32, (16, 896), 0) == 0
    for b in range(16):
        moved = [(pltpu.roll(g, (WIDTH - 96 * b) % WIDTH, 1) if b else g)[:, :HEAD] for g in gains]
        row = jnp.concatenate([bias[...], *moved, jnp.zeros((1, HEAD), F32)], axis=1)
        rest_rows = jnp.where(first_row, jnp.broadcast_to(row, (16, 896)), 0.0).astype(BF)
        y, z = b // 4, b % 4
        if len(outs) == 1:
            outs[0][z, y, pl.ds(0, 96), :] = scratch[pl.ds(b * 96, 96), :]
            outs[0][z, y, pl.ds(96, 16), :] = rest_rows
        else:
            for k in range(4):

                @pl.when(lax.rem(place[2] + k, 4) == z)
                def _(k=k):
                    outs[k][y, pl.ds(0, 96), :] = scratch[pl.ds(b * 96, 96), :]
                    outs[k][y, pl.ds(96, 16), :] = rest_rows


def weight_grad(place, apart, *args):
    shapes = (arr((4, 112, 896)),) * 4 if apart else (arr((4, 4, 112, 896)),)
    return call(
        weight_grad_kernel,
        shapes,
        [SMEM] + [VMEM] * 7,
        (place, *args),
        [pltpu.VMEM((WIDTH, 896), BF)],
        flops=2 * 128 * 1536 * 896,
        size=6_000_000,
    )


def ring_scatter(parts, done, last):
    total = parts[0].astype(F32)
    for k in (1, 2, 3):
        total = total + after(shifted(parts[k], "z", k), done).astype(F32)
    total = total.astype(BF)
    y = lax.axis_index("y")
    blocks = [lax.dynamic_index_in_dim(total, lax.rem(y + j, 4), 0, keepdims=False) for j in range(4)]
    result = blocks[0].astype(F32)
    for j in (1, 2, 3):
        result = result + after(shifted(blocks[j], "y", j), last).astype(F32)
    return result.astype(BF), total


def after_heads_kernel(pieces, xin, gain, mixed, second):
    total = xin[...].astype(F32) + jnp.sum(pieces[...].astype(F32), axis=0)
    mixed[...] = total
    low = (total * inverse_rms(total) * gain[...]).astype(BF)
    for t in range(8):
        second[t] = low


def after_heads(pieces, xin, gain):
    return call(
        after_heads_kernel,
        (arr((32, WIDTH), F32), arr((8, 32, WIDTH))),
        [VMEM] * 3,
        (pieces, xin, gain),
        size=1_500_000,
    )


def after_feed_kernel(pieces, mixed, out):
    out[...] = (mixed[...] + jnp.sum(pieces[...].astype(F32), axis=0)).astype(BF)


def after_feed(pieces, mixed):
    return call(after_feed_kernel, arr((32, WIDTH)), [VMEM] * 2, (pieces, mixed), size=1_500_000)


def norm_back(grad, values, gain, grad_out):
    inverse = inverse_rms(values)
    norm = values * inverse
    scaled = grad * gain
    grad_gain = jnp.sum(grad * norm, axis=0, keepdims=True)
    return grad_out + inverse * (scaled - norm * jnp.mean(scaled * norm, axis=-1, keepdims=True)), grad_gain


def before_heads_kernel(pieces, mixed, gain, grad_out, grad_mixed, low, grad_gain):
    grad = jnp.sum(pieces[...].astype(F32), axis=0)
    result, sums = norm_back(grad, mixed[...], gain[...], grad_out[...].astype(F32))
    grad_mixed[...] = result
    low[...] = result.astype(BF)
    grad_gain[...] = sums


def before_heads(pieces, mixed, gain, grad_out):
    return call(
        before_heads_kernel,
        (arr((32, WIDTH), F32), arr((32, WIDTH)), arr((1, WIDTH), F32)),
        [VMEM] * 4,
        (pieces, mixed, gain, grad_out),
        size=1_500_000,
    )


def layer_start_kernel(pieces, xin, gain, grad_mixed, grad_in, spread):
    grad = jnp.sum(pieces[...].astype(F32), axis=0)
    result, _ = norm_back(grad, xin[...].astype(F32), gain[...], grad_mixed[...])
    low = result.astype(BF)
    grad_in[...] = low
    for t in range(8):
        spread[t] = low


def layer_start(pieces, xin, gain, grad_mixed):
    return call(
        layer_start_kernel,
        (arr((32, WIDTH)), arr((8, 32, WIDTH))),
        [VMEM] * 4,
        (pieces, xin, gain, grad_mixed),
        size=1_500_000,
    )


def pack_kernel(gate, up, down, out):
    out[...] = jnp.zeros(out.shape, BF)
    for z in range(4):
        first = z * PAD_FF
        size = min(PAD_FF, 4 * LOCAL_FF - first)
        pieces = (
            gate[:, pl.ds(first, size)],
            up[:, pl.ds(first, size)],
            down[pl.ds(first, size), :].astype(F32).T.astype(BF),
        )
        for s in range(2):
            for i, piece in enumerate(pieces):
                out[4 * s + z, :, pl.ds(i * PAD_FF, size)] = piece


def pack(gate, up, down):
    return call(pack_kernel, arr((8, 96, FW)), [VMEM] * 3, (gate, up, down), size=4_500_000)


def unpack_kernel(pieces, gate, up, down):
    for z in range(4):
        first = z * PAD_FF
        size = min(PAD_FF, 4 * LOCAL_FF - first)
        total = pieces[z].astype(F32) + pieces[4 + z].astype(F32)
        gate[:, pl.ds(first, size)] = total[:, :size]
        up[:, pl.ds(first, size)] = total[:, PAD_FF : PAD_FF + size]
        down[pl.ds(first, size), :] = total[:, GU : GU + size].T


def unpack(pieces):
    wide = 4 * LOCAL_FF
    return call(
        unpack_kernel,
        (arr((96, wide), F32), arr((96, wide), F32), arr((wide, 96), F32)),
        [VMEM],
        (pieces,),
        size=7_000_000,
    )


def local(
    inputs, cotangent, segments, gain_one, w_query, b_query, w_keyval, b_keyval, w_out, gain_two, w_gate, w_up, w_down
):
    on_first = lax.axis_index("s") == 0
    core, chip = lax.axis_index("c"), lax.axis_index("x")
    block = lax.axis_index("y") * 4 + lax.axis_index("z")
    member = chip * 2 + core
    flag = jnp.stack([(core == 0).astype(jnp.int32), block.astype(jnp.int32)])

    def pick(first, second):
        return jnp.where(on_first, first, second)

    def gathered(piece, axes):
        return lax.all_gather(piece, axes, axis=0, tiled=True)

    def pair_gather(rows, axis):
        given = swap(rows, axis)
        is_low = lax.axis_index(axis) == 0
        return jnp.concatenate([jnp.where(is_low, rows, given), jnp.where(is_low, given, rows)], axis=0)

    def spread(rows, count, axes):
        return exchange(jnp.broadcast_to(rows[None], (count,) + rows.shape), axes)

    small = jnp.concatenate([gain_one[0], gain_two[0], b_keyval[0], jnp.zeros((72,), BF)])
    kv_blocks = w_keyval[0].reshape(24, 4, HEAD).transpose(1, 0, 2)
    kv_blocks = jnp.stack([kv_blocks[b] for b in BLOCK_ORDER])
    payload = jnp.concatenate(
        [kv_blocks, jnp.broadcast_to(small[None, None], (4, 1, HEAD)), jnp.zeros((4, 7, HEAD), BF)], axis=1
    )
    payload = exchange(jnp.concatenate([payload, payload], axis=0), ("s", "x", "c")).reshape(2, 4, 32, HEAD)
    bias_rows = jnp.pad(b_query, ((0, 15), (0, QCOLS)))
    own = jnp.concatenate([jnp.concatenate([w_query[0], w_out[0].T], axis=1), bias_rows], axis=0)
    other = swap(own, "s")

    def attention_rows(layer, matrices):
        kv = payload[layer]
        kv = jnp.concatenate([kv[:, :24].reshape(96, HEAD), kv[:, 24], jnp.zeros((12, HEAD), BF)], axis=0)
        return jnp.concatenate([matrices[:, :QCOLS], kv], axis=1)

    xin = pick(inputs[0], inputs[1])
    cot = pick(cotangent[0], cotangent[1])
    x_block1 = pair_gather(pair_gather(xin, "c"), "x")
    place_y, place_z = lax.axis_index("y").astype(jnp.int32), lax.axis_index("z").astype(jnp.int32)
    y_then_z = jnp.stack([place_y, jnp.int32(4), place_z, jnp.int32(1)])
    z_then_y = jnp.stack([place_z, jnp.int32(1), place_y, jnp.int32(4)])
    first, second = pick(own, other), pick(other, own)
    rows_first = jnp.concatenate([attention_rows(0, first), first[:, QCOLS:]], axis=1)
    rows_second = jnp.concatenate([attention_rows(1, second), second[:, QCOLS:]], axis=1)
    ring = ring_gather(rows_first, "z", "y", x_block1)
    ffn_packed = after(pack(w_gate[0], w_up[0], w_down[0]), ring[0])
    ffn_both = exchange(ffn_packed, ("s", "z")).reshape(2, 384, FW)
    ffn_both = after(ffn_both, ring)
    qkv_first, out_first, tail_first = assemble(z_then_y, ring, (512, QCOLS))

    seg = pick(segments[0], segments[1])
    local_pos = block * HEAD + jnp.arange(HEAD, dtype=jnp.int32)
    inverse_freq = THETA ** (-(jnp.arange(HEAD // 2, dtype=F32) * 2.0) / HEAD)
    angles = local_pos.astype(F32)[:, None] * inverse_freq[None, :]
    cosine = jnp.cos(angles)
    sine = jnp.sin(angles)
    cosine = jnp.concatenate([cosine, cosine], axis=1)
    sine = jnp.concatenate([-sine, sine], axis=1)
    seg_row = lax.dynamic_slice_in_dim(seg, block * HEAD, HEAD, 0)[None]
    seg_col = seg[:, None]

    def smalls(tail):
        bits = tail[:, :4, QCOLS : QCOLS + 56].reshape(64, 56)
        gain_a = bits[:, :24].reshape(1, WIDTH).astype(F32)
        gain_b = bits[:, 24:48].reshape(1, WIDTH).astype(F32)
        kv_bias = lax.dynamic_slice_in_dim(bits[:, 48:].reshape(1, 512), (core * 2 + chip) * HEAD, HEAD, 1)
        bias = jnp.concatenate([tail[:1, 0, :QCOLS], kv_bias], axis=1).astype(F32)
        return gain_a, gain_b, bias

    gain_a1, gain_b1, bias1 = smalls(tail_first)
    normed1, query1, kv = qkv_columns(flag, x_block1, gain_a1, qkv_first, bias1, cosine, sine)
    own1 = gathered(ffn_both[0], "y")
    kv_mine1 = exchange(kv, ("y", "z")).reshape(SEQ, HEAD)
    kv_other1 = swap(kv_mine1, "c")
    attended1, lse1, part = attend(flag, query1, kv_mine1, kv_other1, seg_col, seg_row, out_first)
    all_second = gathered(after(rows_second, part), ("y", "z")).reshape(16, 112, 896)
    mixed1, low = after_heads(exchange(part, ("x", "c")), xin, gain_b1)
    second1 = exchange(low, ("z", "x")).reshape(256, WIDTH)
    cot_low = spread(after(cot, second1), 8, ("z", "x")).reshape(256, WIDTH)
    second1 = after(second1, cot_low)
    own2 = gathered(after(ffn_both[1], second1), "y")
    other1 = swap(own1, "c")
    part, gate_up1 = feed(second1, own1, other1)
    pieces = exchange(part.reshape(8, 32, WIDTH), ("z", "x"))
    out_one = after_feed(pieces, mixed1)

    x_block2 = gathered(out_one, ("x", "c"))
    gain_a2, gain_b2, bias2 = smalls(all_second[:, 96:, :512])
    normed2, query2, kv = qkv_columns(flag, x_block2, gain_a2, all_second, bias2, cosine, sine)
    kv_mine2 = exchange(kv, ("y", "z")).reshape(SEQ, HEAD)
    kv_other2 = swap(kv_mine2, "c")
    attended2, lse2, part = attend(flag, query2, kv_mine2, kv_other2, seg_col, seg_row, all_second)
    mixed2, low = after_heads(exchange(part, ("x", "c")), out_one, gain_b2)
    other2 = swap(after(own2, low), "c")
    second2 = exchange(low, ("z", "x")).reshape(256, WIDTH)
    part, gate_up2 = feed(second2, own2, other2)
    last_part = part

    def backward(grad_out, grad_low, gate_up, second, own, other, mixed, gain_b, xin, x_block, gain_a, query,
                 kv_mine, kv_other, lse, weight, out_t, earlier=None):
        part, for_own, for_other = feed_back(grad_low, own, other, gate_up)
        pieces = exchange(part.reshape(8, 32, WIDTH), ("z", "x"))
        given = swap(for_other, "c")
        second_other, grad_other = swap(second, "c"), swap(grad_low, "c")
        grad_ffn = feed_grad(second, second_other, grad_low, grad_other, for_own, given)
        pieces, grad_ffn = lax.optimization_barrier((pieces, grad_ffn))
        grad_mixed, low, grad_gain_b = before_heads(pieces, mixed, gain_b, grad_out)
        grad_att = gathered(low, ("x", "c"))
        if earlier is not None:
            grad_ffn = after(grad_ffn, (earlier, grad_att))
        grad_ffn = lax.psum_scatter(grad_ffn, "y", scatter_dimension=0, tiled=True)
        grad_query, kept_half, sent_half = attend_back(
            flag, query, kv_mine, kv_other, seg_col, seg_row, lse, grad_att, out_t, cosine, sine
        )
        grad_kv = (kept_half + swap(sent_half, "c").astype(F32)).astype(BF)
        grad_kv = exchange(grad_kv.reshape(16, HEAD, HEAD), ("y", "z"))
        grad_qkv, grad_bias, grad_gain_a, part = qkv_back(flag, grad_kv, grad_query, weight, x_block, cosine, sine)
        pieces = exchange(part, ("x", "c"))
        grad_in, low = layer_start(pieces, xin, gain_a, grad_mixed)
        return grad_in, low, grad_qkv, grad_att, grad_ffn, (grad_bias, grad_gain_a, grad_gain_b)

    grad_two, low, grad_qkv2, grad_att2, ffn_two, small_two = backward(
        cot, cot_low, gate_up2, second2, own2, other2, mixed2, gain_b2, out_one, x_block2, gain_a2, query2, kv_mine2,
        kv_other2, lse2, all_second, all_second
    )
    grad_low = exchange(low, ("z", "x")).reshape(256, WIDTH)
    (attn_two,) = weight_grad(y_then_z, False, normed2, grad_qkv2, grad_att2, attended2, *small_two)
    attn_two, grad_low = lax.optimization_barrier((attn_two, grad_low))
    attn_two = after(attn_two, ffn_two)
    attn_two = lax.psum_scatter(attn_two.reshape(16 * 112, 896), "z", scatter_dimension=0, tiled=True)
    grad_one, _, grad_qkv1, grad_att1, ffn_one, small_one = backward(
        grad_two, grad_low, gate_up1, second1, own1, other1, mixed1, gain_b1, xin, x_block1, gain_a1, query1, kv_mine1,
        kv_other1, lse1, qkv_first, out_first, attn_two
    )
    out_two = after_feed(exchange(after(last_part, grad_one).reshape(8, 32, WIDTH), ("z", "x")), mixed2)
    parts = weight_grad(y_then_z, True, normed1, grad_qkv1, grad_att1, attended1, *small_one)
    ffn_payload = jnp.concatenate([ffn_one, ffn_two], axis=0).reshape(8, 96, FW)
    ffn_sum = exchange(ffn_payload, ("s", "z"))
    attn_one, halfway = ring_scatter(parts, (ffn_payload, out_two), ffn_sum)
    attn_two = lax.psum_scatter(after(attn_two, (ffn_one, grad_one, halfway)), "y", scatter_dimension=0, tiled=True)

    grad_gate, grad_up, grad_down = unpack(ffn_sum)
    attn_sum = pick(attn_one, attn_two).astype(F32) + swap(pick(attn_two, attn_one), "s").astype(F32)
    main, row = attn_sum[:96], attn_sum[96]
    gains = jnp.concatenate([row[512:608].reshape(4, 24), row[640:736].reshape(4, 24)], axis=1)
    payload = jnp.concatenate(
        [
            main[:, QCOLS:512].reshape(4, 24, HEAD),
            jnp.pad(gains, ((0, 0), (0, HEAD - 48)))[:, None],
            jnp.broadcast_to(row[None, None, QCOLS:512], (4, 1, HEAD)),
            jnp.zeros((4, 6, HEAD), F32),
        ],
        axis=1,
    )
    arrived = [lax.dynamic_index_in_dim(payload, member, 0, keepdims=False)]
    for step in (1, 2, 3):
        given = lax.dynamic_index_in_dim(payload, member ^ step, 0, keepdims=False)
        arrived.append(lax.ppermute(given, ("x", "c"), [(m, m ^ step) for m in range(4)]))
    arrived = jnp.stack(arrived)
    payload = jnp.stack([lax.dynamic_index_in_dim(arrived, member ^ b, 0, keepdims=False) for b in BLOCK_ORDER])
    grad_keyval = payload[:, :24].transpose(1, 0, 2).reshape(24, 512)
    gains = jnp.sum(payload[:, 24], axis=0)
    kv_bias_row = lax.dynamic_index_in_dim(payload[:, 25], lax.axis_index("y"), 0, keepdims=False)
    grad_b_keyval = lax.dynamic_slice_in_dim(kv_bias_row, (lax.axis_index("z") * 4 + member) * 8, 8, 0)

    def both(first, second):
        given = swap(pick(second, first), "s")
        return jnp.stack([pick(first, given), pick(given, second)])[None]

    return (
        both(out_one, out_two),
        both(grad_one, grad_two),
        gains[None, :24],
        main[None, :, :QCOLS],
        row[None, :QCOLS],
        grad_keyval[None],
        grad_b_keyval[None],
        main[:, 512:].T[None],
        gains[None, 24:48],
        grad_gate[None],
        grad_up[None],
        grad_down[None],
    )


def solution(mesh):
    fine = Mesh(np.asarray(mesh.devices).reshape(2, 4, 4, 2, 2), AXES)
    block, member = ("y", "z"), ("x", "c")
    every = block + member
    tokens = P(None, every, None)
    split = P("s", every)
    columns = P("s", block, member)
    rows = P("s", member, block)
    keyval = P("s", every, None)
    outs = P("s", None, every, None)
    return jax.shard_map(
        local,
        mesh=fine,
        in_specs=(
            tokens, tokens, P(), split, columns, P("s", member), keyval, split, rows, split, columns, columns, rows,
        ),
        out_specs=(
            outs, outs, split, columns, P("s", member), keyval, split, rows, split, columns, columns, rows,
        ),
        check_vma=False,
    )
```

time: 825 us -> 639 us (0.77)
  Pallas kernels: 0 us -> 108 us
  matrix products: 92.1 us -> 0 us
  waiting for transfers between devices: 293 us -> 216 us
  local copies, waits for them, and re-layouts: 105 us -> 33 us
  other arithmetic: 75.2 us -> 17.8 us
    unnamed x10 -> x7, waiting for transfers between devices: 123 us -> 0.12 us
    pallas_call x0 -> x27, Pallas kernels: none -> 108 us  [call(): pl.pallas_call(kernel, out_shape=out_shape, in_specs=in_specs, scratch_sh...]
    dot_general x42 -> x0, matrix products: 92.1 us -> none  [the longest x14 36.9 us: nn(): return jnp.dot(left, right, preferred_element_type=F32)]
    ppermute x4 -> x15, waiting for transfers between devices: 1.57 us -> 80.5 us  [the longest x12 79.8 us: shifted(): return lax.ppermute(value, axis, [(i, (i + steps) % 4) for i in range(4)])]
    ppermute x16 -> x18, waiting for transfers between devices: 50 us -> 16.1 us  [swap(): return lax.ppermute(value, axis, [(0, 1), (1, 0)])]
    all_to_all x14 -> x12, waiting for transfers between devices: 92.6 us -> 58.9 us  [exchange(): return lax.all_to_all(value, axes, split_axis=0, concat_axis=0, tiled=True)]
    reduce_scatter x2 -> x4, waiting for transfers between devices: 0.02 us -> 23.8 us  [the longest x1 9.23 us: local(): lax.psum_scatter(after(attn_two, (ffn_one, grad_one, halfway)), 'y', scat...]
    slice x33 -> x10, local copies, waits for them, and re-layouts: 22.8 us -> 1.58 us  [the longest x2 0.78 us: smalls(): bits = tail[:, :4, QCOLS:QCOLS + 56].reshape(64, 56)]
  transfers between devices with their start and end apart: 42 -> 52, of which waited for: 25 -> 28; matrix products, arithmetic and copies ran while one was open for 28% -> 4% of each run, Pallas kernels for 0% -> 15%
where the time goes in v2:
time: 639 us; the launch traced here: 629 us
  waiting for transfers between devices  216 us (34%)
  blocking collectives  133 us (21%)
  Pallas kernels  108 us (17%)
  starting transfers between devices  105 us (16%)
  local copies, waits for them, and re-layouts  33 us (5%)
  other arithmetic  17.8 us (3%)
  between operations  15.3 us (2%)
    all_to_all x7, blocking collectives, exchange(): return lax.all_to_all(value, axes, split_axis=0, concat_axis=0, tiled=True)  112 us
    pallas_call x27, Pallas kernels, call(): pl.pallas_call(kernel, out_shape=out_shape, in_specs=in_specs, scratch_sh...  108 us
    ppermute x12, waiting for transfers between devices, shifted(): return lax.ppermute(value, axis, [(i, (i + steps) % 4) for i in range(4)])  79.8 us
    all_to_all x12, waiting for transfers between devices, exchange(): return lax.all_to_all(value, axes, split_axis=0, concat_axis=0, tiled=True)  58.9 us
    all_to_all x12, starting transfers between devices, exchange(): return lax.all_to_all(value, axes, split_axis=0, concat_axis=0, tiled=True)  55.2 us
    all_gather x3, waiting for transfers between devices, gathered(): return lax.all_gather(piece, axes, axis=0, tiled=True)  37.1 us
    ppermute x18, starting transfers between devices, swap(): return lax.ppermute(value, axis, [(0, 1), (1, 0)])  25.6 us
    all_gather x3, blocking collectives, gathered(): return lax.all_gather(piece, axes, axis=0, tiled=True)  21.6 us
  transfers between devices with their start and end apart: 52, of which 28 were waited for; matrix products, arithmetic and copies ran while one was open for 4% of the time, Pallas kernels for 15%

profile of v2, /device:TPU:1, one launch (start us, length us, event | category | flops | bytes accessed | tf_op | source)
XLA Modules:
  0.0 629.1 jit_solution(1059586147063031452)
XLA Ops:
  52.9 14.9 %collective-permute-done.6.refs_2_ = bf16[4,112,896]{2,1,0:T(8,128)(2,1)S(1)} collective-permute-done((bf16[4,112,896]{2,1,0:T(8,128)(2,1)S(1)}, bf16[4,112,896]{2,1,0:T(8,128)(2,1)S(1)}, u32[]{:S(2)}, u32[]{:S(2)}) %collective-permute-start.6) | collective-permute-done | bytes 802848 | tf_op jit(solution)/shard_map/ppermute | solution.py:385
  67.8 18.2 %collective-permute-done.7.refs_3_ = bf16[4,112,896]{2,1,0:T(8,128)(2,1)S(1)} collective-permute-done((bf16[4,112,896]{2,1,0:T(8,128)(2,1)S(1)}, bf16[4,112,896]{2,1,0:T(8,128)(2,1)S(1)}, u32[]{:S(2)}, u32[]{:S(2)}) %collective-permute-start.7) | collective-permute-done | bytes 802848 | tf_op jit(solution)/shard_map/ppermute | solution.py:385
  105.5 12.7 %all-to-all-done.1 = bf16[16,128,128]{2,1,0:T(8,128)(2,1)S(1)} async-done(((bf16[16,128,128]{2,1,0:T(8,128)(2,1)}), bf16[16,128,128]{2,1,0:T(8,128)(2,1)S(1)}, u32[]{:S(2)}, u32[]{:S(2)}) %all-to-all-start.1) | async-done | bytes 524320 | tf_op jit(solution)/shard_map/all_to_all | solution.py:37
  144.9 11.6 %all-to-all-done.3 = bf16[8,32,1536]{2,1,0:T(8,128)(2,1)S(1)} async-done(((bf16[8,32,1536]{2,1,0:T(8,128)(2,1)}), bf16[8,32,1536]{2,1,0:T(8,128)(2,1)S(1)}, u32[]{:S(2)}, u32[]{:S(2)}) %all-to-all-start.3) | async-done | bytes 786464 | tf_op jit(solution)/shard_map/all_to_all | solution.py:37
  156.5 15.0 %all_to_all.95 = bf16[8,32,1536]{2,1,0:T(8,128)(2,1)} all-to-all(bf16[8,32,1536]{2,1,0:T(8,128)(2,1)S(1)} %broadcast_in_dim.70), channel_id=1, replica_groups=mesh['s'=2,'y'=4,'z'=4,'x'=2,'c'=2] {'z','x'}, dimensions={0} | all-to-all | bytes 1572864 | tf_op jit(solution)/shard_map/all_to_all | solution.py:37
  174.4 9.4 %collective-permute-done.10.other = bf16[1536,1920]{1,0:T(8,128)(2,1)S(1)} collective-permute-done((bf16[1536,1920]{1,0:T(8,128)(2,1)}, bf16[1536,1920]{1,0:T(8,128)(2,1)S(1)}, u32[]{:S(2)}, u32[]{:S(2)}) %collective-permute-start.10) | collective-permute-done | bytes 5898272 | tf_op jit(solution)/shard_map/ppermute | solution.py:33
  186.4 7.8 %shard_map.225 = (bf16[256,1536]{1,0:T(8,128)(2,1)}, bf16[2,256,1280]{2,1,0:T(8,128)(2,1)}) custom-call(bf16[256,1536]{1,0:T(8,128)(2,1)S(1)} %bitcast.115, bf16[1536,1920]{1,0:T(8,128)(2,1)} %bitcast.140, bf16[1536,1920]{1,0:T(8,128)(2,1)} %copy-done.46), custom_call_target="tpu_custom_call" | custom-call | flops 3019898880 | bytes 15000000 | tf_op jit(solution)/shard_map/pallas_call | solution.py:61
  197.8 21.3 %all-gather.5.cloned.1.call-done = bf16[1792,896]{1,0:T(8,128)(2,1)} async-done(((bf16[112,896]{1,0:T(8,128)(2,1)}), bf16[1792,896]{1,0:T(8,128)(2,1)}) %all-gather.5.cloned.1.call-update) | async-done | bytes 3211280 | tf_op jit(solution)/shard_map/all_gather | solution.py:593
  221.1 7.8 %all_gather.19.xin = bf16[128,1536]{1,0:T(8,128)(2,1)S(1)} all-gather(bf16[32,1536]{1,0:T(8,128)(2,1)S(1)} %shard_map.226.xin), channel_id=1, replica_groups=mesh['s'=2,'y'=4,'z'=4,'x'=2,'c'=2] {'x','c'}, dimensions={0}, use_global_device_ids=true | all-gather | bytes 491520 | tf_op jit(solution)/shard_map/all_gather | solution.py:593
  231.7 18.4 %all_to_all.96 = bf16[16,128,128]{2,1,0:T(8,128)(2,1)S(1)} all-to-all(bf16[16,128,128]{2,1,0:T(8,128)(2,1)S(1)} %get-tuple-element.111), channel_id=1, replica_groups=mesh['s'=2,'y'=4,'z'=4,'x'=2,'c'=2] {'y','z'}, dimensions={0} | all-to-all | bytes 1048576 | tf_op jit(solution)/shard_map/all_to_all | solution.py:37
  272.7 15.8 %all-gather.7.cloned.1.call-done.own = bf16[1536,1920]{1,0:T(8,128)(2,1)} async-done(((bf16[384,1920]{1,0:T(8,128)(2,1)}), bf16[1536,1920]{1,0:T(8,128)(2,1)}) %all-gather.7.cloned.1.call-update) | async-done | bytes 5898256 | tf_op jit(solution)/shard_map/all_gather | solution.py:593
  289.2 18.2 %all_to_all.97 = bf16[8,32,1536]{2,1,0:T(8,128)(2,1)S(1)} all-to-all(bf16[8,32,1536]{2,1,0:T(8,128)(2,1)} %copy-done.11), channel_id=1, replica_groups=mesh['s'=2,'y'=4,'z'=4,'x'=2,'c'=2] {'z','x'}, dimensions={0} | all-to-all | bytes 1572864 | tf_op jit(solution)/shard_map/all_to_all | solution.py:37
  309.9 7.8 %shard_map.230 = (bf16[256,1536]{1,0:T(8,128)(2,1)}, bf16[2,256,1280]{2,1,0:T(8,128)(2,1)}) custom-call(bf16[256,1536]{1,0:T(8,128)(2,1)S(1)} %bitcast.118, bf16[1536,1920]{1,0:T(8,128)(2,1)} %all-gather.7.cloned.1.call-done.own, bf16[1536,1920]{1,0:T(8,128)(2,1)} %copy-done.47), custom_call_target="tpu_custom_call" | custom-call | flops 3019898880 | bytes 15000000 | tf_op jit(solution)/shard_map/pallas_call | solution.py:61
  332.3 8.5 %shard_map.232 = bf16[1536,1920]{1,0:T(8,128)(2,1)} custom-call(bf16[256,1536]{1,0:T(8,128)(2,1)S(1)} %bitcast.120, bf16[256,1536]{1,0:T(8,128)(2,1)} %collective-permute-done.13.tokens_other, bf16[256,1536]{1,0:T(8,128)(2,1)} %bitcast.24.grads, bf16[256,1536]{1,0:T(8,128)(2,1)} %collective-permute-done.14.grads_other, ...), custom_call_target="tpu_custom_call" | custom-call | flops 3019898880 | bytes 12000000 | tf_op jit(solution)/shard_map/pallas_call | solution.py:61
  353.6 8.9 %shard_map.234 = (bf16[128,384]{1,0:T(8,128)(2,1)S(1)}, f32[2048,128]{1,0:T(8,128)}, bf16[2048,128]{1,0:T(8,128)(2,1)S(1)}) custom-call(s32[2]{0:T(128)S(1)} %pad_add_fusion.flag, bf16[3,128,128]{2,1,0:T(8,128)(2,1)S(1)} %get-tuple-element.110.query, bf16[2048,128]{1,0:T(8,128)(2,1)S(1)} %bitcast.114, bf16[2048,128]{1,0:T(8,128)(2,1)} %copy-done.1, ...), custom_call_target="tpu_custom_call" | custom-call | flops 1560281088 | bytes 5000000 | tf_op jit(solution)/shard_map/pallas_call | solution.py:61
  365.7 19.1 %all_to_all.98.pieces = bf16[16,128,128]{2,1,0:T(8,128)(2,1)S(1)} all-to-all(bf16[16,128,128]{2,1,0:T(8,128)(2,1)S(1)} %bitcast.144), channel_id=1, replica_groups=mesh['s'=2,'y'=4,'z'=4,'x'=2,'c'=2] {'y','z'}, dimensions={0} | all-to-all | bytes 1048576 | tf_op jit(solution)/shard_map/all_to_all | solution.py:37
  387.5 10.7 %all_to_all.99.pieces = bf16[4,32,1536]{2,1,0:T(8,128)(2,1)S(1)} all-to-all(bf16[4,32,1536]{2,1,0:T(8,128)(2,1)S(1)} %get-tuple-element.135), channel_id=1, replica_groups=mesh['s'=2,'y'=4,'z'=4,'x'=2,'c'=2] {'x','c'}, dimensions={0} | all-to-all | bytes 786432 | tf_op jit(solution)/shard_map/all_to_all | solution.py:37
  415.4 7.8 %shard_map.238 = (bf16[256,1536]{1,0:T(8,128)(2,1)S(1)}, bf16[256,1920]{1,0:T(8,128)(2,1)}, bf16[256,1920]{1,0:T(8,128)(2,1)}) custom-call(bf16[256,1536]{1,0:T(8,128)(2,1)S(1)} %bitcast.121, bf16[1536,1920]{1,0:T(8,128)(2,1)} %bitcast.141, bf16[1536,1920]{1,0:T(8,128)(2,1)} %copy-done.46, bf16[2,256,1280]{2,1,0:T(8,128)(2,1)} %get-tuple-element.139.gate_up_in), custom_call_target="tpu_custom_call" | custom-call | flops 3019898880 | bytes 17000000 | tf_op jit(solution)/shard_map/pallas_call | solution.py:61
  430.8 8.6 %shard_map.239 = bf16[1536,1920]{1,0:T(8,128)(2,1)} custom-call(bf16[256,1536]{1,0:T(8,128)(2,1)S(1)} %bitcast.117, bf16[256,1536]{1,0:T(8,128)(2,1)} %collective-permute-done.17.tokens_other, bf16[256,1536]{1,0:T(8,128)(2,1)} %bitcast.123, bf16[256,1536]{1,0:T(8,128)(2,1)} %collective-permute-done.18.grads_other, bf16[256,1920]{1,0:T(8,128)(2,1)} %get-tuple-element.141.own, ...), custom_call_target="tpu_custom_call" | custom-call | flops 3019898880 | bytes 12000000 | tf_op jit(solution)/shard_map/pallas_call | solution.py:61
  463.5 7.9 %shard_map.241 = (bf16[128,384]{1,0:T(8,128)(2,1)S(1)}, f32[2048,128]{1,0:T(8,128)}, bf16[2048,128]{1,0:T(8,128)(2,1)S(1)}) custom-call(s32[2]{0:T(128)S(1)} %copy-done.27, bf16[3,128,128]{2,1,0:T(8,128)(2,1)S(1)} %copy-done.20, bf16[2048,128]{1,0:T(8,128)(2,1)S(1)} %bitcast.127, bf16[2048,128]{1,0:T(8,128)(2,1)} %copy-done.14, s32[2048,1]{1,0:T(8,128)} %copy.51.seg_col, ...), custom_call_target="tpu_custom_call" | custom-call | flops 1560281088 | bytes 5000000 | tf_op jit(solution)/shard_map/pallas_call | solution.py:61
  475.2 19.2 %all_to_all.100.pieces = bf16[16,128,128]{2,1,0:T(8,128)(2,1)S(1)} all-to-all(bf16[16,128,128]{2,1,0:T(8,128)(2,1)S(1)} %bitcast.145), channel_id=1, replica_groups=mesh['s'=2,'y'=4,'z'=4,'x'=2,'c'=2] {'y','z'}, dimensions={0} | all-to-all | bytes 1048576 | tf_op jit(solution)/shard_map/all_to_all | solution.py:37
  496.6 11.2 %all_to_all.101.pieces = bf16[4,32,1536]{2,1,0:T(8,128)(2,1)S(1)} all-to-all(bf16[4,32,1536]{2,1,0:T(8,128)(2,1)S(1)} %get-tuple-element.149), channel_id=1, replica_groups=mesh['s'=2,'y'=4,'z'=4,'x'=2,'c'=2] {'x','c'}, dimensions={0} | all-to-all | bytes 786432 | tf_op jit(solution)/shard_map/all_to_all | solution.py:37
  544.3 31.4 %collective-permute-done.24 = bf16[4,112,896]{2,1,0:T(8,128)(2,1)} collective-permute-done((bf16[4,112,896]{2,1,0:T(8,128)(2,1)}, bf16[4,112,896]{2,1,0:T(8,128)(2,1)}, u32[]{:S(2)}, u32[]{:S(2)}) %collective-permute-start.24) | collective-permute-done | bytes 802848 | tf_op jit(solution)/shard_map/ppermute | solution.py:385
  596.4 9.2 %reduce-scatter.11.cloned.1.call-done = bf16[112,896]{1,0:T(8,128)(2,1)} async-done(((bf16[448,896]{1,0:T(8,128)(2,1)}), bf16[112,896]{1,0:T(8,128)(2,1)}) %reduce-scatter.11.cloned.1.call-update) | async-done | bytes 200720 | tf_op jit(solution)/shard_map/reduce_scatter | solution.py:723
  (327 shorter events, 292.5 us)
Async XLA Ops:
  8.1 18.7 %collective-permute-start.2 = (bf16[112,768]{1,0:T(8,128)(2,1)S(1)}, bf16[112,768]{1,0:T(8,128)(2,1)S(1)}, u32[]{:S(2)}, u32[]{:S(2)}) collective-permute-start(bf16[112,768]{1,0:T(8,128)(2,1)S(1)} %fusion.8), channel_id=1, source_target_pairs={{0,64},{64,0},{1,65},{65,1},{2,66},{66,2},{3,67},{67,3},{4,68},{68... | collective-permute-start | bytes 516104 | tf_op jit(solution)/shard_map/ppermute | solution.py:33
  41.7 44.2 %all-to-all-start.5 = ((bf16[8,96,1920]{2,1,0:T(8,128)(2,1)}), bf16[8,96,1920]{2,1,0:T(8,128)(2,1)}, u32[]{:S(2)}, u32[]{:S(2)}) async-start(bf16[8,96,1920]{2,1,0:T(8,128)(2,1)} %shard_map.224), calls=%async_computation.5 | async-start | bytes 5898240 | tf_op jit(solution)/shard_map/all_to_all | solution.py:37
  47.8 123.8 %all-gather.9.cloned.1.call-start = ((), (), s32[]{:S(2)}) async-start(), calls=%async_computation.29 | async-start | bytes 7372800 | tf_op jit(solution)/shard_map/all_gather | solution.py:593
  47.8 20.0 %collective-permute-start.6 = (bf16[4,112,896]{2,1,0:T(8,128)(2,1)S(1)}, bf16[4,112,896]{2,1,0:T(8,128)(2,1)S(1)}, u32[]{:S(2)}, u32[]{:S(2)}) collective-permute-start(bf16[4,112,896]{2,1,0:T(8,128)(2,1)S(1)} %pad_maximum_fusion.1.refs_1_), channel_id=1, source_target_pairs={{0,16},{16,32},{32,48},{48,0},{1,17},{17,33},{33,49},{49,1},{2,18}... | collective-permute-start | bytes 2408456 | tf_op jit(solution)/shard_map/ppermute | solution.py:385
  49.2 36.8 %collective-permute-start.7 = (bf16[4,112,896]{2,1,0:T(8,128)(2,1)S(1)}, bf16[4,112,896]{2,1,0:T(8,128)(2,1)S(1)}, u32[]{:S(2)}, u32[]{:S(2)}) collective-permute-start(bf16[4,112,896]{2,1,0:T(8,128)(2,1)S(1)} %pad_maximum_fusion.1.refs_1_), channel_id=1, source_target_pairs={{0,32},{16,48},{32,0},{48,16},{1,33},{17,49},{33,1},{49,17},{2,34}... | collective-permute-start | bytes 2408456 | tf_op jit(solution)/shard_map/ppermute | solution.py:385
  51.8 34.2 %collective-permute-start.8 = (bf16[4,112,896]{2,1,0:T(8,128)(2,1)S(1)}, bf16[4,112,896]{2,1,0:T(8,128)(2,1)}, u32[]{:S(2)}, u32[]{:S(2)}) collective-permute-start(bf16[4,112,896]{2,1,0:T(8,128)(2,1)S(1)} %pad_maximum_fusion.1.refs_1_), channel_id=1, source_target_pairs={{0,48},{16,0},{32,16},{48,32},{1,49},{17,1},{33,17},{49,33},{2,50}... | collective-permute-start | bytes 2408456 | tf_op jit(solution)/shard_map/ppermute | solution.py:385
  97.1 21.1 %all-to-all-start.1 = ((bf16[16,128,128]{2,1,0:T(8,128)(2,1)}), bf16[16,128,128]{2,1,0:T(8,128)(2,1)S(1)}, u32[]{:S(2)}, u32[]{:S(2)}) async-start(bf16[16,128,128]{2,1,0:T(8,128)(2,1)} %get-tuple-element.99), calls=%async_computation.1 | async-start | bytes 1048576 | tf_op jit(solution)/shard_map/all_to_all | solution.py:37
  104.1 115.0 %all-gather.5.cloned.1.call-start = ((), (), s32[]{:S(2)}) async-start(), calls=%async_computation.23 | async-start | bytes 3411968 | tf_op jit(solution)/shard_map/all_gather | solution.py:593
  144.8 143.7 %all-gather.7.cloned.1.call-start = ((), (), s32[]{:S(2)}) async-start(), calls=%async_computation.24 | async-start | bytes 7372800 | tf_op jit(solution)/shard_map/all_gather | solution.py:593
  194.2 26.7 %all-to-all-start.6 = ((bf16[8,32,1536]{2,1,0:T(8,128)(2,1)}), bf16[8,32,1536]{2,1,0:T(8,128)(2,1)S(1)}, u32[]{:S(2)}, u32[]{:S(2)}) async-start(bf16[8,32,1536]{2,1,0:T(8,128)(2,1)} %bitcast.30), calls=%async_computation.6 | async-start | bytes 1572864 | tf_op jit(solution)/shard_map/all_to_all | solution.py:37
  288.5 18.9 %collective-permute-start.12 = (bf16[1536,1920]{1,0:T(8,128)(2,1)}, bf16[1536,1920]{1,0:T(8,128)(2,1)S(1)}, u32[]{:S(2)}, u32[]{:S(2)}) collective-permute-start(bf16[1536,1920]{1,0:T(8,128)(2,1)} %all-gather.7.cloned.1.call-done.own), channel_id=1, source_target_pairs={{0,1},{1,0},{2,3},{3,2},{4,5},{5,4},{6,7},{7,6},{8,9},{9,8},{10,11... | collective-permute-start | bytes 17694728 | tf_op jit(solution)/shard_map/ppermute | solution.py:33
  328.0 17.3 %all-to-all-start.10 = ((bf16[8,32,1536]{2,1,0:T(8,128)(2,1)}), bf16[8,32,1536]{2,1,0:T(8,128)(2,1)}, u32[]{:S(2)}, u32[]{:S(2)}) async-start(bf16[8,32,1536]{2,1,0:T(8,128)(2,1)} %bitcast.129), calls=%async_computation.10 | async-start | bytes 1572864 | tf_op jit(solution)/shard_map/all_to_all | solution.py:37
  332.2 83.2 %reduce-scatter.5.cloned.1.call-start = ((), (), s32[]{:S(2)}) async-start(), calls=%async_computation.25 | async-start | bytes 7372800 | tf_op jit(solution)/shard_map/reduce_scatter | solution.py:694
  399.4 16.0 %all-to-all-start.13 = ((bf16[8,32,1536]{2,1,0:T(8,128)(2,1)}), bf16[8,32,1536]{2,1,0:T(8,128)(2,1)S(1)}, u32[]{:S(2)}, u32[]{:S(2)}) async-start(bf16[8,32,1536]{2,1,0:T(8,128)(2,1)} %copy-done.10), calls=%async_computation.13 | async-start | bytes 1572864 | tf_op jit(solution)/shard_map/all_to_all | solution.py:37
  403.7 58.8 %reduce-scatter.7.cloned.1.call-start = ((), (), s32[]{:S(2)}) async-start(), calls=%async_computation.26 | async-start | bytes 4014080 | tf_op jit(solution)/shard_map/reduce_scatter | solution.py:713
  426.8 20.3 %all-to-all-start.14 = ((bf16[8,32,1536]{2,1,0:T(8,128)(2,1)}), bf16[8,32,1536]{2,1,0:T(8,128)(2,1)S(1)}, u32[]{:S(2)}, u32[]{:S(2)}) async-start(bf16[8,32,1536]{2,1,0:T(8,128)(2,1)} %bitcast.130), calls=%async_computation.14 | async-start | bytes 1572864 | tf_op jit(solution)/shard_map/all_to_all | solution.py:37
  430.3 100.5 %reduce-scatter.9.cloned.1.call-start = ((), (), s32[]{:S(2)}) async-start(), calls=%async_computation.27 | async-start | bytes 7372800 | tf_op jit(solution)/shard_map/reduce_scatter | solution.py:694
  508.9 25.6 %all-to-all-start.17 = ((bf16[8,32,1536]{2,1,0:T(8,128)(2,1)}), bf16[8,32,1536]{2,1,0:T(8,128)(2,1)S(1)}, u32[]{:S(2)}, u32[]{:S(2)}) async-start(bf16[8,32,1536]{2,1,0:T(8,128)(2,1)} %bitcast.44), calls=%async_computation.17 | async-start | bytes 1572864 | tf_op jit(solution)/shard_map/all_to_all | solution.py:37
  518.2 26.1 %collective-permute-start.23 = (bf16[4,112,896]{2,1,0:T(8,128)(2,1)}, bf16[4,112,896]{2,1,0:T(8,128)(2,1)}, u32[]{:S(2)}, u32[]{:S(2)}) collective-permute-start(bf16[4,112,896]{2,1,0:T(8,128)(2,1)} %get-tuple-element.160), channel_id=1, source_target_pairs={{0,4},{4,8},{8,12},{12,0},{1,5},{5,9},{9,13},{13,1},{2,6},{6,10},{... | collective-permute-start | bytes 2408456 | tf_op jit(solution)/shard_map/ppermute | solution.py:385
  519.8 56.0 %collective-permute-start.24 = (bf16[4,112,896]{2,1,0:T(8,128)(2,1)}, bf16[4,112,896]{2,1,0:T(8,128)(2,1)}, u32[]{:S(2)}, u32[]{:S(2)}) collective-permute-start(bf16[4,112,896]{2,1,0:T(8,128)(2,1)} %get-tuple-element.167), channel_id=1, source_target_pairs={{0,8},{4,12},{8,0},{12,4},{1,9},{5,13},{9,1},{13,5},{2,10},{6,14},... | collective-permute-start | bytes 2408456 | tf_op jit(solution)/shard_map/ppermute | solution.py:385
  522.1 53.7 %collective-permute-start.25 = (bf16[4,112,896]{2,1,0:T(8,128)(2,1)}, bf16[4,112,896]{2,1,0:T(8,128)(2,1)}, u32[]{:S(2)}, u32[]{:S(2)}) collective-permute-start(bf16[4,112,896]{2,1,0:T(8,128)(2,1)} %get-tuple-element.169), channel_id=1, source_target_pairs={{0,12},{4,0},{8,4},{12,8},{1,13},{5,1},{9,5},{13,9},{2,14},{6,2},{... | collective-permute-start | bytes 2408456 | tf_op jit(solution)/shard_map/ppermute | solution.py:385
  534.5 57.4 %all-to-all-start.18 = ((bf16[8,96,1920]{2,1,0:T(8,128)(2,1)}), bf16[8,96,1920]{2,1,0:T(8,128)(2,1)}, u32[]{:S(2)}, u32[]{:S(2)}) async-start(bf16[8,96,1920]{2,1,0:T(8,128)(2,1)} %bitcast.143), calls=%async_computation.21 | async-start | bytes 5898240 | tf_op jit(solution)/shard_map/all_to_all | solution.py:37
  541.1 64.6 %reduce-scatter.11.cloned.1.call-start = ((), (), s32[]{:S(2)}) async-start(), calls=%async_computation.28 | async-start | bytes 1003520 | tf_op jit(solution)/shard_map/reduce_scatter | solution.py:723
  541.3 37.4 %collective-permute-start.22 = (bf16[32,1536]{1,0:T(8,128)(2,1)S(1)}, bf16[32,1536]{1,0:T(8,128)(2,1)S(1)}, u32[]{:S(2)}, u32[]{:S(2)}) collective-permute-start(bf16[32,1536]{1,0:T(8,128)(2,1)S(1)} %broadcast_select_fusion.7), channel_id=1, source_target_pairs={{0,64},{64,0},{1,65},{65,1},{2,66},{66,2},{3,67},{67,3},{4,68},{68... | collective-permute-start | bytes 294920 | tf_op jit(solution)/shard_map/ppermute | solution.py:33
  (84 other events, 1504.7 us)
Sparse Core Ops, SparseCore 0:
  90.1 69.8 all-gather.8
  162.7 56.2 all-gather.4
  220.7 67.6 all-gather.6
  345.5 64.9 reduce-scatter.4
  415.5 46.8 reduce-scatter.6
  464.9 65.9 reduce-scatter.8
  578.8 26.8 reduce-scatter.10

commit v3 on v2

--- a/solution.py
+++ b/solution.py
@@ -57,13 +57,13 @@
     return lax.rsqrt(jnp.mean(values * values, axis=-1, keepdims=True) + EPS)
 
 
-def call(kernel, out_shape, in_specs, args, scratch=(), flops=0, size=0, exps=0, **more):
+def call(kernel, out_shape, in_specs, args, scratch=(), flops=0, size=0, exps=0, limit=52, **more):
     return pl.pallas_call(
         kernel,
         out_shape=out_shape,
         in_specs=in_specs,
         scratch_shapes=list(scratch),
-        compiler_params=pltpu.CompilerParams(vmem_limit_bytes=52 * 1024 * 1024),
+        compiler_params=pltpu.CompilerParams(vmem_limit_bytes=limit * 1024 * 1024),
         cost_estimate=pl.CostEstimate(flops=flops, bytes_accessed=size, transcendentals=exps),
         **more,
     )(*args)
@@ -385,85 +385,104 @@
     return lax.ppermute(value, axis, [(i, (i + steps) % 4) for i in range(4)])
 
 
-def ring_gather(piece, first, second, done):
-    some = after(jnp.stack([piece] + [shifted(piece, first, j) for j in (1, 2, 3)]), done)
-    return [some] + [shifted(some, second, k) for k in (1, 2, 3)]
+def ring_first(piece, axis):
+    return jnp.stack([piece] + [shifted(piece, axis, j) for j in (1, 2, 3)])
+
+
+def ring_second(blocks, axis):
+    return [blocks] + [shifted(blocks, axis, k) for k in (1, 2, 3)]
 
 
 def ring_block(place, j, k):
     return lax.rem(place[0] + 4 - j, 4) * place[1] + lax.rem(place[2] + 4 - k, 4) * place[3]
 
 
-def assemble_kernel(columns, place, *refs):
-    pieces, outs, tail = refs[:4], refs[4:-1], refs[-1]
+def assemble_kernel(place, *refs):
+    pieces, out, tail = refs[:4], refs[4], refs[5] if len(refs) > 5 else None
     for k in range(4):
         for j in range(4):
             block = ring_block(place, j, k)
-            first = 0
-            for out, size in zip(outs, columns, strict=True):
-                at = pl.ds(pl.multiple_of(block * 96, 32), 96)
-                out[at, :] = pieces[k][j, pl.ds(0, 96), pl.ds(first, size)]
-                first += size
-            tail[block] = pieces[k][j, pl.ds(96, 16), pl.ds(0, 512)]
-
-
-def assemble(place, pieces, columns):
-    return call(
-        lambda *refs: assemble_kernel(columns, *refs),
-        tuple(arr((WIDTH, size)) for size in columns) + (arr((16, 16, 512)),),
+            out[pl.ds(pl.multiple_of(block * 96, 32), 96), :] = pieces[k][j, pl.ds(0, 96), :]
+            if tail is not None:
+                tail[block] = pieces[k][j, pl.ds(96, 16), :]
+
+
+def assemble(place, pieces):
+    _, rows, columns = pieces[0].shape
+    whole, tail = arr((WIDTH, columns)), arr((16, 16, columns))
+    return call(
+        assemble_kernel,
+        whole if rows == 96 else (whole, tail),
         [SMEM] + [VMEM] * 4,
         (place, *pieces),
-        size=7_000_000,
-    )
-
-
-def weight_grad_kernel(place, normed, grad_qkv, grad_att, attended, bias, gain_a, gain_b, *rest):
-    outs, scratch = rest[:-1], rest[-1]
+        size=4_000_000,
+    )
+
+
+def weight_grad_kernel(normed, grad_qkv, grad_att, attended, out, scratch):
     scratch[:, pl.ds(0, 512)] = tn(normed[...], grad_qkv[...]).astype(BF)
     scratch[:, pl.ds(512, QCOLS)] = tn(grad_att[...], attended[...]).astype(BF)
-    gains = [gain_a[...], gain_b[...]]
-    first_row = lax.broadcasted_iota(jnp.int32, (16, 896), 0) == 0
     for b in range(16):
-        moved = [(pltpu.roll(g, (WIDTH - 96 * b) % WIDTH, 1) if b else g)[:, :HEAD] for g in gains]
-        row = jnp.concatenate([bias[...], *moved, jnp.zeros((1, HEAD), F32)], axis=1)
-        rest_rows = jnp.where(first_row, jnp.broadcast_to(row, (16, 896)), 0.0).astype(BF)
-        y, z = b // 4, b % 4
-        if len(outs) == 1:
-            outs[0][z, y, pl.ds(0, 96), :] = scratch[pl.ds(b * 96, 96), :]
-            outs[0][z, y, pl.ds(96, 16), :] = rest_rows
-        else:
-            for k in range(4):
-
-                @pl.when(lax.rem(place[2] + k, 4) == z)
-                def _(k=k):
-                    outs[k][y, pl.ds(0, 96), :] = scratch[pl.ds(b * 96, 96), :]
-                    outs[k][y, pl.ds(96, 16), :] = rest_rows
-
-
-def weight_grad(place, apart, *args):
-    shapes = (arr((4, 112, 896)),) * 4 if apart else (arr((4, 4, 112, 896)),)
+        out[b % 4, b // 4] = scratch[pl.ds(b * 96, 96), :]
+
+
+def weight_grad(*args):
     return call(
         weight_grad_kernel,
-        shapes,
-        [SMEM] + [VMEM] * 7,
-        (place, *args),
+        arr((4, 4, 96, 896)),
+        [VMEM] * 4,
+        args,
         [pltpu.VMEM((WIDTH, 896), BF)],
         flops=2 * 128 * 1536 * 896,
         size=6_000_000,
     )
 
 
-def ring_scatter(parts, done, last):
-    total = parts[0].astype(F32)
-    for k in (1, 2, 3):
-        total = total + after(shifted(parts[k], "z", k), done).astype(F32)
-    total = total.astype(BF)
+def apart_kernel(place, normed, grad_qkv, grad_att, attended, *rest):
+    smalls, outs, scratch = rest[:-5], rest[-5:-1], rest[-1]
+    scratch[:, pl.ds(0, 512)] = tn(normed[...], grad_qkv[...]).astype(BF)
+    scratch[:, pl.ds(512, QCOLS)] = tn(grad_att[...], attended[...]).astype(BF)
+    row_index = lax.broadcasted_iota(jnp.int32, (16, 512), 0)
+    for b in range(16):
+        y, z = b // 4, b % 4
+        rows = jnp.zeros((16, 512), F32)
+        for layer in range(2):
+            bias, *gains = (ref[...] for ref in smalls[3 * layer : 3 * layer + 3])
+            moved = [(pltpu.roll(g, (WIDTH - 96 * b) % WIDTH, 1) if b else g)[:, :HEAD] for g in gains]
+            gain_row = jnp.concatenate([*moved, jnp.zeros((1, 2 * HEAD), F32)], axis=1)
+            for at, row in ((2 * layer, bias), (2 * layer + 1, gain_row)):
+                rows = jnp.where(row_index == at, jnp.broadcast_to(row, (16, 512)), rows)
+        rows = rows.astype(BF)
+        for k in range(4):
+
+            @pl.when(lax.rem(place[2] + k, 4) == z)
+            def _(k=k):
+                outs[k][y, pl.ds(0, 96), :] = scratch[pl.ds(b * 96, 96), :]
+                outs[k][y, pl.ds(96, 16), pl.ds(0, 512)] = rows
+                outs[k][y, pl.ds(96, 16), pl.ds(512, QCOLS)] = jnp.zeros((16, QCOLS), BF)
+
+
+def apart(place, factors, smalls):
+    parts = call(
+        apart_kernel,
+        (arr((4, 112, 896)),) * 4,
+        [SMEM] + [VMEM] * 10,
+        (place, *factors, *smalls),
+        [pltpu.VMEM((WIDTH, 896), BF)],
+        flops=2 * 128 * 1536 * 896,
+        size=6_000_000,
+    )
+    return [parts[0]] + [shifted(parts[k], "z", k) for k in (1, 2, 3)]
+
+
+def summed(parts):
+    return sum(part.astype(F32) for part in parts).astype(BF)
+
+
+def scatter_blocks(blocks, last):
     y = lax.axis_index("y")
-    blocks = [lax.dynamic_index_in_dim(total, lax.rem(y + j, 4), 0, keepdims=False) for j in range(4)]
-    result = blocks[0].astype(F32)
-    for j in (1, 2, 3):
-        result = result + after(shifted(blocks[j], "y", j), last).astype(F32)
-    return result.astype(BF), total
+    own, *others = (lax.dynamic_index_in_dim(blocks, lax.rem(y + j, 4), 0, keepdims=False) for j in range(4))
+    return summed([own] + [after(shifted(other, "y", j + 1), last) for j, other in enumerate(others)])
 
 
 def after_heads_kernel(pieces, xin, gain, mixed, second):
@@ -556,6 +575,15 @@
     return call(pack_kernel, arr((8, 96, FW)), [VMEM] * 3, (gate, up, down), size=4_500_000)
 
 
+def halves_kernel(pieces, first, second):
+    first[...] = pieces[:4].reshape(384, FW)
+    second[...] = pieces[4:].reshape(384, FW)
+
+
+def halves(pieces):
+    return call(halves_kernel, (arr((384, FW)), arr((384, FW))), [VMEM], (pieces,), size=6_000_000)
+
+
 def unpack_kernel(pieces, gate, up, down):
     for z in range(4):
         first = z * PAD_FF
@@ -618,18 +646,20 @@
 
     xin = pick(inputs[0], inputs[1])
     cot = pick(cotangent[0], cotangent[1])
-    x_block1 = pair_gather(pair_gather(xin, "c"), "x")
     place_y, place_z = lax.axis_index("y").astype(jnp.int32), lax.axis_index("z").astype(jnp.int32)
     y_then_z = jnp.stack([place_y, jnp.int32(4), place_z, jnp.int32(1)])
-    z_then_y = jnp.stack([place_z, jnp.int32(1), place_y, jnp.int32(4)])
     first, second = pick(own, other), pick(other, own)
-    rows_first = jnp.concatenate([attention_rows(0, first), first[:, QCOLS:]], axis=1)
+    rows_first, out_rows = attention_rows(0, first), first[:96, QCOLS:]
     rows_second = jnp.concatenate([attention_rows(1, second), second[:, QCOLS:]], axis=1)
-    ring = ring_gather(rows_first, "z", "y", x_block1)
-    ffn_packed = after(pack(w_gate[0], w_up[0], w_down[0]), ring[0])
-    ffn_both = exchange(ffn_packed, ("s", "z")).reshape(2, 384, FW)
-    ffn_both = after(ffn_both, ring)
-    qkv_first, out_first, tail_first = assemble(z_then_y, ring, (512, QCOLS))
+    ffn_packed = after(pack(w_gate[0], w_up[0], w_down[0]), (rows_first, rows_second))
+    ffn_pieces = exchange(ffn_packed, ("s", "z"))
+    blocks, out_blocks = ring_first(rows_first, "y"), ring_first(out_rows, "y")
+    blocks, out_blocks, ffn_pieces = lax.optimization_barrier((blocks, out_blocks, ffn_pieces))
+    ffn_halves = halves(ffn_pieces)
+    x_block1 = pair_gather(pair_gather(after(xin, ffn_pieces), "c"), "x")
+    ring = ring_second(blocks, "z")
+    qkv_first, tail_first = assemble(y_then_z, ring)
+    out_ring = ring_second(after(out_blocks, ring), "z")
 
     seg = pick(segments[0], segments[1])
     local_pos = block * HEAD + jnp.arange(HEAD, dtype=jnp.int32)
@@ -652,17 +682,17 @@
 
     gain_a1, gain_b1, bias1 = smalls(tail_first)
     normed1, query1, kv = qkv_columns(flag, x_block1, gain_a1, qkv_first, bias1, cosine, sine)
-    own1 = gathered(ffn_both[0], "y")
+    own1 = gathered(ffn_halves[0], "y")
+    all_second = gathered(after(rows_second, kv), ("y", "z")).reshape(16, 112, 896)
     kv_mine1 = exchange(kv, ("y", "z")).reshape(SEQ, HEAD)
+    kv_mine1, out_ring = lax.optimization_barrier((kv_mine1, out_ring))
+    out_first = assemble(y_then_z, out_ring)
     kv_other1 = swap(kv_mine1, "c")
     attended1, lse1, part = attend(flag, query1, kv_mine1, kv_other1, seg_col, seg_row, out_first)
-    all_second = gathered(after(rows_second, part), ("y", "z")).reshape(16, 112, 896)
-    mixed1, low = after_heads(exchange(part, ("x", "c")), xin, gain_b1)
+    other1 = swap(after(own1, kv_mine1), "c")
+    mixed1, low = after_heads(after(exchange(part, ("x", "c")), other1), xin, gain_b1)
     second1 = exchange(low, ("z", "x")).reshape(256, WIDTH)
-    cot_low = spread(after(cot, second1), 8, ("z", "x")).reshape(256, WIDTH)
-    second1 = after(second1, cot_low)
-    own2 = gathered(after(ffn_both[1], second1), "y")
-    other1 = swap(own1, "c")
+    own2 = gathered(after(ffn_halves[1], second1), "y")
     part, gate_up1 = feed(second1, own1, other1)
     pieces = exchange(part.reshape(8, 32, WIDTH), ("z", "x"))
     out_one = after_feed(pieces, mixed1)
@@ -676,12 +706,20 @@
     mixed2, low = after_heads(exchange(part, ("x", "c")), out_one, gain_b2)
     other2 = swap(after(own2, low), "c")
     second2 = exchange(low, ("z", "x")).reshape(256, WIDTH)
+    cot_low = spread(after(cot, second2), 8, ("z", "x")).reshape(256, WIDTH)
     part, gate_up2 = feed(second2, own2, other2)
-    last_part = part
-
-    def backward(grad_out, grad_low, gate_up, second, own, other, mixed, gain_b, xin, x_block, gain_a, query,
-                 kv_mine, kv_other, lse, weight, out_t, earlier=None):
+    part, cot_low = lax.optimization_barrier((part, cot_low))
+    out_pieces = exchange(part.reshape(8, 32, WIDTH), ("z", "x"))
+
+    def both(first, second):
+        given = swap(pick(second, first), "s")
+        return jnp.stack([pick(first, given), pick(given, second)])[None]
+
+    def backward(grad_out, grad_low, gate_up, second, own, other, mixed, gain_b, xin, x_block, gain_a, normed, query,
+                 attended, kv_mine, kv_other, lse, weight, out_t, before=None, earlier=None):
         part, for_own, for_other = feed_back(grad_low, own, other, gate_up)
+        if before is not None:
+            part, before = lax.optimization_barrier((part, before))
         pieces = exchange(part.reshape(8, 32, WIDTH), ("z", "x"))
         given = swap(for_other, "c")
         second_other, grad_other = swap(second, "c"), swap(grad_low, "c")
@@ -690,7 +728,7 @@
         grad_mixed, low, grad_gain_b = before_heads(pieces, mixed, gain_b, grad_out)
         grad_att = gathered(low, ("x", "c"))
         if earlier is not None:
-            grad_ffn = after(grad_ffn, (earlier, grad_att))
+            grad_ffn = after(grad_ffn, earlier)
         grad_ffn = lax.psum_scatter(grad_ffn, "y", scatter_dimension=0, tiled=True)
         grad_query, kept_half, sent_half = attend_back(
             flag, query, kv_mine, kv_other, seg_col, seg_row, lse, grad_att, out_t, cosine, sine
@@ -698,34 +736,44 @@
         grad_kv = (kept_half + swap(sent_half, "c").astype(F32)).astype(BF)
         grad_kv = exchange(grad_kv.reshape(16, HEAD, HEAD), ("y", "z"))
         grad_qkv, grad_bias, grad_gain_a, part = qkv_back(flag, grad_kv, grad_query, weight, x_block, cosine, sine)
+        smalls = (grad_bias, grad_gain_a, grad_gain_b)
+        factors = (normed, grad_qkv, grad_att, attended)
+        if earlier is None:
+            parts = smalls, weight_grad(*factors)
+        else:
+            parts = apart(y_then_z, factors, smalls + small_two)
+            part = after(part, parts[0])
         pieces = exchange(part, ("x", "c"))
         grad_in, low = layer_start(pieces, xin, gain_a, grad_mixed)
-        return grad_in, low, grad_qkv, grad_att, grad_ffn, (grad_bias, grad_gain_a, grad_gain_b)
-
-    grad_two, low, grad_qkv2, grad_att2, ffn_two, small_two = backward(
-        cot, cot_low, gate_up2, second2, own2, other2, mixed2, gain_b2, out_one, x_block2, gain_a2, query2, kv_mine2,
-        kv_other2, lse2, all_second, all_second
-    )
+        return grad_in, low, grad_ffn, parts
+
+    grad_two, low, ffn_two, attn_two = backward(
+        cot, cot_low, gate_up2, second2, own2, other2, mixed2, gain_b2, out_one, x_block2, gain_a2, normed2, query2,
+        attended2, kv_mine2, kv_other2, lse2, all_second, all_second, before=out_pieces
+    )
+    out_two = after_feed(out_pieces, mixed2)
+    both_out = both(out_one, out_two)
     grad_low = exchange(low, ("z", "x")).reshape(256, WIDTH)
-    (attn_two,) = weight_grad(y_then_z, False, normed2, grad_qkv2, grad_att2, attended2, *small_two)
-    attn_two, grad_low = lax.optimization_barrier((attn_two, grad_low))
-    attn_two = after(attn_two, ffn_two)
-    attn_two = lax.psum_scatter(attn_two.reshape(16 * 112, 896), "z", scatter_dimension=0, tiled=True)
-    grad_one, _, grad_qkv1, grad_att1, ffn_one, small_one = backward(
-        grad_two, grad_low, gate_up1, second1, own1, other1, mixed1, gain_b1, xin, x_block1, gain_a1, query1, kv_mine1,
-        kv_other1, lse1, qkv_first, out_first, attn_two
-    )
-    out_two = after_feed(exchange(after(last_part, grad_one).reshape(8, 32, WIDTH), ("z", "x")), mixed2)
-    parts = weight_grad(y_then_z, True, normed1, grad_qkv1, grad_att1, attended1, *small_one)
+    small_two, attn_two = attn_two
+    grad_low = after(grad_low, (attn_two, both_out))
+    attn_two = after(attn_two, (ffn_two, low))
+    attn_two = lax.psum_scatter(attn_two.reshape(16 * 96, 896), "z", scatter_dimension=0, tiled=True)
+    grad_one, _, ffn_one, parts = backward(
+        grad_two, grad_low, gate_up1, second1, own1, other1, mixed1, gain_b1, xin, x_block1, gain_a1, normed1, query1,
+        attended1, kv_mine1, kv_other1, lse1, qkv_first, out_first, earlier=attn_two
+    )
     ffn_payload = jnp.concatenate([ffn_one, ffn_two], axis=0).reshape(8, 96, FW)
-    ffn_sum = exchange(ffn_payload, ("s", "z"))
-    attn_one, halfway = ring_scatter(parts, (ffn_payload, out_two), ffn_sum)
+    halfway = summed(parts)
+    ffn_sum = exchange(after(ffn_payload, parts), ("s", "z"))
+    attn_one = scatter_blocks(halfway, ffn_sum)
     attn_two = lax.psum_scatter(after(attn_two, (ffn_one, grad_one, halfway)), "y", scatter_dimension=0, tiled=True)
 
     grad_gate, grad_up, grad_down = unpack(ffn_sum)
-    attn_sum = pick(attn_one, attn_two).astype(F32) + swap(pick(attn_two, attn_one), "s").astype(F32)
-    main, row = attn_sum[:96], attn_sum[96]
-    gains = jnp.concatenate([row[512:608].reshape(4, 24), row[640:736].reshape(4, 24)], axis=1)
+    given = swap(jnp.concatenate([pick(attn_two, attn_one[:96]), attn_one[96:]], axis=0), "s").astype(F32)
+    main = pick(attn_one[:96], attn_two).astype(F32) + given[:96]
+    row = pick(attn_one[96], attn_one[98]).astype(F32) + pick(given[96], given[98])
+    gains = pick(attn_one[97], attn_one[99]).astype(F32) + pick(given[97], given[99])
+    gains = jnp.concatenate([gains[:96].reshape(4, 24), gains[128:224].reshape(4, 24)], axis=1)
     payload = jnp.concatenate(
         [
             main[:, QCOLS:512].reshape(4, 24, HEAD),
@@ -746,13 +794,9 @@
     kv_bias_row = lax.dynamic_index_in_dim(payload[:, 25], lax.axis_index("y"), 0, keepdims=False)
     grad_b_keyval = lax.dynamic_slice_in_dim(kv_bias_row, (lax.axis_index("z") * 4 + member) * 8, 8, 0)
 
-    def both(first, second):
-        given = swap(pick(second, first), "s")
-        return jnp.stack([pick(first, given), pick(given, second)])[None]
-
     return (
-        both(out_one, out_two),
-        both(grad_one, grad_two),
+        both_out,
+        both(after(grad_one, ffn_sum), grad_two),
         gains[None, :24],
         main[None, :, :QCOLS],
         row[None, :QCOLS],

time: 639 us -> 613 us (0.959)
  blocking collectives: 133 us -> 99.2 us
  starting transfers between devices: 105 us -> 124 us
  local copies, waits for them, and re-layouts: 33 us -> 25 us
  waiting for transfers between devices: 216 us -> 209 us
    all_to_all x12 -> x15, waiting for transfers between devices: 58.9 us -> 111 us  [exchange(): return lax.all_to_all(value, axes, split_axis=0, concat_axis=0, tiled=True)]
    all_to_all x7 -> x4, blocking collectives: 112 us -> 75.1 us  [exchange(): return lax.all_to_all(value, axes, split_axis=0, concat_axis=0, tiled=True)]
    all_gather x3, waiting for transfers between devices: 37.1 us -> 7.92 us  [gathered(): return lax.all_gather(piece, axes, axis=0, tiled=True)]
    ppermute x12 -> x18, waiting for transfers between devices: 79.8 us -> 56.6 us  [shifted(): return lax.ppermute(value, axis, [(i, (i + steps) % 4) for i in range(4)])]
    all_to_all x12 -> x15, starting transfers between devices: 55.2 us -> 74.2 us  [exchange(): return lax.all_to_all(value, axes, split_axis=0, concat_axis=0, tiled=True)]
    reduce_scatter x2, waiting for transfers between devices: 7.47 us -> 17 us  [backward(): grad_ffn = lax.psum_scatter(grad_ffn, 'y', scatter_dimension=0, tiled=True)]
    reduce_scatter x1, waiting for transfers between devices: 9.23 us -> 0.01 us  [local(): lax.psum_scatter(after(attn_two, (ffn_one, grad_one, halfway)), 'y', scat...]
    reduce_scatter x1, waiting for transfers between devices: 7.06 us -> 0.01 us  [local(): lax.psum_scatter(attn_two.reshape(16 * 96, 896), 'z', scatter_dimension=0...]
  transfers between devices with their start and end apart: 52 -> 61, of which waited for: 28 -> 35; matrix products, arithmetic and copies ran while one was open for 4% -> 4% of each run, Pallas kernels for 15% -> 18%
where the time goes in v3:
time: 613 us; the launch traced here: 602 us
  waiting for transfers between devices  209 us (34%)
  starting transfers between devices  124 us (20%)
  Pallas kernels  112 us (18%)
  blocking collectives  99.2 us (16%)
  local copies, waits for them, and re-layouts  25 us (4%)
  between operations  16.9 us (3%)
  other arithmetic  16.3 us (3%)
    pallas_call x29, Pallas kernels, call(): pl.pallas_call(kernel, out_shape=out_shape, in_specs=in_specs, scratch_sh...  112 us
    all_to_all x15, waiting for transfers between devices, exchange(): return lax.all_to_all(value, axes, split_axis=0, concat_axis=0, tiled=True)  111 us
    all_to_all x4, blocking collectives, exchange(): return lax.all_to_all(value, axes, split_axis=0, concat_axis=0, tiled=True)  75.1 us
    all_to_all x15, starting transfers between devices, exchange(): return lax.all_to_all(value, axes, split_axis=0, concat_axis=0, tiled=True)  74.2 us
    ppermute x18, waiting for transfers between devices, shifted(): return lax.ppermute(value, axis, [(i, (i + steps) % 4) for i in range(4)])  56.6 us
    ppermute x18, starting transfers between devices, shifted(): return lax.ppermute(value, axis, [(i, (i + steps) % 4) for i in range(4)])  26.5 us
    all_gather x3, blocking collectives, gathered(): return lax.all_gather(piece, axes, axis=0, tiled=True)  24.1 us
    ppermute x18, starting transfers between devices, swap(): return lax.ppermute(value, axis, [(0, 1), (1, 0)])  19.5 us
  transfers between devices with their start and end apart: 61, of which 35 were waited for; matrix products, arithmetic and copies ran while one was open for 4% of the time, Pallas kernels for 18%

profile of v3, /device:TPU:1, one launch (start us, length us, event | category | flops | bytes accessed | tf_op | source)
XLA Modules:
  0.0 602.2 jit_solution(13538368732100375452)
XLA Ops:
  45.5 22.7 %all-to-all-done.1.pieces = bf16[8,96,1920]{2,1,0:T(8,128)(2,1)} async-done(((bf16[8,96,1920]{2,1,0:T(8,128)(2,1)}), bf16[8,96,1920]{2,1,0:T(8,128)(2,1)}, u32[]{:S(2)}, u32[]{:S(2)}) %all-to-all-start.1) | async-done | bytes 2949152 | tf_op jit(solution)/shard_map/all_to_all | solution.py:37
  88.1 10.3 %collective-permute-done.11.refs_3_ = bf16[4,112,512]{2,1,0:T(8,128)(2,1)S(1)} collective-permute-done((bf16[4,112,512]{2,1,0:T(8,128)(2,1)S(1)}, bf16[4,112,512]{2,1,0:T(8,128)(2,1)S(1)}, u32[]{:S(2)}, u32[]{:S(2)}) %collective-permute-start.11) | collective-permute-done | bytes 458784 | tf_op jit(solution)/shard_map/ppermute | solution.py:385
  104.7 7.3 %all-to-all-start.2 = ((bf16[16,128,128]{2,1,0:T(8,128)(2,1)}), bf16[16,128,128]{2,1,0:T(8,128)(2,1)S(1)}, u32[]{:S(2)}, u32[]{:S(2)}) async-start(bf16[16,128,128]{2,1,0:T(8,128)(2,1)} %get-tuple-element.113), calls=%async_computation.2 | async-start | bytes 1048576 | tf_op jit(solution)/shard_map/all_to_all | solution.py:37
  117.1 10.1 %collective-permute-done.12.refs_1_ = bf16[4,96,384]{2,1,0:T(8,128)(2,1)S(1)} collective-permute-done((bf16[4,96,384]{2,1,0:T(8,128)(2,1)S(1)}, bf16[4,96,384]{2,1,0:T(8,128)(2,1)S(1)}, u32[]{:S(2)}, u32[]{:S(2)}) %collective-permute-start.12) | collective-permute-done | bytes 294944 | tf_op jit(solution)/shard_map/ppermute | solution.py:385
  167.7 20.7 %all_to_all.95 = bf16[8,32,1536]{2,1,0:T(8,128)(2,1)S(1)} all-to-all(bf16[8,32,1536]{2,1,0:T(8,128)(2,1)S(1)} %get-tuple-element.125), channel_id=1, replica_groups=mesh['s'=2,'y'=4,'z'=4,'x'=2,'c'=2] {'z','x'}, dimensions={0} | all-to-all | bytes 1572864 | tf_op jit(solution)/shard_map/all_to_all | solution.py:37
  188.4 7.9 %shard_map.227 = (bf16[256,1536]{1,0:T(8,128)(2,1)}, bf16[2,256,1280]{2,1,0:T(8,128)(2,1)}) custom-call(bf16[256,1536]{1,0:T(8,128)(2,1)S(1)} %bitcast.114, bf16[1536,1920]{1,0:T(8,128)(2,1)} %all-gather.4.cloned.1.call-done.own, bf16[1536,1920]{1,0:T(8,128)(2,1)} %collective-permute-done.16.other), custom_call_target="tpu_custom_call" | custom-call | flops 3019898880 | bytes 15000000 | tf_op jit(solution)/shard_map/pallas_call | solution.py:61
  201.7 9.0 %all-to-all-done.5.pieces = bf16[8,32,1536]{2,1,0:T(8,128)(2,1)S(1)} async-done(((bf16[8,32,1536]{2,1,0:T(8,128)(2,1)}), bf16[8,32,1536]{2,1,0:T(8,128)(2,1)S(1)}, u32[]{:S(2)}, u32[]{:S(2)}) %all-to-all-start.5) | async-done | bytes 786464 | tf_op jit(solution)/shard_map/all_to_all | solution.py:37
  210.9 9.0 %all_gather.19.xin = bf16[128,1536]{1,0:T(8,128)(2,1)S(1)} all-gather(bf16[32,1536]{1,0:T(8,128)(2,1)S(1)} %shard_map.228.xin), channel_id=1, replica_groups=mesh['s'=2,'y'=4,'z'=4,'x'=2,'c'=2] {'x','c'}, dimensions={0}, use_global_device_ids=true | all-gather | bytes 491520 | tf_op jit(solution)/shard_map/all_gather | solution.py:621
  222.4 18.1 %all_to_all.96 = bf16[16,128,128]{2,1,0:T(8,128)(2,1)S(1)} all-to-all(bf16[16,128,128]{2,1,0:T(8,128)(2,1)S(1)} %get-tuple-element.130), channel_id=1, replica_groups=mesh['s'=2,'y'=4,'z'=4,'x'=2,'c'=2] {'y','z'}, dimensions={0} | all-to-all | bytes 1048576 | tf_op jit(solution)/shard_map/all_to_all | solution.py:37
  272.3 11.8 %all-to-all-done.8 = bf16[8,32,1536]{2,1,0:T(8,128)(2,1)S(1)} async-done(((bf16[8,32,1536]{2,1,0:T(8,128)(2,1)}), bf16[8,32,1536]{2,1,0:T(8,128)(2,1)S(1)}, u32[]{:S(2)}, u32[]{:S(2)}) %all-to-all-start.8) | async-done | bytes 786464 | tf_op jit(solution)/shard_map/all_to_all | solution.py:37
  305.2 7.8 %shard_map.234 = (bf16[256,1536]{1,0:T(8,128)(2,1)S(1)}, bf16[256,1920]{1,0:T(8,128)(2,1)}, bf16[256,1920]{1,0:T(8,128)(2,1)}) custom-call(bf16[256,1536]{1,0:T(8,128)(2,1)} %bitcast.39.grads, bf16[1536,1920]{1,0:T(8,128)(2,1)} %all-gather.8.cloned.1.call-done.own, bf16[1536,1920]{1,0:T(8,128)(2,1)} %collective-permute-done.18.other, ...), custom_call_target="tpu_custom_call" | custom-call | flops 3019898880 | bytes 17000000 | tf_op jit(solution)/shard_map/pallas_call | solution.py:61
  322.2 8.5 %shard_map.235 = bf16[1536,1920]{1,0:T(8,128)(2,1)} custom-call(bf16[256,1536]{1,0:T(8,128)(2,1)S(1)} %bitcast.119, bf16[256,1536]{1,0:T(8,128)(2,1)} %collective-permute-done.20.tokens_other, bf16[256,1536]{1,0:T(8,128)(2,1)} %bitcast.39.grads, bf16[256,1536]{1,0:T(8,128)(2,1)} %collective-permute-done.21.grads_other, ...), custom_call_target="tpu_custom_call" | custom-call | flops 3019898880 | bytes 12000000 | tf_op jit(solution)/shard_map/pallas_call | solution.py:61
  335.1 8.3 %all_gather.22.grad_att = bf16[128,1536]{1,0:T(8,128)(2,1)S(1)} all-gather(bf16[32,1536]{1,0:T(8,128)(2,1)S(1)} %get-tuple-element.149), channel_id=1, replica_groups=mesh['s'=2,'y'=4,'z'=4,'x'=2,'c'=2] {'x','c'}, dimensions={0}, use_global_device_ids=true | all-gather | bytes 491520 | tf_op jit(solution)/shard_map/all_gather | solution.py:621
  343.5 8.7 %shard_map.237 = (bf16[128,384]{1,0:T(8,128)(2,1)S(1)}, f32[2048,128]{1,0:T(8,128)}, bf16[2048,128]{1,0:T(8,128)(2,1)S(1)}) custom-call(s32[2]{0:T(128)S(1)} %pad_add_fusion.flag, bf16[3,128,128]{2,1,0:T(8,128)(2,1)S(1)} %get-tuple-element.129.query, bf16[2048,128]{1,0:T(8,128)(2,1)S(1)} %bitcast.113, bf16[2048,128]{1,0:T(8,128)(2,1)} %copy-done.1, ...), custom_call_target="tpu_custom_call" | custom-call | flops 1560281088 | bytes 5000000 | tf_op jit(solution)/shard_map/pallas_call | solution.py:61
  355.4 18.8 %all_to_all.97.pieces = bf16[16,128,128]{2,1,0:T(8,128)(2,1)S(1)} all-to-all(bf16[16,128,128]{2,1,0:T(8,128)(2,1)S(1)} %bitcast.141), channel_id=1, replica_groups=mesh['s'=2,'y'=4,'z'=4,'x'=2,'c'=2] {'y','z'}, dimensions={0} | all-to-all | bytes 1048576 | tf_op jit(solution)/shard_map/all_to_all | solution.py:37
  391.6 8.4 %reduce-scatter.5.cloned.1.call-done = bf16[384,1920]{1,0:T(8,128)(2,1)} async-done(((bf16[1536,1920]{1,0:T(8,128)(2,1)}), bf16[384,1920]{1,0:T(8,128)(2,1)}) %reduce-scatter.5.cloned.1.call-update) | async-done | bytes 1474576 | tf_op jit(solution)/shard_map/reduce_scatter | solution.py:732
  409.2 15.3 %all-to-all-done.14 = bf16[8,32,1536]{2,1,0:T(8,128)(2,1)S(1)} async-done(((bf16[8,32,1536]{2,1,0:T(8,128)(2,1)}), bf16[8,32,1536]{2,1,0:T(8,128)(2,1)S(1)}, u32[]{:S(2)}, u32[]{:S(2)}) %all-to-all-start.14) | async-done | bytes 786464 | tf_op jit(solution)/shard_map/all_to_all | solution.py:37
  424.5 7.9 %shard_map.241 = (bf16[256,1536]{1,0:T(8,128)(2,1)S(1)}, bf16[256,1920]{1,0:T(8,128)(2,1)}, bf16[256,1920]{1,0:T(8,128)(2,1)}) custom-call(bf16[256,1536]{1,0:T(8,128)(2,1)S(1)} %bitcast.120, bf16[1536,1920]{1,0:T(8,128)(2,1)} %all-gather.4.cloned.1.call-done.own, bf16[1536,1920]{1,0:T(8,128)(2,1)} %collective-permute-done.16.other, ...), custom_call_target="tpu_custom_call" | custom-call | flops 3019898880 | bytes 17000000 | tf_op jit(solution)/shard_map/pallas_call | solution.py:61
  440.3 8.6 %shard_map.242 = bf16[1536,1920]{1,0:T(8,128)(2,1)} custom-call(bf16[256,1536]{1,0:T(8,128)(2,1)S(1)} %bitcast.116, bf16[256,1536]{1,0:T(8,128)(2,1)} %collective-permute-done.24.tokens_other, bf16[256,1536]{1,0:T(8,128)(2,1)} %bitcast.122, bf16[256,1536]{1,0:T(8,128)(2,1)} %collective-permute-done.25.grads_other, bf16[256,1920]{1,0:T(8,128)(2,1)} %get-tuple-element.162.own, ...), custom_call_target="tpu_custom_call" | custom-call | flops 3019898880 | bytes 12000000 | tf_op jit(solution)/shard_map/pallas_call | solution.py:61
  459.9 7.9 %shard_map.244 = (bf16[128,384]{1,0:T(8,128)(2,1)S(1)}, f32[2048,128]{1,0:T(8,128)}, bf16[2048,128]{1,0:T(8,128)(2,1)S(1)}) custom-call(s32[2]{0:T(128)S(1)} %copy-done.29, bf16[3,128,128]{2,1,0:T(8,128)(2,1)S(1)} %copy-done.22, bf16[2048,128]{1,0:T(8,128)(2,1)S(1)} %bitcast.126, bf16[2048,128]{1,0:T(8,128)(2,1)} %copy-done.15, s32[2048,1]{1,0:T(8,128)} %copy.53.seg_col, ...), custom_call_target="tpu_custom_call" | custom-call | flops 1560281088 | bytes 5000000 | tf_op jit(solution)/shard_map/pallas_call | solution.py:61
  471.2 17.5 %all_to_all.98.pieces = bf16[16,128,128]{2,1,0:T(8,128)(2,1)S(1)} all-to-all(bf16[16,128,128]{2,1,0:T(8,128)(2,1)S(1)} %bitcast.142), channel_id=1, replica_groups=mesh['s'=2,'y'=4,'z'=4,'x'=2,'c'=2] {'y','z'}, dimensions={0} | all-to-all | bytes 1048576 | tf_op jit(solution)/shard_map/all_to_all | solution.py:37
  506.6 8.6 %reduce-scatter.9.cloned.1.call-done = bf16[384,1920]{1,0:T(8,128)(2,1)} async-done(((bf16[1536,1920]{1,0:T(8,128)(2,1)}), bf16[384,1920]{1,0:T(8,128)(2,1)}) %reduce-scatter.9.cloned.1.call-update) | async-done | bytes 1474576 | tf_op jit(solution)/shard_map/reduce_scatter | solution.py:732
  518.9 15.1 %collective-permute-done.29 = bf16[4,112,896]{2,1,0:T(8,128)(2,1)} collective-permute-done((bf16[4,112,896]{2,1,0:T(8,128)(2,1)}, bf16[4,112,896]{2,1,0:T(8,128)(2,1)}, u32[]{:S(2)}, u32[]{:S(2)}) %collective-permute-start.29) | collective-permute-done | bytes 802848 | tf_op jit(solution)/shard_map/ppermute | solution.py:385
  549.7 25.9 %all-to-all-done.18.pieces = bf16[8,96,1920]{2,1,0:T(8,128)(2,1)} async-done(((bf16[8,96,1920]{2,1,0:T(8,128)(2,1)}), bf16[8,96,1920]{2,1,0:T(8,128)(2,1)}, u32[]{:S(2)}, u32[]{:S(2)}) %all-to-all-start.18) | async-done | bytes 2949152 | tf_op jit(solution)/shard_map/all_to_all | solution.py:37
  (345 shorter events, 291.2 us)
Async XLA Ops:
  26.5 41.7 %all-to-all-start.1 = ((bf16[8,96,1920]{2,1,0:T(8,128)(2,1)}), bf16[8,96,1920]{2,1,0:T(8,128)(2,1)}, u32[]{:S(2)}, u32[]{:S(2)}) async-start(bf16[8,96,1920]{2,1,0:T(8,128)(2,1)} %shard_map.220), calls=%async_computation.1 | async-start | bytes 5898240 | tf_op jit(solution)/shard_map/all_to_all | solution.py:37
  32.8 107.1 %all-gather.4.cloned.1.call-start = ((), (), s32[]{:S(2)}) async-start(), calls=%async_computation.23 | async-start | bytes 7372800 | tf_op jit(solution)/shard_map/all_gather | solution.py:621
  77.8 20.6 %collective-permute-start.11 = (bf16[4,112,512]{2,1,0:T(8,128)(2,1)S(1)}, bf16[4,112,512]{2,1,0:T(8,128)(2,1)S(1)}, u32[]{:S(2)}, u32[]{:S(2)}) collective-permute-start(bf16[4,112,512]{2,1,0:T(8,128)(2,1)S(1)} %pad_maximum_fusion.1.refs_0_), channel_id=1, source_target_pairs={{0,12},{4,0},{8,4},{12,8},{1,13},{5,1},{9,5},{13,9},{2,14},{6,2},{... | collective-permute-start | bytes 1376264 | tf_op jit(solution)/shard_map/ppermute | solution.py:385
  78.8 20.3 %collective-permute-start.9 = (bf16[4,112,512]{2,1,0:T(8,128)(2,1)S(1)}, bf16[4,112,512]{2,1,0:T(8,128)(2,1)S(1)}, u32[]{:S(2)}, u32[]{:S(2)}) collective-permute-start(bf16[4,112,512]{2,1,0:T(8,128)(2,1)S(1)} %pad_maximum_fusion.1.refs_0_), channel_id=1, source_target_pairs={{0,4},{4,8},{8,12},{12,0},{1,5},{5,9},{9,13},{13,1},{2,6},{6,10},{... | collective-permute-start | bytes 1376264 | tf_op jit(solution)/shard_map/ppermute | solution.py:385
  104.7 28.9 %all-to-all-start.2 = ((bf16[16,128,128]{2,1,0:T(8,128)(2,1)}), bf16[16,128,128]{2,1,0:T(8,128)(2,1)S(1)}, u32[]{:S(2)}, u32[]{:S(2)}) async-start(bf16[16,128,128]{2,1,0:T(8,128)(2,1)} %get-tuple-element.113), calls=%async_computation.2 | async-start | bytes 1048576 | tf_op jit(solution)/shard_map/all_to_all | solution.py:37
  112.0 87.8 %all-gather.6.cloned.1.call-start = ((), (), s32[]{:S(2)}) async-start(), calls=%async_computation.24 | async-start | bytes 3411968 | tf_op jit(solution)/shard_map/all_gather | solution.py:621
  113.5 20.1 %collective-permute-start.13 = (bf16[4,96,384]{2,1,0:T(8,128)(2,1)S(1)}, bf16[4,96,384]{2,1,0:T(8,128)(2,1)S(1)}, u32[]{:S(2)}, u32[]{:S(2)}) collective-permute-start(bf16[4,96,384]{2,1,0:T(8,128)(2,1)S(1)} %pad_maximum_fusion.3.refs_0_), channel_id=1, source_target_pairs={{0,8},{4,12},{8,0},{12,4},{1,9},{5,13},{9,1},{13,5},{2,10},{6,14},... | collective-permute-start | bytes 884744 | tf_op jit(solution)/shard_map/ppermute | solution.py:385
  115.9 17.7 %collective-permute-start.14 = (bf16[4,96,384]{2,1,0:T(8,128)(2,1)S(1)}, bf16[4,96,384]{2,1,0:T(8,128)(2,1)S(1)}, u32[]{:S(2)}, u32[]{:S(2)}) collective-permute-start(bf16[4,96,384]{2,1,0:T(8,128)(2,1)S(1)} %pad_maximum_fusion.3.refs_0_), channel_id=1, source_target_pairs={{0,12},{4,0},{8,4},{12,8},{1,13},{5,1},{9,5},{13,9},{2,14},{6,2},{... | collective-permute-start | bytes 884744 | tf_op jit(solution)/shard_map/ppermute | solution.py:385
  139.9 27.6 %collective-permute-start.16 = (bf16[1536,1920]{1,0:T(8,128)(2,1)}, bf16[1536,1920]{1,0:T(8,128)(2,1)}, u32[]{:S(2)}, u32[]{:S(2)}) collective-permute-start(bf16[1536,1920]{1,0:T(8,128)(2,1)} %all-gather.4.cloned.1.call-done.own), channel_id=1, source_target_pairs={{0,1},{1,0},{2,3},{3,2},{4,5},{5,4},{6,7},{7,6},{8,9},{9,8},{10,11... | collective-permute-start | bytes 17694728 | tf_op jit(solution)/shard_map/ppermute | solution.py:33
  160.9 104.5 %all-gather.8.cloned.1.call-start = ((), (), s32[]{:S(2)}) async-start(), calls=%async_computation.25 | async-start | bytes 7372800 | tf_op jit(solution)/shard_map/all_gather | solution.py:621
  265.4 23.8 %collective-permute-start.18 = (bf16[1536,1920]{1,0:T(8,128)(2,1)}, bf16[1536,1920]{1,0:T(8,128)(2,1)}, u32[]{:S(2)}, u32[]{:S(2)}) collective-permute-start(bf16[1536,1920]{1,0:T(8,128)(2,1)} %all-gather.8.cloned.1.call-done.own), channel_id=1, source_target_pairs={{0,1},{1,0},{2,3},{3,2},{4,5},{5,4},{6,7},{7,6},{8,9},{9,8},{10,11... | collective-permute-start | bytes 17694728 | tf_op jit(solution)/shard_map/ppermute | solution.py:33
  266.3 17.8 %all-to-all-start.8 = ((bf16[8,32,1536]{2,1,0:T(8,128)(2,1)}), bf16[8,32,1536]{2,1,0:T(8,128)(2,1)S(1)}, u32[]{:S(2)}, u32[]{:S(2)}) async-start(bf16[8,32,1536]{2,1,0:T(8,128)(2,1)} %copy-done.12), calls=%async_computation.8 | async-start | bytes 1572864 | tf_op jit(solution)/shard_map/all_to_all | solution.py:37
  322.1 77.9 %reduce-scatter.5.cloned.1.call-start = ((), (), s32[]{:S(2)}) async-start(), calls=%async_computation.26 | async-start | bytes 7372800 | tf_op jit(solution)/shard_map/reduce_scatter | solution.py:732
  383.8 69.0 %reduce-scatter.7.cloned.1.call-start = ((), (), s32[]{:S(2)}) async-start(), calls=%async_computation.27 | async-start | bytes 3440640 | tf_op jit(solution)/shard_map/reduce_scatter | solution.py:760
  404.1 20.5 %all-to-all-start.14 = ((bf16[8,32,1536]{2,1,0:T(8,128)(2,1)}), bf16[8,32,1536]{2,1,0:T(8,128)(2,1)S(1)}, u32[]{:S(2)}, u32[]{:S(2)}) async-start(bf16[8,32,1536]{2,1,0:T(8,128)(2,1)} %copy-done.9), calls=%async_computation.14 | async-start | bytes 1572864 | tf_op jit(solution)/shard_map/all_to_all | solution.py:37
  439.8 75.4 %reduce-scatter.9.cloned.1.call-start = ((), (), s32[]{:S(2)}) async-start(), calls=%async_computation.28 | async-start | bytes 7372800 | tf_op jit(solution)/shard_map/reduce_scatter | solution.py:732
  495.9 23.0 %collective-permute-start.28 = (bf16[4,112,896]{2,1,0:T(8,128)(2,1)}, bf16[4,112,896]{2,1,0:T(8,128)(2,1)S(1)}, u32[]{:S(2)}, u32[]{:S(2)}) collective-permute-start(bf16[4,112,896]{2,1,0:T(8,128)(2,1)} %get-tuple-element.188), channel_id=1, source_target_pairs={{0,4},{4,8},{8,12},{12,0},{1,5},{5,9},{9,13},{13,1},{2,6},{6,10},{... | collective-permute-start | bytes 2408456 | tf_op jit(solution)/shard_map/ppermute | solution.py:385
  496.1 37.9 %collective-permute-start.29 = (bf16[4,112,896]{2,1,0:T(8,128)(2,1)}, bf16[4,112,896]{2,1,0:T(8,128)(2,1)}, u32[]{:S(2)}, u32[]{:S(2)}) collective-permute-start(bf16[4,112,896]{2,1,0:T(8,128)(2,1)} %get-tuple-element.189), channel_id=1, source_target_pairs={{0,8},{4,12},{8,0},{12,4},{1,9},{5,13},{9,1},{13,5},{2,10},{6,14},... | collective-permute-start | bytes 2408456 | tf_op jit(solution)/shard_map/ppermute | solution.py:385
  499.8 34.2 %collective-permute-start.30 = (bf16[4,112,896]{2,1,0:T(8,128)(2,1)}, bf16[4,112,896]{2,1,0:T(8,128)(2,1)}, u32[]{:S(2)}, u32[]{:S(2)}) collective-permute-start(bf16[4,112,896]{2,1,0:T(8,128)(2,1)} %get-tuple-element.190), channel_id=1, source_target_pairs={{0,12},{4,0},{8,4},{12,8},{1,13},{5,1},{9,5},{13,9},{2,14},{6,2},{... | collective-permute-start | bytes 2408456 | tf_op jit(solution)/shard_map/ppermute | solution.py:385
  501.1 33.0 %all-to-all-start.17 = ((bf16[4,32,1536]{2,1,0:T(8,128)(2,1)}), bf16[4,32,1536]{2,1,0:T(8,128)(2,1)S(1)}, u32[]{:S(2)}, u32[]{:S(2)}) async-start(bf16[4,32,1536]{2,1,0:T(8,128)(2,1)} %get-tuple-element.181), calls=%async_computation.17 | async-start | bytes 786432 | tf_op jit(solution)/shard_map/all_to_all | solution.py:37
  534.1 41.5 %all-to-all-start.18 = ((bf16[8,96,1920]{2,1,0:T(8,128)(2,1)}), bf16[8,96,1920]{2,1,0:T(8,128)(2,1)}, u32[]{:S(2)}, u32[]{:S(2)}) async-start(bf16[8,96,1920]{2,1,0:T(8,128)(2,1)} %bitcast.139), calls=%async_computation.21 | async-start | bytes 5898240 | tf_op jit(solution)/shard_map/all_to_all | solution.py:37
  540.2 38.3 %reduce-scatter.11.cloned.1.call-start = ((), (), s32[]{:S(2)}) async-start(), calls=%async_computation.29 | async-start | bytes 860160 | tf_op jit(solution)/shard_map/reduce_scatter | solution.py:769
  544.3 31.2 %collective-permute-start.33 = (bf16[112,896]{1,0:T(8,128)(2,1)S(1)}, bf16[112,896]{1,0:T(8,128)(2,1)S(1)}, u32[]{:S(2)}, u32[]{:S(2)}) collective-permute-start(bf16[112,896]{1,0:T(8,128)(2,1)S(1)} %get-tuple-element.252), channel_id=1, source_target_pairs={{0,32},{16,48},{32,0},{48,16},{1,33},{17,49},{33,1},{49,17},{2,34}... | collective-permute-start | bytes 602120 | tf_op jit(solution)/shard_map/ppermute | solution.py:385
  547.0 28.5 %collective-permute-start.34 = (bf16[112,896]{1,0:T(8,128)(2,1)S(1)}, bf16[112,896]{1,0:T(8,128)(2,1)S(1)}, u32[]{:S(2)}, u32[]{:S(2)}) collective-permute-start(bf16[112,896]{1,0:T(8,128)(2,1)S(1)} %get-tuple-element.251), channel_id=1, source_target_pairs={{0,48},{16,0},{32,16},{48,32},{1,49},{17,1},{33,17},{49,33},{2,50}... | collective-permute-start | bytes 602120 | tf_op jit(solution)/shard_map/ppermute | solution.py:385
  (90 other events, 1750.7 us)
Sparse Core Ops, SparseCore 0:
  71.9 67.9 all-gather.3
  333.8 66.0 reduce-scatter.4
  543.4 22.6 reduce-scatter.10
Sparse Core Ops, SparseCore 1:
  140.7 56.1 all-gather.5
  198.4 67.0 all-gather.7
  400.1 43.2 reduce-scatter.6
  452.9 62.2 reduce-scatter.8

commit v4 on v3

--- a/solution.py
+++ b/solution.py
@@ -1,3 +1,5 @@
+import functools
+
 import jax
 import jax.numpy as jnp
 import numpy as np
@@ -15,10 +17,12 @@
 QCOLS = 384
 SEQ = 2048
 CHUNK = 512
-LOCAL_FF = 560
-PAD_FF = 640
-GU = 2 * PAD_FF
-FW = 3 * PAD_FF
+MAIN = 512
+PART = 64
+TAIL = 4 * MAIN
+GU = 2 * MAIN + 2 * PART
+DOWN = MAIN + 2 * PART
+FW = GU + DOWN
 SCALE = HEAD**-0.5
 AXES = ("s", "y", "z", "x", "c")
 BLOCK_ORDER = (0, 2, 1, 3)
@@ -77,21 +81,24 @@
     return values * cosine + pltpu.roll(values, HEAD // 2, 1) * sine
 
 
-def whole_weight(ref, scratch, first, size):
-    if len(ref.shape) == 2:
-        return ref[...]
-    for b in range(16):
-        scratch[pl.ds(b * 96, 96), :] = ref[b, pl.ds(0, 96), pl.ds(first, size)]
-    return scratch[...]
-
-
-def qkv_kernel(flag, xin, gain, weight, bias, cosine, sine, normed, query, kv, scratch):
-    whole = whole_weight(weight, scratch, 0, 512)
+def fetch(weight, first, into, sem):
+    copy = pltpu.make_async_copy(weight.at[:, pl.ds(first, into.shape[1])], into, sem)
+    copy.start()
+    return copy
+
+
+def fetched(columns):
+    return [pltpu.VMEM((WIDTH, columns), BF), pltpu.SemaphoreType.DMA]
+
+
+def qkv_kernel(flag, xin, gain, weight, bias, cosine, sine, normed, query, kv, whole, sem):
+    copy = fetch(weight, 0, whole, sem)
     cos, sin = cosine[...], sine[...]
     rows = xin[...].astype(F32)
     low = (rows * inverse_rms(rows) * gain[...]).astype(BF)
     normed[...] = low
-    out = nn(low, whole) + bias[...]
+    copy.wait()
+    out = nn(low, whole[...]) + bias[...]
     for h in range(3):
         query[h] = turned(out[:, h * HEAD : (h + 1) * HEAD], cos, sin).astype(BF)
     last = out[:, QCOLS:]
@@ -104,9 +111,9 @@
     return call(
         qkv_kernel,
         (arr((HEAD, WIDTH)), arr((3, HEAD, HEAD)), arr((16, HEAD, HEAD))),
-        [SMEM] + [VMEM] * 6,
+        [SMEM, VMEM, VMEM, ANY, VMEM, VMEM, VMEM],
         (flag, xin, gain, weight, bias, cosine, sine),
-        [pltpu.VMEM((WIDTH, 512), BF)],
+        fetched(512),
         flops=2 * 128 * 1536 * 512,
         size=3_000_000,
     )
@@ -120,7 +127,10 @@
     return [jnp.where(allowed, scores[:, h * HEAD : (h + 1) * HEAD], NEG) for h in range(3)]
 
 
-def attend_kernel(flag, query, kv_mine, kv_other, seg_col, seg_row, out_t, attended, lse, part, top, total, acc, scratch):
+def attend_kernel(
+    first, flag, query, kv_mine, kv_other, seg_col, seg_row, weight, attended, lse, part, top, total, acc, out_t, sem
+):
+    copy = fetch(weight, first, out_t, sem)
     query_all = query[...].reshape(3 * HEAD, HEAD)
     is_key = flag[0] == 1
     first_query = flag[1] * HEAD
@@ -149,22 +159,23 @@
     done = acc[...] / total[...]
     for h in range(3):
         attended[:, pl.ds(h * HEAD, HEAD)] = done[:, h * HEAD : (h + 1) * HEAD].T.astype(BF)
-    out = nt(attended[...], whole_weight(out_t, scratch, 512, QCOLS)).astype(BF)
+    copy.wait()
+    out = nt(attended[...], out_t[...]).astype(BF)
     for t in range(4):
         part[t] = out[t * 32 : (t + 1) * 32]
 
 
-def attend(flag, query, kv_mine, kv_other, seg_col, seg_row, out_t):
-    return call(
-        attend_kernel,
+def attend(flag, query, kv_mine, kv_other, seg_col, seg_row, weight, first):
+    return call(
+        functools.partial(attend_kernel, first),
         (arr((HEAD, QCOLS)), arr((1, QCOLS), F32), arr((4, 32, WIDTH))),
-        [SMEM] + [VMEM] * 6,
-        (flag, query, kv_mine, kv_other, seg_col, seg_row, out_t),
+        [SMEM] + [VMEM] * 5 + [ANY],
+        (flag, query, kv_mine, kv_other, seg_col, seg_row, weight),
         [
             pltpu.VMEM((1, QCOLS), F32),
             pltpu.VMEM((1, QCOLS), F32),
             pltpu.VMEM((HEAD, QCOLS), F32),
-            pltpu.VMEM((WIDTH, QCOLS), BF),
+            *fetched(QCOLS),
         ],
         flops=4 * 384 * 2048 * 128 + 2 * 128 * 384 * 1536,
         size=3_000_000,
@@ -173,15 +184,21 @@
 
 
 def attend_back_kernel(
-    flag, query, kv_mine, kv_other, seg_col, seg_row, lse, grad_att, out_t, cosine, sine,
-    grad_query, kept, sent, low, acc, scratch
+    first, flag, query, kv_mine, kv_other, seg_col, seg_row, lse, attended, grad_att, cosine, sine, weight,
+    grad_query, kept, sent, low, acc, out_t, sem
 ):
+    copy = fetch(weight, first, out_t, sem)
     query_all = query[...].reshape(3 * HEAD, HEAD)
     is_key = flag[0] == 1
     first_query = flag[1] * HEAD
-    grad_attended = nn(grad_att[...], whole_weight(out_t, scratch, 512, QCOLS)).astype(BF)
+    sums = []
+    copy.wait()
+    grad_attended = nn(grad_att[...], out_t[...]).astype(BF)
     for h in range(3):
-        low[pl.ds(h * HEAD, HEAD), :] = grad_attended[:, h * HEAD : (h + 1) * HEAD]
+        grad_head = grad_attended[:, h * HEAD : (h + 1) * HEAD]
+        low[pl.ds(h * HEAD, HEAD), :] = grad_head
+        with_output = grad_head.astype(F32) * attended[:, pl.ds(h * HEAD, HEAD)].astype(F32)
+        sums.append(jnp.sum(with_output.T, axis=0, keepdims=True))
     grad_rows = low[...]
     lse_row = lse[...]
 
@@ -196,16 +213,6 @@
         return at, keys, probs, grad_probs
 
     acc[...] = jnp.zeros(acc.shape, F32)
-
-    def row_sums(step, sums):
-        _, _, probs, grad_probs = chunk(step)
-        return tuple(
-            sums[h] + jnp.sum(probs[h] * grad_probs[:, h * HEAD : (h + 1) * HEAD], axis=0, keepdims=True)
-            for h in range(3)
-        )
-
-    zero = jnp.zeros((1, HEAD), F32)
-    sums = lax.fori_loop(0, SEQ // CHUNK, row_sums, (zero, zero, zero))
 
     @pl.loop(0, SEQ // CHUNK)
     def _(step):
@@ -230,30 +237,31 @@
         grad_query[:, pl.ds(h * HEAD, HEAD)] = turned(rows, cos, -sin).astype(BF)
 
 
-def attend_back(flag, query, kv_mine, kv_other, seg_col, seg_row, lse, grad_att, out_t, cosine, sine):
-    return call(
-        attend_back_kernel,
+def attend_back(flag, query, kv_mine, kv_other, seg_col, seg_row, lse, attended, grad_att, cosine, sine, weight, first):
+    return call(
+        functools.partial(attend_back_kernel, first),
         (arr((HEAD, QCOLS)), arr((SEQ, HEAD), F32), arr((SEQ, HEAD))),
-        [SMEM] + [VMEM] * 10,
-        (flag, query, kv_mine, kv_other, seg_col, seg_row, lse, grad_att, out_t, cosine, sine),
-        [pltpu.VMEM((3 * HEAD, HEAD), BF), pltpu.VMEM((HEAD, QCOLS), F32), pltpu.VMEM((WIDTH, QCOLS), BF)],
-        flops=14 * 384 * 2048 * 128 + 2 * 128 * 384 * 1536,
+        [SMEM] + [VMEM] * 10 + [ANY],
+        (flag, query, kv_mine, kv_other, seg_col, seg_row, lse, attended, grad_att, cosine, sine, weight),
+        [pltpu.VMEM((3 * HEAD, HEAD), BF), pltpu.VMEM((HEAD, QCOLS), F32), *fetched(QCOLS)],
+        flops=10 * 384 * 2048 * 128 + 2 * 128 * 384 * 1536,
         size=5_000_000,
         exps=2 * 384 * 2048,
     )
 
 
 def qkv_back_kernel(
-    flag, pieces, grad_query, weight, xin, cosine, sine, grad_qkv, grad_bias, grad_gain, part, scratch
+    flag, pieces, grad_query, weight, xin, cosine, sine, grad_qkv, grad_bias, grad_gain, part, whole, sem
 ):
-    whole = whole_weight(weight, scratch, 0, 512)
+    copy = fetch(weight, 0, whole, sem)
     total = jnp.sum(pieces[...].astype(F32), axis=0)
     total = jnp.where(flag[0] == 1, turned(total, cosine[...], -sine[...]), total).astype(BF)
     grad_qkv[:, pl.ds(0, QCOLS)] = grad_query[...]
     grad_qkv[:, pl.ds(QCOLS, HEAD)] = total
     grads = grad_qkv[...]
     grad_bias[...] = jnp.sum(grads.astype(F32), axis=0, keepdims=True)
-    out = nt(grads, whole)
+    copy.wait()
+    out = nt(grads, whole[...])
     rows = xin[...].astype(F32)
     grad_gain[...] = jnp.sum(out * rows * inverse_rms(rows), axis=0, keepdims=True)
     low = out.astype(BF)
@@ -265,9 +273,9 @@
     return call(
         qkv_back_kernel,
         (arr((HEAD, 512)), arr((1, 512), F32), arr((1, WIDTH), F32), arr((4, 32, WIDTH))),
-        [SMEM] + [VMEM] * 6,
+        [SMEM, VMEM, VMEM, ANY, VMEM, VMEM, VMEM],
         (flag, pieces, grad_query, weight, xin, cosine, sine),
-        [pltpu.VMEM((WIDTH, 512), BF)],
+        fetched(512),
         flops=2 * 128 * 1536 * 512,
         size=3_000_000,
     )
@@ -277,7 +285,7 @@
     copies = {}
     for i, ref in enumerate((own, other)):
         for name in order:
-            start, size, buffer = (0, GU, gate_up) if name == "gate_up" else (GU, PAD_FF, down)
+            start, size, buffer = (0, GU, gate_up) if name == "gate_up" else (GU, DOWN, down)
             copies[i, name] = pltpu.make_async_copy(
                 ref.at[:, pl.ds(start, size)], buffer.at[i], sems.at[2 * i + (name == "down")]
             )
@@ -287,6 +295,17 @@
     return copies
 
 
+def gate_and_up(both):
+    tail = both[:, 2 * MAIN :]
+    gate = jnp.concatenate([both[:, :MAIN], tail], axis=1)
+    return gate, jnp.concatenate([both[:, MAIN : 2 * MAIN], pltpu.roll(tail, PART, 1)], axis=1)
+
+
+def known(hidden):
+    lane = lax.broadcasted_iota(jnp.int32, hidden.shape, 1)
+    return jnp.where(lane < MAIN + PART, hidden, 0.0)
+
+
 def feed_kernel(tokens, own, other, part, gate_up_out, gate_up, down, acc, sems):
     copies = weight_copies(own, other, gate_up, down, sems, ("gate_up", "down"))
     rows = tokens[...]
@@ -294,8 +313,8 @@
         copies[i, "gate_up"].wait()
         both = nn(rows, gate_up[i])
         gate_up_out[i] = both.astype(BF)
-        gate, up = both[:, :PAD_FF], both[:, PAD_FF:]
-        hidden = (gate * jax.nn.sigmoid(gate) * up).astype(BF)
+        gate, up = gate_and_up(both)
+        hidden = known(gate * jax.nn.sigmoid(gate) * up).astype(BF)
         copies[i, "down"].wait()
         out = nt(hidden, down[i])
         if i == 0:
@@ -306,7 +325,7 @@
 
 FEED_SCRATCH = [
     pltpu.VMEM((2, WIDTH, GU), BF),
-    pltpu.VMEM((2, WIDTH, PAD_FF), BF),
+    pltpu.VMEM((2, WIDTH, DOWN), BF),
     pltpu.VMEM((256, WIDTH), F32),
     pltpu.SemaphoreType.DMA((4,)),
 ]
@@ -331,13 +350,16 @@
     for i, result in enumerate((for_own, for_other)):
         copies[i, "down"].wait()
         grad_hidden = nn(rows, down[i])
-        gate = gate_up_in[i, :, pl.ds(0, PAD_FF)].astype(F32)
-        up = gate_up_in[i, :, pl.ds(PAD_FF, PAD_FF)].astype(F32)
+        gate, up = gate_and_up(gate_up_in[i].astype(F32))
         sig = jax.nn.sigmoid(gate)
         silu = gate * sig
-        result[:, pl.ds(0, PAD_FF)] = (grad_hidden * up * sig * (1.0 + gate * (1.0 - sig))).astype(BF)
-        result[:, pl.ds(PAD_FF, PAD_FF)] = (grad_hidden * silu).astype(BF)
-        result[:, pl.ds(GU, PAD_FF)] = (silu * up).astype(BF)
+        grad_gate = grad_hidden * up * sig * (1.0 + gate * (1.0 - sig))
+        grad_up = grad_hidden * silu
+        tail = grad_gate[:, MAIN:] + pltpu.roll(grad_up[:, MAIN:], PART, 1)
+        result[:, pl.ds(0, MAIN)] = grad_gate[:, :MAIN].astype(BF)
+        result[:, pl.ds(MAIN, MAIN)] = grad_up[:, :MAIN].astype(BF)
+        result[:, pl.ds(2 * MAIN, 2 * PART)] = tail.astype(BF)
+        result[:, pl.ds(GU, DOWN)] = known(silu * up).astype(BF)
         copies[i, "gate_up"].wait()
         out = nt(result[:, pl.ds(0, GU)], gate_up[i])
         if i == 0:
@@ -360,7 +382,7 @@
 
 
 def feed_grad_kernel(tokens, tokens_other, grads, grads_other, own, given, out):
-    gate_up, hidden = pl.ds(0, GU), pl.ds(GU, PAD_FF)
+    gate_up, hidden = pl.ds(0, GU), pl.ds(GU, DOWN)
     out[:, gate_up] = (tn(tokens[...], own[:, gate_up]) + tn(tokens_other[...], given[:, gate_up])).astype(BF)
     out[:, hidden] = (tn(grads[...], own[:, hidden]) + tn(grads_other[...], given[:, hidden])).astype(BF)
 
@@ -439,9 +461,9 @@
 
 
 def apart_kernel(place, normed, grad_qkv, grad_att, attended, *rest):
-    smalls, outs, scratch = rest[:-5], rest[-5:-1], rest[-1]
-    scratch[:, pl.ds(0, 512)] = tn(normed[...], grad_qkv[...]).astype(BF)
-    scratch[:, pl.ds(512, QCOLS)] = tn(grad_att[...], attended[...]).astype(BF)
+    smalls, outs, scratch, scratch_out = rest[:-10], rest[-10:-2], rest[-2], rest[-1]
+    scratch[...] = tn(normed[...], grad_qkv[...]).astype(BF)
+    scratch_out[...] = tn(grad_att[...], attended[...]).astype(BF)
     row_index = lax.broadcasted_iota(jnp.int32, (16, 512), 0)
     for b in range(16):
         y, z = b // 4, b % 4
@@ -458,31 +480,38 @@
             @pl.when(lax.rem(place[2] + k, 4) == z)
             def _(k=k):
                 outs[k][y, pl.ds(0, 96), :] = scratch[pl.ds(b * 96, 96), :]
-                outs[k][y, pl.ds(96, 16), pl.ds(0, 512)] = rows
-                outs[k][y, pl.ds(96, 16), pl.ds(512, QCOLS)] = jnp.zeros((16, QCOLS), BF)
+                outs[k][y, pl.ds(96, 16), :] = rows
+
+            @pl.when(lax.rem(place[0] + k, 4) == y)
+            def _(k=k):
+                outs[4 + k][z] = scratch_out[pl.ds(b * 96, 96), :]
 
 
 def apart(place, factors, smalls):
     parts = call(
         apart_kernel,
-        (arr((4, 112, 896)),) * 4,
+        (arr((4, 112, 512)),) * 4 + (arr((4, 96, QCOLS)),) * 4,
         [SMEM] + [VMEM] * 10,
         (place, *factors, *smalls),
-        [pltpu.VMEM((WIDTH, 896), BF)],
+        [pltpu.VMEM((WIDTH, 512), BF), pltpu.VMEM((WIDTH, QCOLS), BF)],
         flops=2 * 128 * 1536 * 896,
         size=6_000_000,
     )
-    return [parts[0]] + [shifted(parts[k], "z", k) for k in (1, 2, 3)]
+    return parts[:4], parts[4:]
+
+
+def sent(parts, axis):
+    return [parts[0]] + [shifted(parts[k], axis, k) for k in (1, 2, 3)]
 
 
 def summed(parts):
     return sum(part.astype(F32) for part in parts).astype(BF)
 
 
-def scatter_blocks(blocks, last):
-    y = lax.axis_index("y")
-    own, *others = (lax.dynamic_index_in_dim(blocks, lax.rem(y + j, 4), 0, keepdims=False) for j in range(4))
-    return summed([own] + [after(shifted(other, "y", j + 1), last) for j, other in enumerate(others)])
+def scatter_blocks(blocks, axis, last):
+    here = lax.axis_index(axis)
+    own, *others = (lax.dynamic_index_in_dim(blocks, lax.rem(here + j, 4), 0, keepdims=False) for j in range(4))
+    return summed([own] + [after(shifted(other, axis, j + 1), last) for j, other in enumerate(others)])
 
 
 def after_heads_kernel(pieces, xin, gain, mixed, second):
@@ -556,23 +585,25 @@
     )
 
 
-def pack_kernel(gate, up, down, out):
-    out[...] = jnp.zeros(out.shape, BF)
+def pack_kernel(gate, up, down, tails, out):
     for z in range(4):
-        first = z * PAD_FF
-        size = min(PAD_FF, 4 * LOCAL_FF - first)
+        main = pl.ds(z * MAIN, MAIN)
         pieces = (
-            gate[:, pl.ds(first, size)],
-            up[:, pl.ds(first, size)],
-            down[pl.ds(first, size), :].astype(F32).T.astype(BF),
+            (0, gate[:, main]),
+            (MAIN, up[:, main]),
+            (2 * MAIN, tails[z, :, pl.ds(0, 2 * PART)]),
+            (GU, down[main, :].astype(F32).T.astype(BF)),
+            (GU + MAIN, tails[z, :, pl.ds(2 * PART, 2 * PART)]),
         )
         for s in range(2):
-            for i, piece in enumerate(pieces):
-                out[4 * s + z, :, pl.ds(i * PAD_FF, size)] = piece
+            for at, piece in pieces:
+                out[4 * s + z, :, pl.ds(at, piece.shape[1])] = piece
 
 
 def pack(gate, up, down):
-    return call(pack_kernel, arr((8, 96, FW)), [VMEM] * 3, (gate, up, down), size=4_500_000)
+    rest = [jnp.pad(w, ((0, 0), (0, PART))).reshape(96, 4, PART) for w in (gate[:, TAIL:], up[:, TAIL:], down[TAIL:].T)]
+    tails = jnp.concatenate([*rest, jnp.zeros((96, 4, PART), BF)], axis=2).transpose(1, 0, 2)
+    return call(pack_kernel, arr((8, 96, FW)), [VMEM] * 4, (gate, up, down, tails), size=4_500_000)
 
 
 def halves_kernel(pieces, first, second):
@@ -585,17 +616,26 @@
 
 
 def unpack_kernel(pieces, gate, up, down):
+    low = lax.broadcasted_iota(jnp.int32, (96, 2 * PART), 1) < PART
+    tails = []
     for z in range(4):
-        first = z * PAD_FF
-        size = min(PAD_FF, 4 * LOCAL_FF - first)
+        main = pl.ds(z * MAIN, MAIN)
         total = pieces[z].astype(F32) + pieces[4 + z].astype(F32)
-        gate[:, pl.ds(first, size)] = total[:, :size]
-        up[:, pl.ds(first, size)] = total[:, PAD_FF : PAD_FF + size]
-        down[pl.ds(first, size), :] = total[:, GU : GU + size].T
+        gate[:, main] = total[:, :MAIN]
+        up[:, main] = total[:, MAIN : 2 * MAIN]
+        down[main, :] = total[:, GU : GU + MAIN].T
+        if z < 3:
+            tails.append(total[:, 2 * MAIN : GU])
+            down[pl.ds(TAIL + z * PART, PART), :] = total[:, GU + MAIN :].T[:PART]
+    turned_tails = [pltpu.roll(tail, PART, 1) for tail in tails]
+    gate[:, pl.ds(TAIL, 2 * PART)] = jnp.where(low, tails[0], turned_tails[1])
+    gate[:, pl.ds(TAIL + 2 * PART, PART)] = tails[2][:, :PART]
+    up[:, pl.ds(TAIL, 2 * PART)] = jnp.where(low, turned_tails[0], tails[1])
+    up[:, pl.ds(TAIL + 2 * PART, PART)] = turned_tails[2][:, :PART]
 
 
 def unpack(pieces):
-    wide = 4 * LOCAL_FF
+    wide = TAIL + 3 * PART
     return call(
         unpack_kernel,
         (arr((96, wide), F32), arr((96, wide), F32), arr((wide, 96), F32)),
@@ -640,9 +680,10 @@
     other = swap(own, "s")
 
     def attention_rows(layer, matrices):
-        kv = payload[layer]
-        kv = jnp.concatenate([kv[:, :24].reshape(96, HEAD), kv[:, 24], jnp.zeros((12, HEAD), BF)], axis=0)
-        return jnp.concatenate([matrices[:, :QCOLS], kv], axis=1)
+        return jnp.concatenate([matrices[:96, :QCOLS], payload[layer, :, :24].reshape(96, HEAD)], axis=1)
+
+    def small_rows(layer, matrices):
+        return jnp.concatenate([matrices[96:100, :QCOLS], payload[layer, :, 24]], axis=1)
 
     xin = pick(inputs[0], inputs[1])
     cot = pick(cotangent[0], cotangent[1])
@@ -650,7 +691,9 @@
     y_then_z = jnp.stack([place_y, jnp.int32(4), place_z, jnp.int32(1)])
     first, second = pick(own, other), pick(other, own)
     rows_first, out_rows = attention_rows(0, first), first[:96, QCOLS:]
-    rows_second = jnp.concatenate([attention_rows(1, second), second[:, QCOLS:]], axis=1)
+    tails = [small_rows(0, first), small_rows(1, second), jnp.zeros((8, 512), BF)]
+    rows_first = jnp.concatenate([rows_first, *tails], axis=0)
+    rows_second = jnp.concatenate([attention_rows(1, second), second[:96, QCOLS:]], axis=1)
     ffn_packed = after(pack(w_gate[0], w_up[0], w_down[0]), (rows_first, rows_second))
     ffn_pieces = exchange(ffn_packed, ("s", "z"))
     blocks, out_blocks = ring_first(rows_first, "y"), ring_first(out_rows, "y")
@@ -659,7 +702,7 @@
     x_block1 = pair_gather(pair_gather(after(xin, ffn_pieces), "c"), "x")
     ring = ring_second(blocks, "z")
     qkv_first, tail_first = assemble(y_then_z, ring)
-    out_ring = ring_second(after(out_blocks, ring), "z")
+    out_ring = ring_second(after(out_blocks, (ring[1], ring[3])), "z")
 
     seg = pick(segments[0], segments[1])
     local_pos = block * HEAD + jnp.arange(HEAD, dtype=jnp.int32)
@@ -673,23 +716,23 @@
     seg_col = seg[:, None]
 
     def smalls(tail):
-        bits = tail[:, :4, QCOLS : QCOLS + 56].reshape(64, 56)
+        bits = tail[:, :, QCOLS : QCOLS + 56].reshape(64, 56)
         gain_a = bits[:, :24].reshape(1, WIDTH).astype(F32)
         gain_b = bits[:, 24:48].reshape(1, WIDTH).astype(F32)
         kv_bias = lax.dynamic_slice_in_dim(bits[:, 48:].reshape(1, 512), (core * 2 + chip) * HEAD, HEAD, 1)
         bias = jnp.concatenate([tail[:1, 0, :QCOLS], kv_bias], axis=1).astype(F32)
         return gain_a, gain_b, bias
 
-    gain_a1, gain_b1, bias1 = smalls(tail_first)
+    gain_a1, gain_b1, bias1 = smalls(tail_first[:, :4])
     normed1, query1, kv = qkv_columns(flag, x_block1, gain_a1, qkv_first, bias1, cosine, sine)
     own1 = gathered(ffn_halves[0], "y")
-    all_second = gathered(after(rows_second, kv), ("y", "z")).reshape(16, 112, 896)
+    all_second = gathered(after(rows_second, kv), ("y", "z"))
+    kv, out_ring = lax.optimization_barrier((kv, out_ring))
+    out_first = assemble(y_then_z, out_ring)
     kv_mine1 = exchange(kv, ("y", "z")).reshape(SEQ, HEAD)
-    kv_mine1, out_ring = lax.optimization_barrier((kv_mine1, out_ring))
-    out_first = assemble(y_then_z, out_ring)
     kv_other1 = swap(kv_mine1, "c")
-    attended1, lse1, part = attend(flag, query1, kv_mine1, kv_other1, seg_col, seg_row, out_first)
-    other1 = swap(after(own1, kv_mine1), "c")
+    attended1, lse1, part = attend(flag, query1, kv_mine1, kv_other1, seg_col, seg_row, out_first, 0)
+    other1 = swap(after(own1, part), "c")
     mixed1, low = after_heads(after(exchange(part, ("x", "c")), other1), xin, gain_b1)
     second1 = exchange(low, ("z", "x")).reshape(256, WIDTH)
     own2 = gathered(after(ffn_halves[1], second1), "y")
@@ -698,25 +741,21 @@
     out_one = after_feed(pieces, mixed1)
 
     x_block2 = gathered(out_one, ("x", "c"))
-    gain_a2, gain_b2, bias2 = smalls(all_second[:, 96:, :512])
+    gain_a2, gain_b2, bias2 = smalls(tail_first[:, 4:8])
     normed2, query2, kv = qkv_columns(flag, x_block2, gain_a2, all_second, bias2, cosine, sine)
     kv_mine2 = exchange(kv, ("y", "z")).reshape(SEQ, HEAD)
     kv_other2 = swap(kv_mine2, "c")
-    attended2, lse2, part = attend(flag, query2, kv_mine2, kv_other2, seg_col, seg_row, all_second)
+    attended2, lse2, part = attend(flag, query2, kv_mine2, kv_other2, seg_col, seg_row, all_second, 512)
     mixed2, low = after_heads(exchange(part, ("x", "c")), out_one, gain_b2)
-    other2 = swap(after(own2, low), "c")
     second2 = exchange(low, ("z", "x")).reshape(256, WIDTH)
-    cot_low = spread(after(cot, second2), 8, ("z", "x")).reshape(256, WIDTH)
+    other2 = swap(after(own2, second2), "c")
+    cot_low = spread(after(cot, (second2, own2)), 8, ("z", "x")).reshape(256, WIDTH)
+    second2 = after(second2, cot_low)
     part, gate_up2 = feed(second2, own2, other2)
-    part, cot_low = lax.optimization_barrier((part, cot_low))
     out_pieces = exchange(part.reshape(8, 32, WIDTH), ("z", "x"))
 
-    def both(first, second):
-        given = swap(pick(second, first), "s")
-        return jnp.stack([pick(first, given), pick(given, second)])[None]
-
     def backward(grad_out, grad_low, gate_up, second, own, other, mixed, gain_b, xin, x_block, gain_a, normed, query,
-                 attended, kv_mine, kv_other, lse, weight, out_t, before=None, earlier=None):
+                 attended, kv_mine, kv_other, lse, weight, out_t, first, before=None, earlier=None):
         part, for_own, for_other = feed_back(grad_low, own, other, gate_up)
         if before is not None:
             part, before = lax.optimization_barrier((part, before))
@@ -731,7 +770,7 @@
             grad_ffn = after(grad_ffn, earlier)
         grad_ffn = lax.psum_scatter(grad_ffn, "y", scatter_dimension=0, tiled=True)
         grad_query, kept_half, sent_half = attend_back(
-            flag, query, kv_mine, kv_other, seg_col, seg_row, lse, grad_att, out_t, cosine, sine
+            flag, query, kv_mine, kv_other, seg_col, seg_row, lse, attended, grad_att, cosine, sine, out_t, first
         )
         grad_kv = (kept_half + swap(sent_half, "c").astype(F32)).astype(BF)
         grad_kv = exchange(grad_kv.reshape(16, HEAD, HEAD), ("y", "z"))
@@ -742,30 +781,33 @@
             parts = smalls, weight_grad(*factors)
         else:
             parts = apart(y_then_z, factors, smalls + small_two)
-            part = after(part, parts[0])
+            part = after(part, parts)
         pieces = exchange(part, ("x", "c"))
         grad_in, low = layer_start(pieces, xin, gain_a, grad_mixed)
         return grad_in, low, grad_ffn, parts
 
     grad_two, low, ffn_two, attn_two = backward(
         cot, cot_low, gate_up2, second2, own2, other2, mixed2, gain_b2, out_one, x_block2, gain_a2, normed2, query2,
-        attended2, kv_mine2, kv_other2, lse2, all_second, all_second, before=out_pieces
+        attended2, kv_mine2, kv_other2, lse2, all_second, all_second, 512, before=out_pieces
     )
     out_two = after_feed(out_pieces, mixed2)
-    both_out = both(out_one, out_two)
     grad_low = exchange(low, ("z", "x")).reshape(256, WIDTH)
     small_two, attn_two = attn_two
-    grad_low = after(grad_low, (attn_two, both_out))
-    attn_two = after(attn_two, (ffn_two, low))
+    grad_low = after(grad_low, attn_two)
+    attn_two = after(attn_two, (ffn_two, grad_low))
     attn_two = lax.psum_scatter(attn_two.reshape(16 * 96, 896), "z", scatter_dimension=0, tiled=True)
     grad_one, _, ffn_one, parts = backward(
         grad_two, grad_low, gate_up1, second1, own1, other1, mixed1, gain_b1, xin, x_block1, gain_a1, normed1, query1,
-        attended1, kv_mine1, kv_other1, lse1, qkv_first, out_first, earlier=attn_two
+        attended1, kv_mine1, kv_other1, lse1, qkv_first, out_first, 0, earlier=attn_two
     )
     ffn_payload = jnp.concatenate([ffn_one, ffn_two], axis=0).reshape(8, 96, FW)
-    halfway = summed(parts)
-    ffn_sum = exchange(after(ffn_payload, parts), ("s", "z"))
-    attn_one = scatter_blocks(halfway, ffn_sum)
+    qkv_parts = sent(parts[0], "z")
+    ffn_sum = exchange(after(ffn_payload, qkv_parts), ("s", "z"))
+    halfway = summed(qkv_parts)
+    out_parts = sent(after(parts[1], ffn_payload), "y")
+    qkv_one = scatter_blocks(halfway, "y", ffn_sum)
+    out_one_grad = scatter_blocks(summed(out_parts), "z", ffn_sum)
+    attn_one = jnp.concatenate([qkv_one, jnp.pad(out_one_grad, ((0, 16), (0, 0)))], axis=1)
     attn_two = lax.psum_scatter(after(attn_two, (ffn_one, grad_one, halfway)), "y", scatter_dimension=0, tiled=True)
 
     grad_gate, grad_up, grad_down = unpack(ffn_sum)
@@ -794,9 +836,14 @@
     kv_bias_row = lax.dynamic_index_in_dim(payload[:, 25], lax.axis_index("y"), 0, keepdims=False)
     grad_b_keyval = lax.dynamic_slice_in_dim(kv_bias_row, (lax.axis_index("z") * 4 + member) * 8, 8, 0)
 
+    firsts, seconds = jnp.stack([out_one, grad_one]), jnp.stack([out_two, grad_two])
+    given = swap(after(pick(seconds, firsts), ffn_sum), "s")
+    rows = jnp.stack([pick(firsts, given), pick(given, seconds)], axis=1)[:, None]
+    section_out, input_grad = rows[0], rows[1]
+
     return (
-        both_out,
-        both(after(grad_one, ffn_sum), grad_two),
+        section_out,
+        input_grad,
         gains[None, :24],
         main[None, :, :QCOLS],
         row[None, :QCOLS],

time: 613 us -> 591 us (0.964)
  waiting for transfers between devices: 209 us -> 162 us
  blocking collectives: 99.2 us -> 139 us
  starting transfers between devices: 124 us -> 115 us
    all_to_all x4 -> x7, blocking collectives: 75.1 us -> 115 us  [exchange(): return lax.all_to_all(value, axes, split_axis=0, concat_axis=0, tiled=True)]
    all_to_all x15 -> x12, waiting for transfers between devices: 111 us -> 80.1 us  [exchange(): return lax.all_to_all(value, axes, split_axis=0, concat_axis=0, tiled=True)]
    all_to_all x15 -> x12, starting transfers between devices: 74.2 us -> 59.4 us  [exchange(): return lax.all_to_all(value, axes, split_axis=0, concat_axis=0, tiled=True)]
    reduce_scatter x1, waiting for transfers between devices: 0.01 us -> 11.1 us  [local(): lax.psum_scatter(attn_two.reshape(16 * 96, 896), 'z', scatter_dimension=0...]
    reduce_scatter x2, waiting for transfers between devices: 17 us -> 6.01 us  [backward(): grad_ffn = lax.psum_scatter(grad_ffn, 'y', scatter_dimension=0, tiled=True)]
    ppermute x18 -> x17, waiting for transfers between devices: 15.9 us -> 6.74 us  [swap(): return lax.ppermute(value, axis, [(0, 1), (1, 0)])]
    ppermute x18 -> x24, starting transfers between devices: 26.5 us -> 31.2 us  [shifted(): return lax.ppermute(value, axis, [(i, (i + steps) % 4) for i in range(4)])]
    unnamed x108 -> x86, local copies, waits for them, and re-layouts: 16 us -> 13 us
  transfers between devices with their start and end apart: 61 -> 63, of which waited for: 35 -> 31; matrix products, arithmetic and copies ran while one was open for 4% -> 4% of each run, Pallas kernels for 18% -> 17%
where the time goes in v4:
time: 591 us; the launch traced here: 581 us
  waiting for transfers between devices  162 us (27%)
  blocking collectives  139 us (24%)
  starting transfers between devices  115 us (19%)
  Pallas kernels  110 us (19%)
  local copies, waits for them, and re-layouts  21 us (4%)
  between operations  17.1 us (3%)
  other arithmetic  16.7 us (3%)
    all_to_all x7, blocking collectives, exchange(): return lax.all_to_all(value, axes, split_axis=0, concat_axis=0, tiled=True)  115 us
    pallas_call x29, Pallas kernels, call(): pl.pallas_call(kernel, out_shape=out_shape, in_specs=in_specs, scratch_sh...  110 us
    all_to_all x12, waiting for transfers between devices, exchange(): return lax.all_to_all(value, axes, split_axis=0, concat_axis=0, tiled=True)  80.1 us
    all_to_all x12, starting transfers between devices, exchange(): return lax.all_to_all(value, axes, split_axis=0, concat_axis=0, tiled=True)  59.4 us
    ppermute x24, waiting for transfers between devices, shifted(): return lax.ppermute(value, axis, [(i, (i + steps) % 4) for i in range(4)])  53.6 us
    ppermute x24, starting transfers between devices, shifted(): return lax.ppermute(value, axis, [(i, (i + steps) % 4) for i in range(4)])  31.2 us
    all_gather x3, blocking collectives, gathered(): return lax.all_gather(piece, axes, axis=0, tiled=True)  24.7 us
    ppermute x17, starting transfers between devices, swap(): return lax.ppermute(value, axis, [(0, 1), (1, 0)])  20.4 us
  transfers between devices with their start and end apart: 63, of which 31 were waited for; matrix products, arithmetic and copies ran while one was open for 4% of the time, Pallas kernels for 17%

profile of v4, /device:TPU:1, one launch (start us, length us, event | category | flops | bytes accessed | tf_op | source)
XLA Modules:
  0.0 580.7 jit_solution(685593988299060486)
XLA Ops:
  48.4 17.8 %all-to-all-done.1.pieces = bf16[8,96,1792]{2,1,0:T(8,128)(2,1)} async-done(((bf16[8,96,1792]{2,1,0:T(8,128)(2,1)}), bf16[8,96,1792]{2,1,0:T(8,128)(2,1)}, u32[]{:S(2)}, u32[]{:S(2)}) %all-to-all-start.1) | async-done | bytes 2752544 | tf_op jit(solution)/shard_map/all_to_all | solution.py:41
  78.7 7.2 %collective-permute-done.9.refs_1_ = bf16[4,112,512]{2,1,0:T(8,128)(2,1)S(1)} collective-permute-done((bf16[4,112,512]{2,1,0:T(8,128)(2,1)S(1)}, bf16[4,112,512]{2,1,0:T(8,128)(2,1)S(1)}, u32[]{:S(2)}, u32[]{:S(2)}) %collective-permute-start.9) | collective-permute-done | bytes 458784 | tf_op jit(solution)/shard_map/ppermute | solution.py:407
  85.9 10.3 %collective-permute-done.11.refs_3_ = bf16[4,112,512]{2,1,0:T(8,128)(2,1)S(1)} collective-permute-done((bf16[4,112,512]{2,1,0:T(8,128)(2,1)S(1)}, bf16[4,112,512]{2,1,0:T(8,128)(2,1)S(1)}, u32[]{:S(2)}, u32[]{:S(2)}) %collective-permute-start.11) | collective-permute-done | bytes 458784 | tf_op jit(solution)/shard_map/ppermute | solution.py:407
  121.9 13.0 %all-to-all-done.2 = bf16[16,128,128]{2,1,0:T(8,128)(2,1)S(1)} async-done(((bf16[16,128,128]{2,1,0:T(8,128)(2,1)}), bf16[16,128,128]{2,1,0:T(8,128)(2,1)S(1)}, u32[]{:S(2)}, u32[]{:S(2)}) %all-to-all-start.2) | async-done | bytes 524320 | tf_op jit(solution)/shard_map/all_to_all | solution.py:41
  155.6 16.6 %all_to_all.95 = bf16[8,32,1536]{2,1,0:T(8,128)(2,1)S(1)} all-to-all(bf16[8,32,1536]{2,1,0:T(8,128)(2,1)S(1)} %get-tuple-element.135), channel_id=1, replica_groups=mesh['s'=2,'y'=4,'z'=4,'x'=2,'c'=2] {'z','x'}, dimensions={0} | all-to-all | bytes 1572864 | tf_op jit(solution)/shard_map/all_to_all | solution.py:41
  183.4 15.1 %all-to-all-done.5.pieces = bf16[8,32,1536]{2,1,0:T(8,128)(2,1)S(1)} async-done(((bf16[8,32,1536]{2,1,0:T(8,128)(2,1)}), bf16[8,32,1536]{2,1,0:T(8,128)(2,1)S(1)}, u32[]{:S(2)}, u32[]{:S(2)}) %all-to-all-start.5) | async-done | bytes 786464 | tf_op jit(solution)/shard_map/all_to_all | solution.py:41
  198.7 8.4 %all_gather.19.xin = bf16[128,1536]{1,0:T(8,128)(2,1)S(1)} all-gather(bf16[32,1536]{1,0:T(8,128)(2,1)S(1)} %shard_map.228.xin), channel_id=1, replica_groups=mesh['s'=2,'y'=4,'z'=4,'x'=2,'c'=2] {'x','c'}, dimensions={0}, use_global_device_ids=true | all-gather | bytes 491520 | tf_op jit(solution)/shard_map/all_gather | solution.py:661
  209.6 17.4 %all_to_all.96 = bf16[16,128,128]{2,1,0:T(8,128)(2,1)S(1)} all-to-all(bf16[16,128,128]{2,1,0:T(8,128)(2,1)S(1)} %get-tuple-element.142), channel_id=1, replica_groups=mesh['s'=2,'y'=4,'z'=4,'x'=2,'c'=2] {'y','z'}, dimensions={0} | all-to-all | bytes 1048576 | tf_op jit(solution)/shard_map/all_to_all | solution.py:41
  247.8 15.9 %all_to_all.97 = bf16[8,32,1536]{2,1,0:T(8,128)(2,1)S(1)} all-to-all(bf16[8,32,1536]{2,1,0:T(8,128)(2,1)S(1)} %get-tuple-element.146), channel_id=1, replica_groups=mesh['s'=2,'y'=4,'z'=4,'x'=2,'c'=2] {'z','x'}, dimensions={0} | all-to-all | bytes 1572864 | tf_op jit(solution)/shard_map/all_to_all | solution.py:41
  269.1 16.9 %all_to_all.98 = bf16[8,32,1536]{2,1,0:T(8,128)(2,1)} all-to-all(bf16[8,32,1536]{2,1,0:T(8,128)(2,1)S(1)} %broadcast_in_dim.71), channel_id=1, replica_groups=mesh['s'=2,'y'=4,'z'=4,'x'=2,'c'=2] {'z','x'}, dimensions={0} | all-to-all | bytes 1572864 | tf_op jit(solution)/shard_map/all_to_all | solution.py:41
  300.0 7.6 %shard_map.233 = (bf16[256,1536]{1,0:T(8,128)(2,1)S(1)}, bf16[256,1792]{1,0:T(8,128)(2,1)}, bf16[256,1792]{1,0:T(8,128)(2,1)}) custom-call(bf16[256,1536]{1,0:T(8,128)(2,1)} %bitcast.46.grads, bf16[1536,1792]{1,0:T(8,128)(2,1)} %all-gather.8.cloned.1.call-done.own, bf16[1536,1792]{1,0:T(8,128)(2,1)} %copy-done.31, ...), custom_call_target="tpu_custom_call" | custom-call | flops 3019898880 | bytes 17000000 | tf_op jit(solution)/shard_map/pallas_call | solution.py:65
  315.9 8.4 %shard_map.234 = bf16[1536,1792]{1,0:T(8,128)(2,1)} custom-call(bf16[256,1536]{1,0:T(8,128)(2,1)S(1)} %bitcast.142, bf16[256,1536]{1,0:T(8,128)(2,1)} %collective-permute-done.19.tokens_other, bf16[256,1536]{1,0:T(8,128)(2,1)} %bitcast.46.grads, bf16[256,1536]{1,0:T(8,128)(2,1)} %collective-permute-done.20.grads_other, ...), custom_call_target="tpu_custom_call" | custom-call | flops 3019898880 | bytes 12000000 | tf_op jit(solution)/shard_map/pallas_call | solution.py:65
  327.9 9.2 %all_gather.22.grad_att = bf16[128,1536]{1,0:T(8,128)(2,1)S(1)} all-gather(bf16[32,1536]{1,0:T(8,128)(2,1)S(1)} %get-tuple-element.160), channel_id=1, replica_groups=mesh['s'=2,'y'=4,'z'=4,'x'=2,'c'=2] {'x','c'}, dimensions={0}, use_global_device_ids=true | all-gather | bytes 491520 | tf_op jit(solution)/shard_map/all_gather | solution.py:661
  337.2 7.1 %shard_map.236 = (bf16[128,384]{1,0:T(8,128)(2,1)S(1)}, f32[2048,128]{1,0:T(8,128)}, bf16[2048,128]{1,0:T(8,128)(2,1)S(1)}) custom-call(s32[2]{0:T(128)S(1)} %pad_add_fusion.flag, bf16[3,128,128]{2,1,0:T(8,128)(2,1)S(1)} %copy-done.18, bf16[2048,128]{1,0:T(8,128)(2,1)S(1)} %bitcast.131, bf16[2048,128]{1,0:T(8,128)(2,1)} %copy-done.3, ...), custom_call_target="tpu_custom_call" | custom-call | flops 1157627904 | bytes 5000000 | tf_op jit(solution)/shard_map/pallas_call | solution.py:65
  347.7 18.0 %all_to_all.99.pieces = bf16[16,128,128]{2,1,0:T(8,128)(2,1)S(1)} all-to-all(bf16[16,128,128]{2,1,0:T(8,128)(2,1)S(1)} %bitcast.162), channel_id=1, replica_groups=mesh['s'=2,'y'=4,'z'=4,'x'=2,'c'=2] {'y','z'}, dimensions={0} | all-to-all | bytes 1048576 | tf_op jit(solution)/shard_map/all_to_all | solution.py:41
  368.4 10.5 %all_to_all.100.pieces = bf16[4,32,1536]{2,1,0:T(8,128)(2,1)S(1)} all-to-all(bf16[4,32,1536]{2,1,0:T(8,128)(2,1)S(1)} %get-tuple-element.164), channel_id=1, replica_groups=mesh['s'=2,'y'=4,'z'=4,'x'=2,'c'=2] {'x','c'}, dimensions={0} | all-to-all | bytes 786432 | tf_op jit(solution)/shard_map/all_to_all | solution.py:41
  388.1 8.0 %all-to-all-done.14 = bf16[8,32,1536]{2,1,0:T(8,128)(2,1)S(1)} async-done(((bf16[8,32,1536]{2,1,0:T(8,128)(2,1)}), bf16[8,32,1536]{2,1,0:T(8,128)(2,1)S(1)}, u32[]{:S(2)}, u32[]{:S(2)}) %all-to-all-start.14) | async-done | bytes 786464 | tf_op jit(solution)/shard_map/all_to_all | solution.py:41
  396.1 8.5 %shard_map.240 = (bf16[256,1536]{1,0:T(8,128)(2,1)}, bf16[256,1792]{1,0:T(8,128)(2,1)}, bf16[256,1792]{1,0:T(8,128)(2,1)}) custom-call(bf16[256,1536]{1,0:T(8,128)(2,1)S(1)} %bitcast.137, bf16[1536,1792]{1,0:T(8,128)(2,1)} %all-gather.4.cloned.1.call-done.own, bf16[1536,1792]{1,0:T(8,128)(2,1)} %collective-permute-done.16.other, ...), custom_call_target="tpu_custom_call" | custom-call | flops 3019898880 | bytes 17000000 | tf_op jit(solution)/shard_map/pallas_call | solution.py:65
  411.6 8.3 %shard_map.241 = bf16[1536,1792]{1,0:T(8,128)(2,1)} custom-call(bf16[256,1536]{1,0:T(8,128)(2,1)S(1)} %bitcast.136, bf16[256,1536]{1,0:T(8,128)(2,1)S(1)} %collective-permute-done.23.tokens_other, bf16[256,1536]{1,0:T(8,128)(2,1)} %bitcast.139, bf16[256,1536]{1,0:T(8,128)(2,1)} %collective-permute-done.24.grads_other, ...), custom_call_target="tpu_custom_call" | custom-call | flops 3019898880 | bytes 12000000 | tf_op jit(solution)/shard_map/pallas_call | solution.py:65
  419.9 8.5 %all-to-all-done.15.pieces = bf16[8,32,1536]{2,1,0:T(8,128)(2,1)} async-done(((bf16[8,32,1536]{2,1,0:T(8,128)(2,1)}), bf16[8,32,1536]{2,1,0:T(8,128)(2,1)}, u32[]{:S(2)}, u32[]{:S(2)}) %all-to-all-start.15) | async-done | bytes 786464 | tf_op jit(solution)/shard_map/all_to_all | solution.py:41
  428.4 11.1 %reduce-scatter.7.cloned.1.call-done = bf16[384,896]{1,0:T(8,128)(2,1)} async-done(((bf16[1536,896]{1,0:T(8,128)(2,1)}), bf16[384,896]{1,0:T(8,128)(2,1)}) %reduce-scatter.7.cloned.1.call-update) | async-done | bytes 688144 | tf_op jit(solution)/shard_map/reduce_scatter | solution.py:798
  448.9 7.7 %shard_map.243 = (bf16[128,384]{1,0:T(8,128)(2,1)S(1)}, f32[2048,128]{1,0:T(8,128)}, bf16[2048,128]{1,0:T(8,128)(2,1)S(1)}) custom-call(s32[2]{0:T(128)S(1)} %pad_add_fusion.flag, bf16[3,128,128]{2,1,0:T(8,128)(2,1)S(1)} %copy-done.22, bf16[2048,128]{1,0:T(8,128)(2,1)S(1)} %bitcast.146, bf16[2048,128]{1,0:T(8,128)(2,1)} %copy-done.13, ...), custom_call_target="tpu_custom_call" | custom-call | flops 1157627904 | bytes 5000000 | tf_op jit(solution)/shard_map/pallas_call | solution.py:65
  460.0 19.3 %all_to_all.101.pieces = bf16[16,128,128]{2,1,0:T(8,128)(2,1)S(1)} all-to-all(bf16[16,128,128]{2,1,0:T(8,128)(2,1)S(1)} %bitcast.163), channel_id=1, replica_groups=mesh['s'=2,'y'=4,'z'=4,'x'=2,'c'=2] {'y','z'}, dimensions={0} | all-to-all | bytes 1048576 | tf_op jit(solution)/shard_map/all_to_all | solution.py:41
  531.2 7.9 %collective-permute-done.34 = bf16[4,96,384]{2,1,0:T(8,128)(2,1)} collective-permute-done((bf16[4,96,384]{2,1,0:T(8,128)(2,1)S(1)}, bf16[4,96,384]{2,1,0:T(8,128)(2,1)}, u32[]{:S(2)}, u32[]{:S(2)}) %collective-permute-start.34) | collective-permute-done | bytes 294944 | tf_op jit(solution)/shard_map/ppermute | solution.py:407
  (344 shorter events, 284.8 us)
Async XLA Ops:
  26.2 40.1 %all-to-all-start.1 = ((bf16[8,96,1792]{2,1,0:T(8,128)(2,1)}), bf16[8,96,1792]{2,1,0:T(8,128)(2,1)}, u32[]{:S(2)}, u32[]{:S(2)}) async-start(bf16[8,96,1792]{2,1,0:T(8,128)(2,1)} %shard_map.220), calls=%async_computation.1 | async-start | bytes 5505024 | tf_op jit(solution)/shard_map/all_to_all | solution.py:41
  33.0 111.6 %all-gather.4.cloned.1.call-start = ((), (), s32[]{:S(2)}) async-start(), calls=%async_computation.23 | async-start | bytes 6881280 | tf_op jit(solution)/shard_map/all_gather | solution.py:661
  74.2 26.7 %collective-permute-start.10 = (bf16[4,112,512]{2,1,0:T(8,128)(2,1)S(1)}, bf16[4,112,512]{2,1,0:T(8,128)(2,1)S(1)}, u32[]{:S(2)}, u32[]{:S(2)}) collective-permute-start(bf16[4,112,512]{2,1,0:T(8,128)(2,1)S(1)} %pad_maximum_fusion.1.refs_0_), channel_id=1, source_target_pairs={{0,8},{4,12},{8,0},{12,4},{1,9},{5,13},{9,1},{13,5},{2,10},{6,14},... | collective-permute-start | bytes 1376264 | tf_op jit(solution)/shard_map/ppermute | solution.py:407
  76.9 19.3 %collective-permute-start.11 = (bf16[4,112,512]{2,1,0:T(8,128)(2,1)S(1)}, bf16[4,112,512]{2,1,0:T(8,128)(2,1)S(1)}, u32[]{:S(2)}, u32[]{:S(2)}) collective-permute-start(bf16[4,112,512]{2,1,0:T(8,128)(2,1)S(1)} %pad_maximum_fusion.1.refs_0_), channel_id=1, source_target_pairs={{0,12},{4,0},{8,4},{12,8},{1,13},{5,1},{9,5},{13,9},{2,14},{6,2},{... | collective-permute-start | bytes 1376264 | tf_op jit(solution)/shard_map/ppermute | solution.py:407
  98.3 15.7 %collective-permute-start.13 = (bf16[4,96,384]{2,1,0:T(8,128)(2,1)S(1)}, bf16[4,96,384]{2,1,0:T(8,128)(2,1)S(1)}, u32[]{:S(2)}, u32[]{:S(2)}) collective-permute-start(bf16[4,96,384]{2,1,0:T(8,128)(2,1)S(1)} %pad_maximum_fusion.3.refs_0_), channel_id=1, source_target_pairs={{0,8},{4,12},{8,0},{12,4},{1,9},{5,13},{9,1},{13,5},{2,10},{6,14},... | collective-permute-start | bytes 884744 | tf_op jit(solution)/shard_map/ppermute | solution.py:407
  114.0 20.9 %all-to-all-start.2 = ((bf16[16,128,128]{2,1,0:T(8,128)(2,1)}), bf16[16,128,128]{2,1,0:T(8,128)(2,1)S(1)}, u32[]{:S(2)}, u32[]{:S(2)}) async-start(bf16[16,128,128]{2,1,0:T(8,128)(2,1)} %get-tuple-element.126), calls=%async_computation.2 | async-start | bytes 1048576 | tf_op jit(solution)/shard_map/all_to_all | solution.py:41
  120.4 86.7 %all-gather.6.cloned.1.call-start = ((), (), s32[]{:S(2)}) async-start(), calls=%async_computation.24 | async-start | bytes 2924544 | tf_op jit(solution)/shard_map/all_gather | solution.py:661
  148.8 118.7 %all-gather.8.cloned.1.call-start = ((), (), s32[]{:S(2)}) async-start(), calls=%async_computation.25 | async-start | bytes 6881280 | tf_op jit(solution)/shard_map/all_gather | solution.py:661
  179.2 19.4 %all-to-all-start.5 = ((bf16[8,32,1536]{2,1,0:T(8,128)(2,1)}), bf16[8,32,1536]{2,1,0:T(8,128)(2,1)S(1)}, u32[]{:S(2)}, u32[]{:S(2)}) async-start(bf16[8,32,1536]{2,1,0:T(8,128)(2,1)} %bitcast.39), calls=%async_computation.5 | async-start | bytes 1572864 | tf_op jit(solution)/shard_map/all_to_all | solution.py:41
  267.5 18.5 %collective-permute-start.18 = (bf16[1536,1792]{1,0:T(8,128)(2,1)}, bf16[1536,1792]{1,0:T(8,128)(2,1)S(1)}, u32[]{:S(2)}, u32[]{:S(2)}) collective-permute-start(bf16[1536,1792]{1,0:T(8,128)(2,1)} %all-gather.8.cloned.1.call-done.own), channel_id=1, source_target_pairs={{0,1},{1,0},{2,3},{3,2},{4,5},{5,4},{6,7},{7,6},{8,9},{9,8},{10,11... | collective-permute-start | bytes 16515080 | tf_op jit(solution)/shard_map/ppermute | solution.py:37
  295.6 15.9 %all-to-all-start.10 = ((bf16[8,32,1536]{2,1,0:T(8,128)(2,1)}), bf16[8,32,1536]{2,1,0:T(8,128)(2,1)}, u32[]{:S(2)}, u32[]{:S(2)}) async-start(bf16[8,32,1536]{2,1,0:T(8,128)(2,1)} %bitcast.153), calls=%async_computation.10 | async-start | bytes 1572864 | tf_op jit(solution)/shard_map/all_to_all | solution.py:41
  311.6 14.9 %all-to-all-start.11 = ((bf16[8,32,1536]{2,1,0:T(8,128)(2,1)}), bf16[8,32,1536]{2,1,0:T(8,128)(2,1)}, u32[]{:S(2)}, u32[]{:S(2)}) async-start(bf16[8,32,1536]{2,1,0:T(8,128)(2,1)} %bitcast.152), calls=%async_computation.11 | async-start | bytes 1572864 | tf_op jit(solution)/shard_map/all_to_all | solution.py:41
  315.8 80.3 %reduce-scatter.5.cloned.1.call-start = ((), (), s32[]{:S(2)}) async-start(), calls=%async_computation.26 | async-start | bytes 6881280 | tf_op jit(solution)/shard_map/reduce_scatter | solution.py:771
  380.1 16.0 %all-to-all-start.14 = ((bf16[8,32,1536]{2,1,0:T(8,128)(2,1)}), bf16[8,32,1536]{2,1,0:T(8,128)(2,1)S(1)}, u32[]{:S(2)}, u32[]{:S(2)}) async-start(bf16[8,32,1536]{2,1,0:T(8,128)(2,1)} %copy-done.8), calls=%async_computation.14 | async-start | bytes 1572864 | tf_op jit(solution)/shard_map/all_to_all | solution.py:41
  384.4 55.2 %reduce-scatter.7.cloned.1.call-start = ((), (), s32[]{:S(2)}) async-start(), calls=%async_computation.27 | async-start | bytes 3440640 | tf_op jit(solution)/shard_map/reduce_scatter | solution.py:798
  407.3 21.1 %all-to-all-start.15 = ((bf16[8,32,1536]{2,1,0:T(8,128)(2,1)}), bf16[8,32,1536]{2,1,0:T(8,128)(2,1)}, u32[]{:S(2)}, u32[]{:S(2)}) async-start(bf16[8,32,1536]{2,1,0:T(8,128)(2,1)} %bitcast.51), calls=%async_computation.15 | async-start | bytes 1572864 | tf_op jit(solution)/shard_map/all_to_all | solution.py:41
  411.5 93.2 %reduce-scatter.9.cloned.1.call-start = ((), (), s32[]{:S(2)}) async-start(), calls=%async_computation.28 | async-start | bytes 6881280 | tf_op jit(solution)/shard_map/reduce_scatter | solution.py:771
  487.8 20.5 %collective-permute-start.27 = (bf16[4,112,512]{2,1,0:T(8,128)(2,1)}, bf16[4,112,512]{2,1,0:T(8,128)(2,1)S(1)}, u32[]{:S(2)}, u32[]{:S(2)}) collective-permute-start(bf16[4,112,512]{2,1,0:T(8,128)(2,1)} %get-tuple-element.190), channel_id=1, source_target_pairs={{0,4},{4,8},{8,12},{12,0},{1,5},{5,9},{9,13},{13,1},{2,6},{6,10},{... | collective-permute-start | bytes 1376264 | tf_op jit(solution)/shard_map/ppermute | solution.py:407
  488.1 23.0 %collective-permute-start.28 = (bf16[4,112,512]{2,1,0:T(8,128)(2,1)}, bf16[4,112,512]{2,1,0:T(8,128)(2,1)S(1)}, u32[]{:S(2)}, u32[]{:S(2)}) collective-permute-start(bf16[4,112,512]{2,1,0:T(8,128)(2,1)} %get-tuple-element.191), channel_id=1, source_target_pairs={{0,8},{4,12},{8,0},{12,4},{1,9},{5,13},{9,1},{13,5},{2,10},{6,14},... | collective-permute-start | bytes 1376264 | tf_op jit(solution)/shard_map/ppermute | solution.py:407
  492.0 19.5 %collective-permute-start.29 = (bf16[4,112,512]{2,1,0:T(8,128)(2,1)}, bf16[4,112,512]{2,1,0:T(8,128)(2,1)}, u32[]{:S(2)}, u32[]{:S(2)}) collective-permute-start(bf16[4,112,512]{2,1,0:T(8,128)(2,1)} %get-tuple-element.192), channel_id=1, source_target_pairs={{0,12},{4,0},{8,4},{12,8},{1,13},{5,1},{9,5},{13,9},{2,14},{6,2},{... | collective-permute-start | bytes 1376264 | tf_op jit(solution)/shard_map/ppermute | solution.py:407
  493.3 18.7 %all-to-all-start.17 = ((bf16[4,32,1536]{2,1,0:T(8,128)(2,1)}), bf16[4,32,1536]{2,1,0:T(8,128)(2,1)S(1)}, u32[]{:S(2)}, u32[]{:S(2)}) async-start(bf16[4,32,1536]{2,1,0:T(8,128)(2,1)} %get-tuple-element.197), calls=%async_computation.17 | async-start | bytes 786432 | tf_op jit(solution)/shard_map/all_to_all | solution.py:41
  511.9 40.6 %all-to-all-start.18 = ((bf16[8,96,1792]{2,1,0:T(8,128)(2,1)}), bf16[8,96,1792]{2,1,0:T(8,128)(2,1)}, u32[]{:S(2)}, u32[]{:S(2)}) async-start(bf16[8,96,1792]{2,1,0:T(8,128)(2,1)} %bitcast.160), calls=%async_computation.21 | async-start | bytes 5505024 | tf_op jit(solution)/shard_map/all_to_all | solution.py:41
  518.4 37.5 %reduce-scatter.11.cloned.1.call-start = ((), (), s32[]{:S(2)}) async-start(), calls=%async_computation.29 | async-start | bytes 860160 | tf_op jit(solution)/shard_map/reduce_scatter | solution.py:811
  522.5 16.6 %collective-permute-start.34 = (bf16[4,96,384]{2,1,0:T(8,128)(2,1)S(1)}, bf16[4,96,384]{2,1,0:T(8,128)(2,1)}, u32[]{:S(2)}, u32[]{:S(2)}) collective-permute-start(bf16[4,96,384]{2,1,0:T(8,128)(2,1)S(1)} %get-tuple-element.210), channel_id=1, source_target_pairs={{0,16},{16,32},{32,48},{48,0},{1,17},{17,33},{33,49},{49,1},{2,18}... | collective-permute-start | bytes 884744 | tf_op jit(solution)/shard_map/ppermute | solution.py:407
  (80 other events, 832.8 us)
Sparse Core Ops, SparseCore 0:
  69.8 63.3 all-gather.3
  326.6 63.1 reduce-scatter.4
  524.4 23.5 reduce-scatter.10
Sparse Core Ops, SparseCore 1:
  144.8 57.0 all-gather.5
  203.5 64.0 all-gather.7
  396.2 43.3 reduce-scatter.6
  442.1 62.6 reduce-scatter.8

commit v5 on v4

--- a/solution.py
+++ b/solution.py
@@ -128,7 +128,7 @@
 
 
 def attend_kernel(
-    first, flag, query, kv_mine, kv_other, seg_col, seg_row, weight, attended, lse, part, top, total, acc, out_t, sem
+    first, flag, query, kv_mine, kv_other, seg_col, seg_row, weight, attended, wide, lse, part, top, total, acc, out_t, sem
 ):
     copy = fetch(weight, first, out_t, sem)
     query_all = query[...].reshape(3 * HEAD, HEAD)
@@ -157,6 +157,7 @@
 
     lse[...] = top[...] + jnp.log(total[...])
     done = acc[...] / total[...]
+    wide[...] = done
     for h in range(3):
         attended[:, pl.ds(h * HEAD, HEAD)] = done[:, h * HEAD : (h + 1) * HEAD].T.astype(BF)
     copy.wait()
@@ -168,7 +169,7 @@
 def attend(flag, query, kv_mine, kv_other, seg_col, seg_row, weight, first):
     return call(
         functools.partial(attend_kernel, first),
-        (arr((HEAD, QCOLS)), arr((1, QCOLS), F32), arr((4, 32, WIDTH))),
+        (arr((HEAD, QCOLS)), arr((HEAD, QCOLS), F32), arr((1, QCOLS), F32), arr((4, 32, WIDTH))),
         [SMEM] + [VMEM] * 5 + [ANY],
         (flag, query, kv_mine, kv_other, seg_col, seg_row, weight),
         [
@@ -184,7 +185,7 @@
 
 
 def attend_back_kernel(
-    first, flag, query, kv_mine, kv_other, seg_col, seg_row, lse, attended, grad_att, cosine, sine, weight,
+    first, flag, query, kv_mine, kv_other, seg_col, seg_row, lse, wide, grad_att, cosine, sine, weight,
     grad_query, kept, sent, low, acc, out_t, sem
 ):
     copy = fetch(weight, first, out_t, sem)
@@ -197,8 +198,8 @@
     for h in range(3):
         grad_head = grad_attended[:, h * HEAD : (h + 1) * HEAD]
         low[pl.ds(h * HEAD, HEAD), :] = grad_head
-        with_output = grad_head.astype(F32) * attended[:, pl.ds(h * HEAD, HEAD)].astype(F32)
-        sums.append(jnp.sum(with_output.T, axis=0, keepdims=True))
+        with_output = grad_head.astype(F32).T * wide[:, pl.ds(h * HEAD, HEAD)]
+        sums.append(jnp.sum(with_output, axis=0, keepdims=True))
     grad_rows = low[...]
     lse_row = lse[...]
 
@@ -237,12 +238,12 @@
         grad_query[:, pl.ds(h * HEAD, HEAD)] = turned(rows, cos, -sin).astype(BF)
 
 
-def attend_back(flag, query, kv_mine, kv_other, seg_col, seg_row, lse, attended, grad_att, cosine, sine, weight, first):
+def attend_back(flag, query, kv_mine, kv_other, seg_col, seg_row, lse, wide, grad_att, cosine, sine, weight, first):
     return call(
         functools.partial(attend_back_kernel, first),
         (arr((HEAD, QCOLS)), arr((SEQ, HEAD), F32), arr((SEQ, HEAD))),
         [SMEM] + [VMEM] * 10 + [ANY],
-        (flag, query, kv_mine, kv_other, seg_col, seg_row, lse, attended, grad_att, cosine, sine, weight),
+        (flag, query, kv_mine, kv_other, seg_col, seg_row, lse, wide, grad_att, cosine, sine, weight),
         [pltpu.VMEM((3 * HEAD, HEAD), BF), pltpu.VMEM((HEAD, QCOLS), F32), *fetched(QCOLS)],
         flops=10 * 384 * 2048 * 128 + 2 * 128 * 384 * 1536,
         size=5_000_000,
@@ -344,6 +345,20 @@
     )
 
 
+def feed_grads(gate, up, grad_hidden, result):
+    sig = jax.nn.sigmoid(gate)
+    silu = gate * sig
+    grad_gate = grad_hidden * up * sig * (1.0 + gate * (1.0 - sig))
+    grad_up = grad_hidden * silu
+    tail = grad_gate[:, MAIN:] + pltpu.roll(grad_up[:, MAIN:], PART, 1)
+    hidden = known(silu * up).astype(BF)
+    result[:, pl.ds(0, MAIN)] = grad_gate[:, :MAIN].astype(BF)
+    result[:, pl.ds(MAIN, MAIN)] = grad_up[:, :MAIN].astype(BF)
+    result[:, pl.ds(2 * MAIN, 2 * PART)] = tail.astype(BF)
+    result[:, pl.ds(GU, DOWN)] = hidden
+    return hidden
+
+
 def feed_back_kernel(grads, own, other, gate_up_in, part, for_own, for_other, gate_up, down, acc, sems):
     copies = weight_copies(own, other, gate_up, down, sems, ("down", "gate_up"))
     rows = grads[...]
@@ -351,15 +366,7 @@
         copies[i, "down"].wait()
         grad_hidden = nn(rows, down[i])
         gate, up = gate_and_up(gate_up_in[i].astype(F32))
-        sig = jax.nn.sigmoid(gate)
-        silu = gate * sig
-        grad_gate = grad_hidden * up * sig * (1.0 + gate * (1.0 - sig))
-        grad_up = grad_hidden * silu
-        tail = grad_gate[:, MAIN:] + pltpu.roll(grad_up[:, MAIN:], PART, 1)
-        result[:, pl.ds(0, MAIN)] = grad_gate[:, :MAIN].astype(BF)
-        result[:, pl.ds(MAIN, MAIN)] = grad_up[:, :MAIN].astype(BF)
-        result[:, pl.ds(2 * MAIN, 2 * PART)] = tail.astype(BF)
-        result[:, pl.ds(GU, DOWN)] = known(silu * up).astype(BF)
+        feed_grads(gate, up, grad_hidden, result)
         copies[i, "gate_up"].wait()
         out = nt(result[:, pl.ds(0, GU)], gate_up[i])
         if i == 0:
@@ -376,6 +383,39 @@
         (grads, own, other, gate_up),
         FEED_SCRATCH,
         flops=2 * 256 * 1536 * 3840,
+        size=17_000_000,
+        exps=256 * 1280,
+    )
+
+
+def feed_both_kernel(
+    tokens, grads, own, other, part, for_own, for_other, gate_up, down, acc, acc_back, sems
+):
+    copies = weight_copies(own, other, gate_up, down, sems, ("gate_up", "down"))
+    rows, grad_rows = tokens[...], grads[...]
+    for i, result in enumerate((for_own, for_other)):
+        copies[i, "gate_up"].wait()
+        gate, up = gate_and_up(nn(rows, gate_up[i]))
+        copies[i, "down"].wait()
+        grad_hidden = nn(grad_rows, down[i])
+        hidden = feed_grads(gate, up, grad_hidden, result)
+        out, back = nt(hidden, down[i]), nt(result[:, pl.ds(0, GU)], gate_up[i])
+        if i == 0:
+            acc[...] = out
+            acc_back[...] = back
+        else:
+            part[:, pl.ds(0, 32), :] = (acc_back[...] + back).astype(BF).reshape(8, 32, WIDTH)
+            part[:, pl.ds(32, 32), :] = (acc[...] + out).astype(BF).reshape(8, 32, WIDTH)
+
+
+def feed_both(tokens, grads, own, other):
+    return call(
+        feed_both_kernel,
+        (arr((8, 64, WIDTH)), arr((256, FW)), arr((256, FW))),
+        [VMEM, VMEM, ANY, ANY],
+        (tokens, grads, own, other),
+        FEED_SCRATCH[:3] + [pltpu.VMEM((256, WIDTH), F32)] + FEED_SCRATCH[3:],
+        flops=4 * 256 * 1536 * 3840,
         size=17_000_000,
         exps=256 * 1280,
     )
@@ -533,7 +573,8 @@
 
 
 def after_feed_kernel(pieces, mixed, out):
-    out[...] = (mixed[...] + jnp.sum(pieces[...].astype(F32), axis=0)).astype(BF)
+    last = pl.ds(pieces.shape[1] - 32, 32)
+    out[...] = (mixed[...] + jnp.sum(pieces[:, last, :].astype(F32), axis=0)).astype(BF)
 
 
 def after_feed(pieces, mixed):
@@ -549,7 +590,7 @@
 
 
 def before_heads_kernel(pieces, mixed, gain, grad_out, grad_mixed, low, grad_gain):
-    grad = jnp.sum(pieces[...].astype(F32), axis=0)
+    grad = jnp.sum(pieces[:, pl.ds(0, 32), :].astype(F32), axis=0)
     result, sums = norm_back(grad, mixed[...], gain[...], grad_out[...].astype(F32))
     grad_mixed[...] = result
     low[...] = result.astype(BF)
@@ -731,7 +772,7 @@
     out_first = assemble(y_then_z, out_ring)
     kv_mine1 = exchange(kv, ("y", "z")).reshape(SEQ, HEAD)
     kv_other1 = swap(kv_mine1, "c")
-    attended1, lse1, part = attend(flag, query1, kv_mine1, kv_other1, seg_col, seg_row, out_first, 0)
+    attended1, wide1, lse1, part = attend(flag, query1, kv_mine1, kv_other1, seg_col, seg_row, out_first, 0)
     other1 = swap(after(own1, part), "c")
     mixed1, low = after_heads(after(exchange(part, ("x", "c")), other1), xin, gain_b1)
     second1 = exchange(low, ("z", "x")).reshape(256, WIDTH)
@@ -745,21 +786,18 @@
     normed2, query2, kv = qkv_columns(flag, x_block2, gain_a2, all_second, bias2, cosine, sine)
     kv_mine2 = exchange(kv, ("y", "z")).reshape(SEQ, HEAD)
     kv_other2 = swap(kv_mine2, "c")
-    attended2, lse2, part = attend(flag, query2, kv_mine2, kv_other2, seg_col, seg_row, all_second, 512)
+    attended2, wide2, lse2, part = attend(flag, query2, kv_mine2, kv_other2, seg_col, seg_row, all_second, 512)
     mixed2, low = after_heads(exchange(part, ("x", "c")), out_one, gain_b2)
     second2 = exchange(low, ("z", "x")).reshape(256, WIDTH)
     other2 = swap(after(own2, second2), "c")
     cot_low = spread(after(cot, (second2, own2)), 8, ("z", "x")).reshape(256, WIDTH)
     second2 = after(second2, cot_low)
-    part, gate_up2 = feed(second2, own2, other2)
-    out_pieces = exchange(part.reshape(8, 32, WIDTH), ("z", "x"))
-
-    def backward(grad_out, grad_low, gate_up, second, own, other, mixed, gain_b, xin, x_block, gain_a, normed, query,
-                 attended, kv_mine, kv_other, lse, weight, out_t, first, before=None, earlier=None):
-        part, for_own, for_other = feed_back(grad_low, own, other, gate_up)
-        if before is not None:
-            part, before = lax.optimization_barrier((part, before))
-        pieces = exchange(part.reshape(8, 32, WIDTH), ("z", "x"))
+    fed2 = feed_both(second2, cot_low, own2, other2)
+
+    def backward(grad_out, grad_low, fed, second, mixed, gain_b, xin, x_block, gain_a, normed, query, attended, wide,
+                 kv_mine, kv_other, lse, weight, out_t, first, earlier=None):
+        part, for_own, for_other = fed
+        pieces = fed_pieces = exchange(part.reshape(8, -1, WIDTH), ("z", "x"))
         given = swap(for_other, "c")
         second_other, grad_other = swap(second, "c"), swap(grad_low, "c")
         grad_ffn = feed_grad(second, second_other, grad_low, grad_other, for_own, given)
@@ -767,10 +805,10 @@
         grad_mixed, low, grad_gain_b = before_heads(pieces, mixed, gain_b, grad_out)
         grad_att = gathered(low, ("x", "c"))
         if earlier is not None:
-            grad_ffn = after(grad_ffn, earlier)
+            grad_ffn = after(grad_ffn, (earlier, grad_att))
         grad_ffn = lax.psum_scatter(grad_ffn, "y", scatter_dimension=0, tiled=True)
         grad_query, kept_half, sent_half = attend_back(
-            flag, query, kv_mine, kv_other, seg_col, seg_row, lse, attended, grad_att, cosine, sine, out_t, first
+            flag, query, kv_mine, kv_other, seg_col, seg_row, lse, wide, grad_att, cosine, sine, out_t, first
         )
         grad_kv = (kept_half + swap(sent_half, "c").astype(F32)).astype(BF)
         grad_kv = exchange(grad_kv.reshape(16, HEAD, HEAD), ("y", "z"))
@@ -784,11 +822,11 @@
             part = after(part, parts)
         pieces = exchange(part, ("x", "c"))
         grad_in, low = layer_start(pieces, xin, gain_a, grad_mixed)
-        return grad_in, low, grad_ffn, parts
-
-    grad_two, low, ffn_two, attn_two = backward(
-        cot, cot_low, gate_up2, second2, own2, other2, mixed2, gain_b2, out_one, x_block2, gain_a2, normed2, query2,
-        attended2, kv_mine2, kv_other2, lse2, all_second, all_second, 512, before=out_pieces
+        return grad_in, low, grad_ffn, parts, fed_pieces
+
+    grad_two, low, ffn_two, attn_two, out_pieces = backward(
+        cot, cot_low, fed2, second2, mixed2, gain_b2, out_one, x_block2, gain_a2, normed2, query2, attended2, wide2,
+        kv_mine2, kv_other2, lse2, all_second, all_second, 512
     )
     out_two = after_feed(out_pieces, mixed2)
     grad_low = exchange(low, ("z", "x")).reshape(256, WIDTH)
@@ -796,9 +834,10 @@
     grad_low = after(grad_low, attn_two)
     attn_two = after(attn_two, (ffn_two, grad_low))
     attn_two = lax.psum_scatter(attn_two.reshape(16 * 96, 896), "z", scatter_dimension=0, tiled=True)
-    grad_one, _, ffn_one, parts = backward(
-        grad_two, grad_low, gate_up1, second1, own1, other1, mixed1, gain_b1, xin, x_block1, gain_a1, normed1, query1,
-        attended1, kv_mine1, kv_other1, lse1, qkv_first, out_first, 0, earlier=attn_two
+    fed1 = feed_back(grad_low, own1, other1, gate_up1)
+    grad_one, _, ffn_one, parts, _ = backward(
+        grad_two, grad_low, fed1, second1, mixed1, gain_b1, xin, x_block1, gain_a1, normed1, query1, attended1, wide1,
+        kv_mine1, kv_other1, lse1, qkv_first, out_first, 0, earlier=attn_two
     )
     ffn_payload = jnp.concatenate([ffn_one, ffn_two], axis=0).reshape(8, 96, FW)
     qkv_parts = sent(parts[0], "z")

time: 591 us -> 589 us (level)
  waiting for transfers between devices: 162 us -> 139 us
  blocking collectives: 139 us -> 150 us
  local copies, waits for them, and re-layouts: 21 us -> 30.8 us
  starting transfers between devices: 115 us -> 121 us
    ppermute x24, waiting for transfers between devices: 53.6 us -> 32.2 us  [shifted(): return lax.ppermute(value, axis, [(i, (i + steps) % 4) for i in range(4)])]
    reduce_scatter x1, waiting for transfers between devices: 11.1 us -> 0.74 us  [local(): lax.psum_scatter(attn_two.reshape(16 * 96, 896), 'z', scatter_dimension=0...]
    all_to_all x7, blocking collectives: 115 us -> 124 us  [exchange(): return lax.all_to_all(value, axes, split_axis=0, concat_axis=0, tiled=True)]
    unnamed x86 -> x114, local copies, waits for them, and re-layouts: 13 us -> 21.7 us
    ppermute x24, starting transfers between devices: 31.2 us -> 38.6 us  [shifted(): return lax.ppermute(value, axis, [(i, (i + steps) % 4) for i in range(4)])]
    reduce_scatter x2, waiting for transfers between devices: 6.01 us -> 12 us  [backward(): grad_ffn = lax.psum_scatter(grad_ffn, 'y', scatter_dimension=0, tiled=True)]
    pallas_call x29 -> x28, Pallas kernels: 110 us -> 106 us  [call(): pl.pallas_call(kernel, out_shape=out_shape, in_specs=in_specs, scratch_sh...]
    all_to_all x12 -> x11, starting transfers between devices: 59.4 us -> 56.7 us  [exchange(): return lax.all_to_all(value, axes, split_axis=0, concat_axis=0, tiled=True)]
  transfers between devices with their start and end apart: 63 -> 62, of which waited for: 31 -> 30; matrix products, arithmetic and copies ran while one was open for 4% -> 4% of each run, Pallas kernels for 17% -> 16%
where the time goes in v5:
time: 589 us; the launch traced here: 581 us
  blocking collectives  150 us (25%)
  waiting for transfers between devices  139 us (24%)
  starting transfers between devices  121 us (21%)
  Pallas kernels  106 us (18%)
  local copies, waits for them, and re-layouts  30.8 us (5%)
  other arithmetic  17.8 us (3%)
  between operations  16.8 us (3%)
    all_to_all x7, blocking collectives, exchange(): return lax.all_to_all(value, axes, split_axis=0, concat_axis=0, tiled=True)  124 us
    pallas_call x28, Pallas kernels, call(): pl.pallas_call(kernel, out_shape=out_shape, in_specs=in_specs, scratch_sh...  106 us
    all_to_all x11, waiting for transfers between devices, exchange(): return lax.all_to_all(value, axes, split_axis=0, concat_axis=0, tiled=True)  81.3 us
    all_to_all x11, starting transfers between devices, exchange(): return lax.all_to_all(value, axes, split_axis=0, concat_axis=0, tiled=True)  56.7 us
    ppermute x24, starting transfers between devices, shifted(): return lax.ppermute(value, axis, [(i, (i + steps) % 4) for i in range(4)])  38.6 us
    ppermute x24, waiting for transfers between devices, shifted(): return lax.ppermute(value, axis, [(i, (i + steps) % 4) for i in range(4)])  32.2 us
    all_gather x3, blocking collectives, gathered(): return lax.all_gather(piece, axes, axis=0, tiled=True)  25.4 us
    unnamed x114, local copies, waits for them, and re-layouts  21.7 us
  transfers between devices with their start and end apart: 62, of which 30 were waited for; matrix products, arithmetic and copies ran while one was open for 4% of the time, Pallas kernels for 16%

profile of v5, /device:TPU:1, one launch (start us, length us, event | category | flops | bytes accessed | tf_op | source)
XLA Modules:
  0.0 581.3 jit_solution(4199106043092583075)
XLA Ops:
  47.3 19.0 %all-to-all-done.1.pieces = bf16[8,96,1792]{2,1,0:T(8,128)(2,1)} async-done(((bf16[8,96,1792]{2,1,0:T(8,128)(2,1)}), bf16[8,96,1792]{2,1,0:T(8,128)(2,1)}, u32[]{:S(2)}, u32[]{:S(2)}) %all-to-all-start.1) | async-done | bytes 2752544 | tf_op jit(solution)/shard_map/all_to_all | solution.py:41
  78.8 7.2 %collective-permute-done.11.refs_3_ = bf16[4,112,512]{2,1,0:T(8,128)(2,1)S(1)} collective-permute-done((bf16[4,112,512]{2,1,0:T(8,128)(2,1)S(1)}, bf16[4,112,512]{2,1,0:T(8,128)(2,1)S(1)}, u32[]{:S(2)}, u32[]{:S(2)}) %collective-permute-start.11) | collective-permute-done | bytes 458784 | tf_op jit(solution)/shard_map/ppermute | solution.py:447
  89.5 10.1 %collective-permute-start.13 = (bf16[4,96,384]{2,1,0:T(8,128)(2,1)S(1)}, bf16[4,96,384]{2,1,0:T(8,128)(2,1)S(1)}, u32[]{:S(2)}, u32[]{:S(2)}) collective-permute-start(bf16[4,96,384]{2,1,0:T(8,128)(2,1)S(1)} %pad_maximum_fusion.3.refs_0_), channel_id=1, source_target_pairs={{0,8},{4,12},{8,0},{12,4},{1,9},{5,13},{9,1},{13,5},{2,10},{6,14},... | collective-permute-start | bytes 884744 | tf_op jit(solution)/shard_map/ppermute | solution.py:447
  119.4 12.7 %all-to-all-done.2 = bf16[16,128,128]{2,1,0:T(8,128)(2,1)S(1)} async-done(((bf16[16,128,128]{2,1,0:T(8,128)(2,1)}), bf16[16,128,128]{2,1,0:T(8,128)(2,1)S(1)}, u32[]{:S(2)}, u32[]{:S(2)}) %all-to-all-start.2) | async-done | bytes 524320 | tf_op jit(solution)/shard_map/all_to_all | solution.py:41
  154.9 27.4 %all_to_all.90 = bf16[8,32,1536]{2,1,0:T(8,128)(2,1)S(1)} all-to-all(bf16[8,32,1536]{2,1,0:T(8,128)(2,1)S(1)} %get-tuple-element.134), channel_id=1, replica_groups=mesh['s'=2,'y'=4,'z'=4,'x'=2,'c'=2] {'z','x'}, dimensions={0} | all-to-all | bytes 1572864 | tf_op jit(solution)/shard_map/all_to_all | solution.py:41
  182.3 7.3 %shard_map.227 = (bf16[256,1536]{1,0:T(8,128)(2,1)}, bf16[2,256,1152]{2,1,0:T(8,128)(2,1)}) custom-call(bf16[256,1536]{1,0:T(8,128)(2,1)S(1)} %bitcast.132, bf16[1536,1792]{1,0:T(8,128)(2,1)} %all-gather.4.cloned.1.call-done.own, bf16[1536,1792]{1,0:T(8,128)(2,1)} %collective-permute-done.16.other), custom_call_target="tpu_custom_call" | custom-call | flops 3019898880 | bytes 15000000 | tf_op jit(solution)/shard_map/pallas_call | solution.py:65
  195.9 9.1 %all-to-all-done.5.pieces = bf16[8,32,1536]{2,1,0:T(8,128)(2,1)S(1)} async-done(((bf16[8,32,1536]{2,1,0:T(8,128)(2,1)}), bf16[8,32,1536]{2,1,0:T(8,128)(2,1)S(1)}, u32[]{:S(2)}, u32[]{:S(2)}) %all-to-all-start.5) | async-done | bytes 786464 | tf_op jit(solution)/shard_map/all_to_all | solution.py:41
  205.1 10.4 %all_gather.19.xin = bf16[128,1536]{1,0:T(8,128)(2,1)S(1)} all-gather(bf16[32,1536]{1,0:T(8,128)(2,1)S(1)} %shard_map.228.xin), channel_id=1, replica_groups=mesh['s'=2,'y'=4,'z'=4,'x'=2,'c'=2] {'x','c'}, dimensions={0}, use_global_device_ids=true | all-gather | bytes 491520 | tf_op jit(solution)/shard_map/all_gather | solution.py:702
  218.1 17.6 %all_to_all.91 = bf16[16,128,128]{2,1,0:T(8,128)(2,1)S(1)} all-to-all(bf16[16,128,128]{2,1,0:T(8,128)(2,1)S(1)} %get-tuple-element.141), channel_id=1, replica_groups=mesh['s'=2,'y'=4,'z'=4,'x'=2,'c'=2] {'y','z'}, dimensions={0} | all-to-all | bytes 1048576 | tf_op jit(solution)/shard_map/all_to_all | solution.py:41
  257.1 16.1 %all_to_all.92 = bf16[8,32,1536]{2,1,0:T(8,128)(2,1)S(1)} all-to-all(bf16[8,32,1536]{2,1,0:T(8,128)(2,1)S(1)} %get-tuple-element.145), channel_id=1, replica_groups=mesh['s'=2,'y'=4,'z'=4,'x'=2,'c'=2] {'z','x'}, dimensions={0} | all-to-all | bytes 1572864 | tf_op jit(solution)/shard_map/all_to_all | solution.py:41
  275.2 15.2 %all_to_all.93 = bf16[8,32,1536]{2,1,0:T(8,128)(2,1)S(1)} all-to-all(bf16[8,32,1536]{2,1,0:T(8,128)(2,1)S(1)} %broadcast_in_dim.71), channel_id=1, replica_groups=mesh['s'=2,'y'=4,'z'=4,'x'=2,'c'=2] {'z','x'}, dimensions={0} | all-to-all | bytes 1572864 | tf_op jit(solution)/shard_map/all_to_all | solution.py:41
  292.8 10.8 %shard_map.232 = (bf16[8,64,1536]{2,1,0:T(8,128)(2,1)}, bf16[256,1792]{1,0:T(8,128)(2,1)}, bf16[256,1792]{1,0:T(8,128)(2,1)}) custom-call(bf16[256,1536]{1,0:T(8,128)(2,1)S(1)} %bitcast.147, bf16[256,1536]{1,0:T(8,128)(2,1)S(1)} %bitcast.150, bf16[1536,1792]{1,0:T(8,128)(2,1)} %all-gather.8.cloned.1.call-done.own, bf16[1536,1792]{1,0:T(8,128)(2,1)} %copy-done.52), custom_call_target="tpu_custom_call" | custom-call | flops 6039797760 | bytes 17000000 | tf_op jit(solution)/shard_map/pallas_call | solution.py:65
  315.3 8.2 %shard_map.233 = bf16[1536,1792]{1,0:T(8,128)(2,1)} custom-call(bf16[256,1536]{1,0:T(8,128)(2,1)S(1)} %bitcast.149, bf16[256,1536]{1,0:T(8,128)(2,1)S(1)} %collective-permute-done.19.tokens_other, bf16[256,1536]{1,0:T(8,128)(2,1)} %bitcast.152, bf16[256,1536]{1,0:T(8,128)(2,1)} %copy-done.54, bf16[256,1792]{1,0:T(8,128)(2,1)} %get-tuple-element.152.own, ...), custom_call_target="tpu_custom_call" | custom-call | flops 3019898880 | bytes 12000000 | tf_op jit(solution)/shard_map/pallas_call | solution.py:65
  330.4 7.9 %all_gather.22.grad_att = bf16[128,1536]{1,0:T(8,128)(2,1)S(1)} all-gather(bf16[32,1536]{1,0:T(8,128)(2,1)S(1)} %get-tuple-element.156), channel_id=1, replica_groups=mesh['s'=2,'y'=4,'z'=4,'x'=2,'c'=2] {'x','c'}, dimensions={0}, use_global_device_ids=true | all-gather | bytes 491520 | tf_op jit(solution)/shard_map/all_gather | solution.py:702
  340.2 7.1 %shard_map.235 = (bf16[128,384]{1,0:T(8,128)(2,1)S(1)}, f32[2048,128]{1,0:T(8,128)}, bf16[2048,128]{1,0:T(8,128)(2,1)S(1)}) custom-call(s32[2]{0:T(128)S(1)} %pad_add_fusion.flag, bf16[3,128,128]{2,1,0:T(8,128)(2,1)S(1)} %copy-done.20, bf16[2048,128]{1,0:T(8,128)(2,1)S(1)} %bitcast.129, bf16[2048,128]{1,0:T(8,128)(2,1)} %copy-done.7, ...), custom_call_target="tpu_custom_call" | custom-call | flops 1157627904 | bytes 5000000 | tf_op jit(solution)/shard_map/pallas_call | solution.py:65
  350.6 18.2 %all_to_all.94.pieces = bf16[16,128,128]{2,1,0:T(8,128)(2,1)S(1)} all-to-all(bf16[16,128,128]{2,1,0:T(8,128)(2,1)S(1)} %bitcast.161), channel_id=1, replica_groups=mesh['s'=2,'y'=4,'z'=4,'x'=2,'c'=2] {'y','z'}, dimensions={0} | all-to-all | bytes 1048576 | tf_op jit(solution)/shard_map/all_to_all | solution.py:41
  371.6 10.6 %all_to_all.95.pieces = bf16[4,32,1536]{2,1,0:T(8,128)(2,1)S(1)} all-to-all(bf16[4,32,1536]{2,1,0:T(8,128)(2,1)S(1)} %get-tuple-element.160), channel_id=1, replica_groups=mesh['s'=2,'y'=4,'z'=4,'x'=2,'c'=2] {'x','c'}, dimensions={0} | all-to-all | bytes 786432 | tf_op jit(solution)/shard_map/all_to_all | solution.py:41
  390.6 8.7 %all-to-all-done.13 = bf16[8,32,1536]{2,1,0:T(8,128)(2,1)S(1)} async-done(((bf16[8,32,1536]{2,1,0:T(8,128)(2,1)}), bf16[8,32,1536]{2,1,0:T(8,128)(2,1)S(1)}, u32[]{:S(2)}, u32[]{:S(2)}) %all-to-all-start.13) | async-done | bytes 786464 | tf_op jit(solution)/shard_map/all_to_all | solution.py:41
  399.3 8.5 %shard_map.239 = (bf16[256,1536]{1,0:T(8,128)(2,1)}, bf16[256,1792]{1,0:T(8,128)(2,1)}, bf16[256,1792]{1,0:T(8,128)(2,1)}) custom-call(bf16[256,1536]{1,0:T(8,128)(2,1)S(1)} %bitcast.135, bf16[1536,1792]{1,0:T(8,128)(2,1)} %all-gather.4.cloned.1.call-done.own, bf16[1536,1792]{1,0:T(8,128)(2,1)} %collective-permute-done.16.other, ...), custom_call_target="tpu_custom_call" | custom-call | flops 3019898880 | bytes 17000000 | tf_op jit(solution)/shard_map/pallas_call | solution.py:65
  416.8 8.3 %shard_map.240 = bf16[1536,1792]{1,0:T(8,128)(2,1)} custom-call(bf16[256,1536]{1,0:T(8,128)(2,1)S(1)} %bitcast.134, bf16[256,1536]{1,0:T(8,128)(2,1)S(1)} %copy-done.28, bf16[256,1536]{1,0:T(8,128)(2,1)} %bitcast.137, bf16[256,1536]{1,0:T(8,128)(2,1)} %collective-permute-done.24.grads_other, bf16[256,1792]{1,0:T(8,128)(2,1)} %get-tuple-element.169.own, ...), custom_call_target="tpu_custom_call" | custom-call | flops 3019898880 | bytes 12000000 | tf_op jit(solution)/shard_map/pallas_call | solution.py:65
  442.1 7.1 %shard_map.242 = (bf16[128,384]{1,0:T(8,128)(2,1)S(1)}, f32[2048,128]{1,0:T(8,128)}, bf16[2048,128]{1,0:T(8,128)(2,1)S(1)}) custom-call(s32[2]{0:T(128)S(1)} %pad_add_fusion.flag, bf16[3,128,128]{2,1,0:T(8,128)(2,1)S(1)} %copy-done.24, bf16[2048,128]{1,0:T(8,128)(2,1)S(1)} %bitcast.141, bf16[2048,128]{1,0:T(8,128)(2,1)} %copy-done.15, ...), custom_call_target="tpu_custom_call" | custom-call | flops 1157627904 | bytes 5000000 | tf_op jit(solution)/shard_map/pallas_call | solution.py:65
  453.3 19.1 %all_to_all.96.pieces = bf16[16,128,128]{2,1,0:T(8,128)(2,1)S(1)} all-to-all(bf16[16,128,128]{2,1,0:T(8,128)(2,1)S(1)} %bitcast.162), channel_id=1, replica_groups=mesh['s'=2,'y'=4,'z'=4,'x'=2,'c'=2] {'y','z'}, dimensions={0} | all-to-all | bytes 1048576 | tf_op jit(solution)/shard_map/all_to_all | solution.py:41
  494.2 12.0 %reduce-scatter.9.cloned.1.call-done = bf16[384,1792]{1,0:T(8,128)(2,1)} async-done(((bf16[1536,1792]{1,0:T(8,128)(2,1)}), bf16[384,1792]{1,0:T(8,128)(2,1)}) %reduce-scatter.9.cloned.1.call-update) | async-done | bytes 1376272 | tf_op jit(solution)/shard_map/reduce_scatter | solution.py:809
  543.1 8.0 %all-to-all-done.17.pieces = bf16[8,96,1792]{2,1,0:T(8,128)(2,1)} async-done(((bf16[8,96,1792]{2,1,0:T(8,128)(2,1)}), bf16[8,96,1792]{2,1,0:T(8,128)(2,1)}, u32[]{:S(2)}, u32[]{:S(2)}) %all-to-all-start.17) | async-done | bytes 2752544 | tf_op jit(solution)/shard_map/all_to_all | solution.py:41
  (369 shorter events, 277.7 us)
Async XLA Ops:
  26.2 40.0 %all-to-all-start.1 = ((bf16[8,96,1792]{2,1,0:T(8,128)(2,1)}), bf16[8,96,1792]{2,1,0:T(8,128)(2,1)}, u32[]{:S(2)}, u32[]{:S(2)}) async-start(bf16[8,96,1792]{2,1,0:T(8,128)(2,1)} %shard_map.220), calls=%async_computation.1 | async-start | bytes 5505024 | tf_op jit(solution)/shard_map/all_to_all | solution.py:41
  33.0 111.1 %all-gather.4.cloned.1.call-start = ((), (), s32[]{:S(2)}) async-start(), calls=%async_computation.22 | async-start | bytes 6881280 | tf_op jit(solution)/shard_map/all_gather | solution.py:702
  75.8 23.8 %collective-permute-start.10 = (bf16[4,112,512]{2,1,0:T(8,128)(2,1)S(1)}, bf16[4,112,512]{2,1,0:T(8,128)(2,1)S(1)}, u32[]{:S(2)}, u32[]{:S(2)}) collective-permute-start(bf16[4,112,512]{2,1,0:T(8,128)(2,1)S(1)} %pad_maximum_fusion.1.refs_0_), channel_id=1, source_target_pairs={{0,8},{4,12},{8,0},{12,4},{1,9},{5,13},{9,1},{13,5},{2,10},{6,14},... | collective-permute-start | bytes 1376264 | tf_op jit(solution)/shard_map/ppermute | solution.py:447
  89.5 16.9 %collective-permute-start.12 = (bf16[4,96,384]{2,1,0:T(8,128)(2,1)S(1)}, bf16[4,96,384]{2,1,0:T(8,128)(2,1)S(1)}, u32[]{:S(2)}, u32[]{:S(2)}) collective-permute-start(bf16[4,96,384]{2,1,0:T(8,128)(2,1)S(1)} %pad_maximum_fusion.3.refs_0_), channel_id=1, source_target_pairs={{0,4},{4,8},{8,12},{12,0},{1,5},{5,9},{9,13},{13,1},{2,6},{6,10},{... | collective-permute-start | bytes 884744 | tf_op jit(solution)/shard_map/ppermute | solution.py:447
  89.5 22.1 %collective-permute-start.13 = (bf16[4,96,384]{2,1,0:T(8,128)(2,1)S(1)}, bf16[4,96,384]{2,1,0:T(8,128)(2,1)S(1)}, u32[]{:S(2)}, u32[]{:S(2)}) collective-permute-start(bf16[4,96,384]{2,1,0:T(8,128)(2,1)S(1)} %pad_maximum_fusion.3.refs_0_), channel_id=1, source_target_pairs={{0,8},{4,12},{8,0},{12,4},{1,9},{5,13},{9,1},{13,5},{2,10},{6,14},... | collective-permute-start | bytes 884744 | tf_op jit(solution)/shard_map/ppermute | solution.py:447
  111.5 20.6 %all-to-all-start.2 = ((bf16[16,128,128]{2,1,0:T(8,128)(2,1)}), bf16[16,128,128]{2,1,0:T(8,128)(2,1)S(1)}, u32[]{:S(2)}, u32[]{:S(2)}) async-start(bf16[16,128,128]{2,1,0:T(8,128)(2,1)} %get-tuple-element.125), calls=%async_computation.2 | async-start | bytes 1048576 | tf_op jit(solution)/shard_map/all_to_all | solution.py:41
  117.9 97.7 %all-gather.6.cloned.1.call-start = ((), (), s32[]{:S(2)}) async-start(), calls=%async_computation.23 | async-start | bytes 2924544 | tf_op jit(solution)/shard_map/all_gather | solution.py:702
  148.1 125.1 %all-gather.8.cloned.1.call-start = ((), (), s32[]{:S(2)}) async-start(), calls=%async_computation.24 | async-start | bytes 6881280 | tf_op jit(solution)/shard_map/all_gather | solution.py:702
  273.2 17.2 %collective-permute-start.18 = (bf16[1536,1792]{1,0:T(8,128)(2,1)}, bf16[1536,1792]{1,0:T(8,128)(2,1)S(1)}, u32[]{:S(2)}, u32[]{:S(2)}) collective-permute-start(bf16[1536,1792]{1,0:T(8,128)(2,1)} %all-gather.8.cloned.1.call-done.own), channel_id=1, source_target_pairs={{0,1},{1,0},{2,3},{3,2},{4,5},{5,4},{6,7},{7,6},{8,9},{9,8},{10,11... | collective-permute-start | bytes 16515080 | tf_op jit(solution)/shard_map/ppermute | solution.py:37
  303.6 23.9 %all-to-all-start.10 = ((bf16[8,64,1536]{2,1,0:T(8,128)(2,1)}), bf16[8,64,1536]{2,1,0:T(8,128)(2,1)S(1)}, u32[]{:S(2)}, u32[]{:S(2)}) async-start(bf16[8,64,1536]{2,1,0:T(8,128)(2,1)} %get-tuple-element.151), calls=%async_computation.10 | async-start | bytes 3145728 | tf_op jit(solution)/shard_map/all_to_all | solution.py:41
  307.2 92.0 %reduce-scatter.5.cloned.1.call-start = ((), (), s32[]{:S(2)}) async-start(), calls=%async_computation.25 | async-start | bytes 6881280 | tf_op jit(solution)/shard_map/reduce_scatter | solution.py:809
  383.3 16.0 %all-to-all-start.13 = ((bf16[8,32,1536]{2,1,0:T(8,128)(2,1)}), bf16[8,32,1536]{2,1,0:T(8,128)(2,1)S(1)}, u32[]{:S(2)}, u32[]{:S(2)}) async-start(bf16[8,32,1536]{2,1,0:T(8,128)(2,1)} %get-tuple-element.162), calls=%async_computation.13 | async-start | bytes 1572864 | tf_op jit(solution)/shard_map/all_to_all | solution.py:41
  387.5 53.5 %reduce-scatter.7.cloned.1.call-start = ((), (), s32[]{:S(2)}) async-start(), calls=%async_computation.26 | async-start | bytes 3440640 | tf_op jit(solution)/shard_map/reduce_scatter | solution.py:836
  410.5 21.3 %all-to-all-start.14 = ((bf16[8,32,1536]{2,1,0:T(8,128)(2,1)}), bf16[8,32,1536]{2,1,0:T(8,128)(2,1)}, u32[]{:S(2)}, u32[]{:S(2)}) async-start(bf16[8,32,1536]{2,1,0:T(8,128)(2,1)} %bitcast.49), calls=%async_computation.14 | async-start | bytes 1572864 | tf_op jit(solution)/shard_map/all_to_all | solution.py:41
  414.7 91.5 %reduce-scatter.9.cloned.1.call-start = ((), (), s32[]{:S(2)}) async-start(), calls=%async_computation.27 | async-start | bytes 6881280 | tf_op jit(solution)/shard_map/reduce_scatter | solution.py:809
  483.0 26.7 %collective-permute-start.27 = (bf16[4,112,512]{2,1,0:T(8,128)(2,1)}, bf16[4,112,512]{2,1,0:T(8,128)(2,1)S(1)}, u32[]{:S(2)}, u32[]{:S(2)}) collective-permute-start(bf16[4,112,512]{2,1,0:T(8,128)(2,1)} %get-tuple-element.188), channel_id=1, source_target_pairs={{0,4},{4,8},{8,12},{12,0},{1,5},{5,9},{9,13},{13,1},{2,6},{6,10},{... | collective-permute-start | bytes 1376264 | tf_op jit(solution)/shard_map/ppermute | solution.py:447
  483.3 26.4 %collective-permute-start.28 = (bf16[4,112,512]{2,1,0:T(8,128)(2,1)}, bf16[4,112,512]{2,1,0:T(8,128)(2,1)S(1)}, u32[]{:S(2)}, u32[]{:S(2)}) collective-permute-start(bf16[4,112,512]{2,1,0:T(8,128)(2,1)} %get-tuple-element.189), channel_id=1, source_target_pairs={{0,8},{4,12},{8,0},{12,4},{1,9},{5,13},{9,1},{13,5},{2,10},{6,14},... | collective-permute-start | bytes 1376264 | tf_op jit(solution)/shard_map/ppermute | solution.py:447
  486.9 22.9 %collective-permute-start.29 = (bf16[4,112,512]{2,1,0:T(8,128)(2,1)}, bf16[4,112,512]{2,1,0:T(8,128)(2,1)S(1)}, u32[]{:S(2)}, u32[]{:S(2)}) collective-permute-start(bf16[4,112,512]{2,1,0:T(8,128)(2,1)} %get-tuple-element.190), channel_id=1, source_target_pairs={{0,12},{4,0},{8,4},{12,8},{1,13},{5,1},{9,5},{13,9},{2,14},{6,2},{... | collective-permute-start | bytes 1376264 | tf_op jit(solution)/shard_map/ppermute | solution.py:447
  488.4 22.1 %all-to-all-start.16 = ((bf16[4,32,1536]{2,1,0:T(8,128)(2,1)}), bf16[4,32,1536]{2,1,0:T(8,128)(2,1)S(1)}, u32[]{:S(2)}, u32[]{:S(2)}) async-start(bf16[4,32,1536]{2,1,0:T(8,128)(2,1)} %get-tuple-element.195), calls=%async_computation.16 | async-start | bytes 786432 | tf_op jit(solution)/shard_map/all_to_all | solution.py:41
  511.3 39.8 %all-to-all-start.17 = ((bf16[8,96,1792]{2,1,0:T(8,128)(2,1)}), bf16[8,96,1792]{2,1,0:T(8,128)(2,1)}, u32[]{:S(2)}, u32[]{:S(2)}) async-start(bf16[8,96,1792]{2,1,0:T(8,128)(2,1)} %bitcast.159), calls=%async_computation.20 | async-start | bytes 5505024 | tf_op jit(solution)/shard_map/all_to_all | solution.py:41
  517.9 39.3 %reduce-scatter.11.cloned.1.call-start = ((), (), s32[]{:S(2)}) async-start(), calls=%async_computation.28 | async-start | bytes 860160 | tf_op jit(solution)/shard_map/reduce_scatter | solution.py:850
  520.8 15.9 %collective-permute-start.36 = (bf16[4,96,384]{2,1,0:T(8,128)(2,1)S(1)}, bf16[4,96,384]{2,1,0:T(8,128)(2,1)}, u32[]{:S(2)}, u32[]{:S(2)}) collective-permute-start(bf16[4,96,384]{2,1,0:T(8,128)(2,1)S(1)} %copy-done.32), channel_id=1, source_target_pairs={{0,48},{16,0},{32,16},{48,32},{1,49},{17,1},{33,17},{49,33},{2,50}... | collective-permute-start | bytes 884744 | tf_op jit(solution)/shard_map/ppermute | solution.py:447
  526.2 24.9 %collective-permute-start.32 = (bf16[112,512]{1,0:T(8,128)(2,1)S(1)}, bf16[112,512]{1,0:T(8,128)(2,1)S(1)}, u32[]{:S(2)}, u32[]{:S(2)}) collective-permute-start(bf16[112,512]{1,0:T(8,128)(2,1)S(1)} %get-tuple-element.272), channel_id=1, source_target_pairs={{0,32},{16,48},{32,0},{48,16},{1,33},{17,49},{33,1},{49,17},{2,34}... | collective-permute-start | bytes 344072 | tf_op jit(solution)/shard_map/ppermute | solution.py:447
  529.0 22.1 %collective-permute-start.33 = (bf16[112,512]{1,0:T(8,128)(2,1)S(1)}, bf16[112,512]{1,0:T(8,128)(2,1)S(1)}, u32[]{:S(2)}, u32[]{:S(2)}) collective-permute-start(bf16[112,512]{1,0:T(8,128)(2,1)S(1)} %get-tuple-element.271), channel_id=1, source_target_pairs={{0,48},{16,0},{32,16},{48,32},{1,49},{17,1},{33,17},{49,33},{2,50}... | collective-permute-start | bytes 344072 | tf_op jit(solution)/shard_map/ppermute | solution.py:447
  (93 other events, 879.5 us)
Sparse Core Ops, SparseCore 0:
  69.8 64.2 all-gather.3
  327.7 60.3 reduce-scatter.4
  524.9 24.9 reduce-scatter.10
Sparse Core Ops, SparseCore 1:
  144.4 49.9 all-gather.5
  195.9 62.1 all-gather.7
  399.4 41.6 reduce-scatter.6
  443.6 62.6 reduce-scatter.8

commit v6 on v5

--- a/solution.py
+++ b/solution.py
@@ -485,7 +485,7 @@
     scratch[:, pl.ds(0, 512)] = tn(normed[...], grad_qkv[...]).astype(BF)
     scratch[:, pl.ds(512, QCOLS)] = tn(grad_att[...], attended[...]).astype(BF)
     for b in range(16):
-        out[b % 4, b // 4] = scratch[pl.ds(b * 96, 96), :]
+        out[b // 4, b % 4] = scratch[pl.ds(b * 96, 96), :]
 
 
 def weight_grad(*args):
@@ -715,9 +715,10 @@
     payload = jnp.concatenate(
         [kv_blocks, jnp.broadcast_to(small[None, None], (4, 1, HEAD)), jnp.zeros((4, 7, HEAD), BF)], axis=1
     )
-    payload = exchange(jnp.concatenate([payload, payload], axis=0), ("s", "x", "c")).reshape(2, 4, 32, HEAD)
     bias_rows = jnp.pad(b_query, ((0, 15), (0, QCOLS)))
     own = jnp.concatenate([jnp.concatenate([w_query[0], w_out[0].T], axis=1), bias_rows], axis=0)
+    payload = after(payload, own)
+    payload = exchange(jnp.concatenate([payload, payload], axis=0), ("s", "x", "c")).reshape(2, 4, 32, HEAD)
     other = swap(own, "s")
 
     def attention_rows(layer, matrices):
@@ -768,9 +769,9 @@
     normed1, query1, kv = qkv_columns(flag, x_block1, gain_a1, qkv_first, bias1, cosine, sine)
     own1 = gathered(ffn_halves[0], "y")
     all_second = gathered(after(rows_second, kv), ("y", "z"))
-    kv, out_ring = lax.optimization_barrier((kv, out_ring))
+    kv_mine1 = exchange(after(kv, (out_ring[1], out_ring[3])), ("y", "z")).reshape(SEQ, HEAD)
+    kv_mine1, out_ring = lax.optimization_barrier((kv_mine1, out_ring))
     out_first = assemble(y_then_z, out_ring)
-    kv_mine1 = exchange(kv, ("y", "z")).reshape(SEQ, HEAD)
     kv_other1 = swap(kv_mine1, "c")
     attended1, wide1, lse1, part = attend(flag, query1, kv_mine1, kv_other1, seg_col, seg_row, out_first, 0)
     other1 = swap(after(own1, part), "c")
@@ -833,7 +834,7 @@
     small_two, attn_two = attn_two
     grad_low = after(grad_low, attn_two)
     attn_two = after(attn_two, (ffn_two, grad_low))
-    attn_two = lax.psum_scatter(attn_two.reshape(16 * 96, 896), "z", scatter_dimension=0, tiled=True)
+    attn_two = lax.psum_scatter(attn_two.reshape(16 * 96, 896), "y", scatter_dimension=0, tiled=True)
     fed1 = feed_back(grad_low, own1, other1, gate_up1)
     grad_one, _, ffn_one, parts, _ = backward(
         grad_two, grad_low, fed1, second1, mixed1, gain_b1, xin, x_block1, gain_a1, normed1, query1, attended1, wide1,
@@ -847,7 +848,7 @@
     qkv_one = scatter_blocks(halfway, "y", ffn_sum)
     out_one_grad = scatter_blocks(summed(out_parts), "z", ffn_sum)
     attn_one = jnp.concatenate([qkv_one, jnp.pad(out_one_grad, ((0, 16), (0, 0)))], axis=1)
-    attn_two = lax.psum_scatter(after(attn_two, (ffn_one, grad_one, halfway)), "y", scatter_dimension=0, tiled=True)
+    attn_two = lax.psum_scatter(after(attn_two, (ffn_one, grad_one, halfway)), "z", scatter_dimension=0, tiled=True)
 
     grad_gate, grad_up, grad_down = unpack(ffn_sum)
     given = swap(jnp.concatenate([pick(attn_two, attn_one[:96]), attn_one[96:]], axis=0), "s").astype(F32)

time: 589 us -> 581 us (0.986)
  waiting for transfers between devices: 139 us -> 128 us
    all_to_all x11, waiting for transfers between devices: 81.3 us -> 73.6 us  [exchange(): return lax.all_to_all(value, axes, split_axis=0, concat_axis=0, tiled=True)]
    unnamed x114 -> x118, local copies, waits for them, and re-layouts: 21.7 us -> 21.8 us
  transfers between devices with their start and end apart: 62 -> 62, of which waited for: 30 -> 29; matrix products, arithmetic and copies ran while one was open for 4% -> 4% of each run, Pallas kernels for 16% -> 16%
where the time goes in v6:
time: 581 us; the launch traced here: 573 us
  blocking collectives  149 us (26%)
  waiting for transfers between devices  128 us (22%)
  starting transfers between devices  125 us (22%)
  Pallas kernels  106 us (18%)
  local copies, waits for them, and re-layouts  30.9 us (5%)
  other arithmetic  17.6 us (3%)
  between operations  16.8 us (3%)
    all_to_all x7, blocking collectives, exchange(): return lax.all_to_all(value, axes, split_axis=0, concat_axis=0, tiled=True)  124 us
    pallas_call x28, Pallas kernels, call(): pl.pallas_call(kernel, out_shape=out_shape, in_specs=in_specs, scratch_sh...  106 us
    all_to_all x11, waiting for transfers between devices, exchange(): return lax.all_to_all(value, axes, split_axis=0, concat_axis=0, tiled=True)  73.6 us
    all_to_all x11, starting transfers between devices, exchange(): return lax.all_to_all(value, axes, split_axis=0, concat_axis=0, tiled=True)  54.9 us
    ppermute x24, starting transfers between devices, shifted(): return lax.ppermute(value, axis, [(i, (i + steps) % 4) for i in range(4)])  40 us
    ppermute x24, waiting for transfers between devices, shifted(): return lax.ppermute(value, axis, [(i, (i + steps) % 4) for i in range(4)])  32.2 us
    ppermute x17, starting transfers between devices, swap(): return lax.ppermute(value, axis, [(0, 1), (1, 0)])  25 us
    all_gather x3, blocking collectives, gathered(): return lax.all_gather(piece, axes, axis=0, tiled=True)  24.8 us
  transfers between devices with their start and end apart: 62, of which 29 were waited for; matrix products, arithmetic and copies ran while one was open for 4% of the time, Pallas kernels for 16%

profile of v6, /device:TPU:1, one launch (start us, length us, event | category | flops | bytes accessed | tf_op | source)
XLA Modules:
  0.0 573.2 jit_solution(12549355371949391887)
XLA Ops:
  25.4 7.7 %all-to-all-start.1 = ((bf16[8,96,1792]{2,1,0:T(8,128)(2,1)}), bf16[8,96,1792]{2,1,0:T(8,128)(2,1)}, u32[]{:S(2)}, u32[]{:S(2)}) async-start(bf16[8,96,1792]{2,1,0:T(8,128)(2,1)} %shard_map.220), calls=%async_computation.1 | async-start | bytes 5505024 | tf_op jit(solution)/shard_map/all_to_all | solution.py:41
  47.1 19.3 %all-to-all-done.1.pieces = bf16[8,96,1792]{2,1,0:T(8,128)(2,1)} async-done(((bf16[8,96,1792]{2,1,0:T(8,128)(2,1)}), bf16[8,96,1792]{2,1,0:T(8,128)(2,1)}, u32[]{:S(2)}, u32[]{:S(2)}) %all-to-all-start.1) | async-done | bytes 2752544 | tf_op jit(solution)/shard_map/all_to_all | solution.py:41
  78.8 7.2 %collective-permute-done.11.refs_3_ = bf16[4,112,512]{2,1,0:T(8,128)(2,1)S(1)} collective-permute-done((bf16[4,112,512]{2,1,0:T(8,128)(2,1)S(1)}, bf16[4,112,512]{2,1,0:T(8,128)(2,1)S(1)}, u32[]{:S(2)}, u32[]{:S(2)}) %collective-permute-start.11) | collective-permute-done | bytes 458784 | tf_op jit(solution)/shard_map/ppermute | solution.py:447
  89.5 8.3 %collective-permute-start.13 = (bf16[4,96,384]{2,1,0:T(8,128)(2,1)S(1)}, bf16[4,96,384]{2,1,0:T(8,128)(2,1)S(1)}, u32[]{:S(2)}, u32[]{:S(2)}) collective-permute-start(bf16[4,96,384]{2,1,0:T(8,128)(2,1)S(1)} %pad_maximum_fusion.3.refs_0_), channel_id=1, source_target_pairs={{0,12},{4,0},{8,4},{12,8},{1,13},{5,1},{9,5},{13,9},{2,14},{6,2},{... | collective-permute-start | bytes 884744 | tf_op jit(solution)/shard_map/ppermute | solution.py:447
  149.3 27.6 %all_to_all.90 = bf16[8,32,1536]{2,1,0:T(8,128)(2,1)S(1)} all-to-all(bf16[8,32,1536]{2,1,0:T(8,128)(2,1)S(1)} %get-tuple-element.138), channel_id=1, replica_groups=mesh['s'=2,'y'=4,'z'=4,'x'=2,'c'=2] {'z','x'}, dimensions={0} | all-to-all | bytes 1572864 | tf_op jit(solution)/shard_map/all_to_all | solution.py:41
  176.9 7.3 %shard_map.227 = (bf16[256,1536]{1,0:T(8,128)(2,1)}, bf16[2,256,1152]{2,1,0:T(8,128)(2,1)}) custom-call(bf16[256,1536]{1,0:T(8,128)(2,1)S(1)} %bitcast.132, bf16[1536,1792]{1,0:T(8,128)(2,1)} %all-gather.4.cloned.1.call-done.own, bf16[1536,1792]{1,0:T(8,128)(2,1)} %collective-permute-done.16.other), custom_call_target="tpu_custom_call" | custom-call | flops 3019898880 | bytes 15000000 | tf_op jit(solution)/shard_map/pallas_call | solution.py:65
  190.5 9.6 %all-to-all-done.5.pieces = bf16[8,32,1536]{2,1,0:T(8,128)(2,1)S(1)} async-done(((bf16[8,32,1536]{2,1,0:T(8,128)(2,1)}), bf16[8,32,1536]{2,1,0:T(8,128)(2,1)S(1)}, u32[]{:S(2)}, u32[]{:S(2)}) %all-to-all-start.5) | async-done | bytes 786464 | tf_op jit(solution)/shard_map/all_to_all | solution.py:41
  200.2 10.0 %all_gather.19.xin = bf16[128,1536]{1,0:T(8,128)(2,1)S(1)} all-gather(bf16[32,1536]{1,0:T(8,128)(2,1)S(1)} %shard_map.228.xin), channel_id=1, replica_groups=mesh['s'=2,'y'=4,'z'=4,'x'=2,'c'=2] {'x','c'}, dimensions={0}, use_global_device_ids=true | all-gather | bytes 491520 | tf_op jit(solution)/shard_map/all_gather | solution.py:702
  212.7 17.3 %all_to_all.91 = bf16[16,128,128]{2,1,0:T(8,128)(2,1)S(1)} all-to-all(bf16[16,128,128]{2,1,0:T(8,128)(2,1)S(1)} %get-tuple-element.145), channel_id=1, replica_groups=mesh['s'=2,'y'=4,'z'=4,'x'=2,'c'=2] {'y','z'}, dimensions={0} | all-to-all | bytes 1048576 | tf_op jit(solution)/shard_map/all_to_all | solution.py:41
  251.4 16.1 %all_to_all.92 = bf16[8,32,1536]{2,1,0:T(8,128)(2,1)S(1)} all-to-all(bf16[8,32,1536]{2,1,0:T(8,128)(2,1)S(1)} %get-tuple-element.149), channel_id=1, replica_groups=mesh['s'=2,'y'=4,'z'=4,'x'=2,'c'=2] {'z','x'}, dimensions={0} | all-to-all | bytes 1572864 | tf_op jit(solution)/shard_map/all_to_all | solution.py:41
  269.5 15.2 %all_to_all.93 = bf16[8,32,1536]{2,1,0:T(8,128)(2,1)S(1)} all-to-all(bf16[8,32,1536]{2,1,0:T(8,128)(2,1)S(1)} %broadcast_in_dim.71), channel_id=1, replica_groups=mesh['s'=2,'y'=4,'z'=4,'x'=2,'c'=2] {'z','x'}, dimensions={0} | all-to-all | bytes 1572864 | tf_op jit(solution)/shard_map/all_to_all | solution.py:41
  287.1 10.8 %shard_map.232 = (bf16[8,64,1536]{2,1,0:T(8,128)(2,1)}, bf16[256,1792]{1,0:T(8,128)(2,1)}, bf16[256,1792]{1,0:T(8,128)(2,1)}) custom-call(bf16[256,1536]{1,0:T(8,128)(2,1)S(1)} %bitcast.147, bf16[256,1536]{1,0:T(8,128)(2,1)S(1)} %bitcast.150, bf16[1536,1792]{1,0:T(8,128)(2,1)} %all-gather.8.cloned.1.call-done.own, bf16[1536,1792]{1,0:T(8,128)(2,1)} %copy-done.54), custom_call_target="tpu_custom_call" | custom-call | flops 6039797760 | bytes 17000000 | tf_op jit(solution)/shard_map/pallas_call | solution.py:65
  309.6 8.2 %shard_map.233 = bf16[1536,1792]{1,0:T(8,128)(2,1)} custom-call(bf16[256,1536]{1,0:T(8,128)(2,1)S(1)} %bitcast.149, bf16[256,1536]{1,0:T(8,128)(2,1)S(1)} %collective-permute-done.19.tokens_other, bf16[256,1536]{1,0:T(8,128)(2,1)} %bitcast.152, bf16[256,1536]{1,0:T(8,128)(2,1)} %copy-done.56, bf16[256,1792]{1,0:T(8,128)(2,1)} %get-tuple-element.156.own, ...), custom_call_target="tpu_custom_call" | custom-call | flops 3019898880 | bytes 12000000 | tf_op jit(solution)/shard_map/pallas_call | solution.py:65
  324.7 7.9 %all_gather.22.grad_att = bf16[128,1536]{1,0:T(8,128)(2,1)S(1)} all-gather(bf16[32,1536]{1,0:T(8,128)(2,1)S(1)} %get-tuple-element.160), channel_id=1, replica_groups=mesh['s'=2,'y'=4,'z'=4,'x'=2,'c'=2] {'x','c'}, dimensions={0}, use_global_device_ids=true | all-gather | bytes 491520 | tf_op jit(solution)/shard_map/all_gather | solution.py:702
  334.5 7.1 %shard_map.235 = (bf16[128,384]{1,0:T(8,128)(2,1)S(1)}, f32[2048,128]{1,0:T(8,128)}, bf16[2048,128]{1,0:T(8,128)(2,1)S(1)}) custom-call(s32[2]{0:T(128)S(1)} %pad_add_fusion.flag, bf16[3,128,128]{2,1,0:T(8,128)(2,1)S(1)} %copy-done.20, bf16[2048,128]{1,0:T(8,128)(2,1)S(1)} %bitcast.129, bf16[2048,128]{1,0:T(8,128)(2,1)} %copy-done.7, ...), custom_call_target="tpu_custom_call" | custom-call | flops 1157627904 | bytes 5000000 | tf_op jit(solution)/shard_map/pallas_call | solution.py:65
  345.0 18.2 %all_to_all.94.pieces = bf16[16,128,128]{2,1,0:T(8,128)(2,1)S(1)} all-to-all(bf16[16,128,128]{2,1,0:T(8,128)(2,1)S(1)} %bitcast.161), channel_id=1, replica_groups=mesh['s'=2,'y'=4,'z'=4,'x'=2,'c'=2] {'y','z'}, dimensions={0} | all-to-all | bytes 1048576 | tf_op jit(solution)/shard_map/all_to_all | solution.py:41
  365.9 10.5 %all_to_all.95.pieces = bf16[4,32,1536]{2,1,0:T(8,128)(2,1)S(1)} all-to-all(bf16[4,32,1536]{2,1,0:T(8,128)(2,1)S(1)} %get-tuple-element.164), channel_id=1, replica_groups=mesh['s'=2,'y'=4,'z'=4,'x'=2,'c'=2] {'x','c'}, dimensions={0} | all-to-all | bytes 786432 | tf_op jit(solution)/shard_map/all_to_all | solution.py:41
  384.9 8.7 %all-to-all-done.13 = bf16[8,32,1536]{2,1,0:T(8,128)(2,1)S(1)} async-done(((bf16[8,32,1536]{2,1,0:T(8,128)(2,1)}), bf16[8,32,1536]{2,1,0:T(8,128)(2,1)S(1)}, u32[]{:S(2)}, u32[]{:S(2)}) %all-to-all-start.13) | async-done | bytes 786464 | tf_op jit(solution)/shard_map/all_to_all | solution.py:41
  393.6 8.5 %shard_map.239 = (bf16[256,1536]{1,0:T(8,128)(2,1)}, bf16[256,1792]{1,0:T(8,128)(2,1)}, bf16[256,1792]{1,0:T(8,128)(2,1)}) custom-call(bf16[256,1536]{1,0:T(8,128)(2,1)S(1)} %bitcast.135, bf16[1536,1792]{1,0:T(8,128)(2,1)} %all-gather.4.cloned.1.call-done.own, bf16[1536,1792]{1,0:T(8,128)(2,1)} %collective-permute-done.16.other, ...), custom_call_target="tpu_custom_call" | custom-call | flops 3019898880 | bytes 17000000 | tf_op jit(solution)/shard_map/pallas_call | solution.py:65
  411.2 8.3 %shard_map.240 = bf16[1536,1792]{1,0:T(8,128)(2,1)} custom-call(bf16[256,1536]{1,0:T(8,128)(2,1)S(1)} %bitcast.134, bf16[256,1536]{1,0:T(8,128)(2,1)S(1)} %copy-done.28, bf16[256,1536]{1,0:T(8,128)(2,1)} %bitcast.137, bf16[256,1536]{1,0:T(8,128)(2,1)} %collective-permute-done.24.grads_other, bf16[256,1792]{1,0:T(8,128)(2,1)} %get-tuple-element.173.own, ...), custom_call_target="tpu_custom_call" | custom-call | flops 3019898880 | bytes 12000000 | tf_op jit(solution)/shard_map/pallas_call | solution.py:65
  431.6 7.1 %shard_map.242 = (bf16[128,384]{1,0:T(8,128)(2,1)S(1)}, f32[2048,128]{1,0:T(8,128)}, bf16[2048,128]{1,0:T(8,128)(2,1)S(1)}) custom-call(s32[2]{0:T(128)S(1)} %pad_add_fusion.flag, bf16[3,128,128]{2,1,0:T(8,128)(2,1)S(1)} %copy-done.24, bf16[2048,128]{1,0:T(8,128)(2,1)S(1)} %bitcast.141, bf16[2048,128]{1,0:T(8,128)(2,1)} %copy-done.15, ...), custom_call_target="tpu_custom_call" | custom-call | flops 1157627904 | bytes 5000000 | tf_op jit(solution)/shard_map/pallas_call | solution.py:65
  442.1 19.0 %all_to_all.96.pieces = bf16[16,128,128]{2,1,0:T(8,128)(2,1)S(1)} all-to-all(bf16[16,128,128]{2,1,0:T(8,128)(2,1)S(1)} %bitcast.162), channel_id=1, replica_groups=mesh['s'=2,'y'=4,'z'=4,'x'=2,'c'=2] {'y','z'}, dimensions={0} | all-to-all | bytes 1048576 | tf_op jit(solution)/shard_map/all_to_all | solution.py:41
  482.8 9.8 %reduce-scatter.9.cloned.1.call-done = bf16[384,1792]{1,0:T(8,128)(2,1)} async-done(((bf16[1536,1792]{1,0:T(8,128)(2,1)}), bf16[384,1792]{1,0:T(8,128)(2,1)}) %reduce-scatter.9.cloned.1.call-update) | async-done | bytes 1376272 | tf_op jit(solution)/shard_map/reduce_scatter | solution.py:810
  529.1 12.1 %all-to-all-done.17.pieces = bf16[8,96,1792]{2,1,0:T(8,128)(2,1)} async-done(((bf16[8,96,1792]{2,1,0:T(8,128)(2,1)}), bf16[8,96,1792]{2,1,0:T(8,128)(2,1)}, u32[]{:S(2)}, u32[]{:S(2)}) %all-to-all-start.17) | async-done | bytes 2752544 | tf_op jit(solution)/shard_map/all_to_all | solution.py:41
  (375 shorter events, 274.5 us)
Async XLA Ops:
  25.4 41.0 %all-to-all-start.1 = ((bf16[8,96,1792]{2,1,0:T(8,128)(2,1)}), bf16[8,96,1792]{2,1,0:T(8,128)(2,1)}, u32[]{:S(2)}, u32[]{:S(2)}) async-start(bf16[8,96,1792]{2,1,0:T(8,128)(2,1)} %shard_map.220), calls=%async_computation.1 | async-start | bytes 5505024 | tf_op jit(solution)/shard_map/all_to_all | solution.py:41
  33.1 105.5 %all-gather.4.cloned.1.call-start = ((), (), s32[]{:S(2)}) async-start(), calls=%async_computation.22 | async-start | bytes 6881280 | tf_op jit(solution)/shard_map/all_gather | solution.py:702
  75.8 21.9 %collective-permute-start.10 = (bf16[4,112,512]{2,1,0:T(8,128)(2,1)S(1)}, bf16[4,112,512]{2,1,0:T(8,128)(2,1)S(1)}, u32[]{:S(2)}, u32[]{:S(2)}) collective-permute-start(bf16[4,112,512]{2,1,0:T(8,128)(2,1)S(1)} %pad_maximum_fusion.1.refs_0_), channel_id=1, source_target_pairs={{0,8},{4,12},{8,0},{12,4},{1,9},{5,13},{9,1},{13,5},{2,10},{6,14},... | collective-permute-start | bytes 1376264 | tf_op jit(solution)/shard_map/ppermute | solution.py:447
  104.5 18.4 %all-to-all-start.2 = ((bf16[16,128,128]{2,1,0:T(8,128)(2,1)}), bf16[16,128,128]{2,1,0:T(8,128)(2,1)S(1)}, u32[]{:S(2)}, u32[]{:S(2)}) async-start(bf16[16,128,128]{2,1,0:T(8,128)(2,1)} %get-tuple-element.128), calls=%async_computation.2 | async-start | bytes 1048576 | tf_op jit(solution)/shard_map/all_to_all | solution.py:41
  109.9 100.3 %all-gather.6.cloned.1.call-start = ((), (), s32[]{:S(2)}) async-start(), calls=%async_computation.23 | async-start | bytes 2924544 | tf_op jit(solution)/shard_map/all_gather | solution.py:702
  142.5 125.0 %all-gather.8.cloned.1.call-start = ((), (), s32[]{:S(2)}) async-start(), calls=%async_computation.24 | async-start | bytes 6881280 | tf_op jit(solution)/shard_map/all_gather | solution.py:702
  267.5 17.2 %collective-permute-start.18 = (bf16[1536,1792]{1,0:T(8,128)(2,1)}, bf16[1536,1792]{1,0:T(8,128)(2,1)S(1)}, u32[]{:S(2)}, u32[]{:S(2)}) collective-permute-start(bf16[1536,1792]{1,0:T(8,128)(2,1)} %all-gather.8.cloned.1.call-done.own), channel_id=1, source_target_pairs={{0,1},{1,0},{2,3},{3,2},{4,5},{5,4},{6,7},{7,6},{8,9},{9,8},{10,11... | collective-permute-start | bytes 16515080 | tf_op jit(solution)/shard_map/ppermute | solution.py:37
  297.9 23.9 %all-to-all-start.10 = ((bf16[8,64,1536]{2,1,0:T(8,128)(2,1)}), bf16[8,64,1536]{2,1,0:T(8,128)(2,1)S(1)}, u32[]{:S(2)}, u32[]{:S(2)}) async-start(bf16[8,64,1536]{2,1,0:T(8,128)(2,1)} %get-tuple-element.155), calls=%async_computation.10 | async-start | bytes 3145728 | tf_op jit(solution)/shard_map/all_to_all | solution.py:41
  301.5 92.1 %reduce-scatter.5.cloned.1.call-start = ((), (), s32[]{:S(2)}) async-start(), calls=%async_computation.25 | async-start | bytes 6881280 | tf_op jit(solution)/shard_map/reduce_scatter | solution.py:810
  377.6 16.0 %all-to-all-start.13 = ((bf16[8,32,1536]{2,1,0:T(8,128)(2,1)}), bf16[8,32,1536]{2,1,0:T(8,128)(2,1)S(1)}, u32[]{:S(2)}, u32[]{:S(2)}) async-start(bf16[8,32,1536]{2,1,0:T(8,128)(2,1)} %get-tuple-element.166), calls=%async_computation.13 | async-start | bytes 1572864 | tf_op jit(solution)/shard_map/all_to_all | solution.py:41
  381.9 48.5 %reduce-scatter.7.cloned.1.call-start = ((), (), s32[]{:S(2)}) async-start(), calls=%async_computation.26 | async-start | bytes 3440640 | tf_op jit(solution)/shard_map/reduce_scatter | solution.py:837
  404.8 17.3 %all-to-all-start.14 = ((bf16[8,32,1536]{2,1,0:T(8,128)(2,1)}), bf16[8,32,1536]{2,1,0:T(8,128)(2,1)}, u32[]{:S(2)}, u32[]{:S(2)}) async-start(bf16[8,32,1536]{2,1,0:T(8,128)(2,1)} %bitcast.49), calls=%async_computation.14 | async-start | bytes 1572864 | tf_op jit(solution)/shard_map/all_to_all | solution.py:41
  409.1 83.5 %reduce-scatter.9.cloned.1.call-start = ((), (), s32[]{:S(2)}) async-start(), calls=%async_computation.27 | async-start | bytes 6881280 | tf_op jit(solution)/shard_map/reduce_scatter | solution.py:810
  471.8 24.2 %collective-permute-start.27 = (bf16[4,112,512]{2,1,0:T(8,128)(2,1)}, bf16[4,112,512]{2,1,0:T(8,128)(2,1)S(1)}, u32[]{:S(2)}, u32[]{:S(2)}) collective-permute-start(bf16[4,112,512]{2,1,0:T(8,128)(2,1)} %get-tuple-element.192), channel_id=1, source_target_pairs={{0,4},{4,8},{8,12},{12,0},{1,5},{5,9},{9,13},{13,1},{2,6},{6,10},{... | collective-permute-start | bytes 1376264 | tf_op jit(solution)/shard_map/ppermute | solution.py:447
  472.1 24.0 %collective-permute-start.28 = (bf16[4,112,512]{2,1,0:T(8,128)(2,1)}, bf16[4,112,512]{2,1,0:T(8,128)(2,1)S(1)}, u32[]{:S(2)}, u32[]{:S(2)}) collective-permute-start(bf16[4,112,512]{2,1,0:T(8,128)(2,1)} %get-tuple-element.193), channel_id=1, source_target_pairs={{0,8},{4,12},{8,0},{12,4},{1,9},{5,13},{9,1},{13,5},{2,10},{6,14},... | collective-permute-start | bytes 1376264 | tf_op jit(solution)/shard_map/ppermute | solution.py:447
  476.0 20.1 %collective-permute-start.29 = (bf16[4,112,512]{2,1,0:T(8,128)(2,1)}, bf16[4,112,512]{2,1,0:T(8,128)(2,1)S(1)}, u32[]{:S(2)}, u32[]{:S(2)}) collective-permute-start(bf16[4,112,512]{2,1,0:T(8,128)(2,1)} %get-tuple-element.194), channel_id=1, source_target_pairs={{0,12},{4,0},{8,4},{12,8},{1,13},{5,1},{9,5},{13,9},{2,14},{6,2},{... | collective-permute-start | bytes 1376264 | tf_op jit(solution)/shard_map/ppermute | solution.py:447
  477.2 19.6 %all-to-all-start.16 = ((bf16[4,32,1536]{2,1,0:T(8,128)(2,1)}), bf16[4,32,1536]{2,1,0:T(8,128)(2,1)S(1)}, u32[]{:S(2)}, u32[]{:S(2)}) async-start(bf16[4,32,1536]{2,1,0:T(8,128)(2,1)} %get-tuple-element.199), calls=%async_computation.16 | async-start | bytes 786432 | tf_op jit(solution)/shard_map/all_to_all | solution.py:41
  497.6 43.5 %all-to-all-start.17 = ((bf16[8,96,1792]{2,1,0:T(8,128)(2,1)}), bf16[8,96,1792]{2,1,0:T(8,128)(2,1)}, u32[]{:S(2)}, u32[]{:S(2)}) async-start(bf16[8,96,1792]{2,1,0:T(8,128)(2,1)} %bitcast.159), calls=%async_computation.20 | async-start | bytes 5505024 | tf_op jit(solution)/shard_map/all_to_all | solution.py:41
  504.2 44.3 %reduce-scatter.11.cloned.1.call-start = ((), (), s32[]{:S(2)}) async-start(), calls=%async_computation.28 | async-start | bytes 860160 | tf_op jit(solution)/shard_map/reduce_scatter | solution.py:851
  512.5 28.6 %collective-permute-start.32 = (bf16[112,512]{1,0:T(8,128)(2,1)S(1)}, bf16[112,512]{1,0:T(8,128)(2,1)S(1)}, u32[]{:S(2)}, u32[]{:S(2)}) collective-permute-start(bf16[112,512]{1,0:T(8,128)(2,1)S(1)} %get-tuple-element.276), channel_id=1, source_target_pairs={{0,32},{16,48},{32,0},{48,16},{1,33},{17,49},{33,1},{49,17},{2,34}... | collective-permute-start | bytes 344072 | tf_op jit(solution)/shard_map/ppermute | solution.py:447
  515.3 25.8 %collective-permute-start.33 = (bf16[112,512]{1,0:T(8,128)(2,1)S(1)}, bf16[112,512]{1,0:T(8,128)(2,1)S(1)}, u32[]{:S(2)}, u32[]{:S(2)}) collective-permute-start(bf16[112,512]{1,0:T(8,128)(2,1)S(1)} %get-tuple-element.275), channel_id=1, source_target_pairs={{0,48},{16,0},{32,16},{48,32},{1,49},{17,1},{33,17},{49,33},{2,50}... | collective-permute-start | bytes 344072 | tf_op jit(solution)/shard_map/ppermute | solution.py:447
  524.0 19.6 %collective-permute-start.37 = (bf16[96,384]{1,0:T(8,128)(2,1)S(1)}, bf16[96,384]{1,0:T(8,128)(2,1)S(1)}, u32[]{:S(2)}, u32[]{:S(2)}) collective-permute-start(bf16[96,384]{1,0:T(8,128)(2,1)S(1)} %get-tuple-element.285), channel_id=1, source_target_pairs={{0,4},{4,8},{8,12},{12,0},{1,5},{5,9},{9,13},{13,1},{2,6},{6,10},{... | collective-permute-start | bytes 221192 | tf_op jit(solution)/shard_map/ppermute | solution.py:447
  525.4 19.4 %collective-permute-start.38 = (bf16[96,384]{1,0:T(8,128)(2,1)S(1)}, bf16[96,384]{1,0:T(8,128)(2,1)S(1)}, u32[]{:S(2)}, u32[]{:S(2)}) collective-permute-start(bf16[96,384]{1,0:T(8,128)(2,1)S(1)} %get-tuple-element.287), channel_id=1, source_target_pairs={{0,8},{4,12},{8,0},{12,4},{1,9},{5,13},{9,1},{13,5},{2,10},{6,14},... | collective-permute-start | bytes 221192 | tf_op jit(solution)/shard_map/ppermute | solution.py:447
  527.8 17.0 %collective-permute-start.39 = (bf16[96,384]{1,0:T(8,128)(2,1)S(1)}, bf16[96,384]{1,0:T(8,128)(2,1)S(1)}, u32[]{:S(2)}, u32[]{:S(2)}) collective-permute-start(bf16[96,384]{1,0:T(8,128)(2,1)S(1)} %get-tuple-element.286), channel_id=1, source_target_pairs={{0,12},{4,0},{8,4},{12,8},{1,13},{5,1},{9,5},{13,9},{2,14},{6,2},{... | collective-permute-start | bytes 221192 | tf_op jit(solution)/shard_map/ppermute | solution.py:447
  (95 other events, 909.5 us)
Sparse Core Ops, SparseCore 0:
  69.9 64.6 all-gather.3
  322.0 61.0 reduce-scatter.4
  511.2 34.8 reduce-scatter.10
Sparse Core Ops, SparseCore 1:
  138.8 50.1 all-gather.5
  190.5 62.6 all-gather.7
  393.7 33.4 reduce-scatter.6
  430.5 62.0 reduce-scatter.8

commit v7 on v6

--- a/solution.py
+++ b/solution.py
@@ -551,7 +551,8 @@
 def scatter_blocks(blocks, axis, last):
     here = lax.axis_index(axis)
     own, *others = (lax.dynamic_index_in_dim(blocks, lax.rem(here + j, 4), 0, keepdims=False) for j in range(4))
-    return summed([own] + [after(shifted(other, axis, j + 1), last) for j, other in enumerate(others)])
+    moved = [shifted(other, axis, j + 1) for j, other in enumerate(others)]
+    return summed([own] + (moved if last is None else after(moved, last)))
 
 
 def after_heads_kernel(pieces, xin, gain, mixed, second):
@@ -845,13 +846,14 @@
     ffn_sum = exchange(after(ffn_payload, qkv_parts), ("s", "z"))
     halfway = summed(qkv_parts)
     out_parts = sent(after(parts[1], ffn_payload), "y")
-    qkv_one = scatter_blocks(halfway, "y", ffn_sum)
+    qkv_one = scatter_blocks(halfway, "y", None)
     out_one_grad = scatter_blocks(summed(out_parts), "z", ffn_sum)
     attn_one = jnp.concatenate([qkv_one, jnp.pad(out_one_grad, ((0, 16), (0, 0)))], axis=1)
     attn_two = lax.psum_scatter(after(attn_two, (ffn_one, grad_one, halfway)), "z", scatter_dimension=0, tiled=True)
 
     grad_gate, grad_up, grad_down = unpack(ffn_sum)
-    given = swap(jnp.concatenate([pick(attn_two, attn_one[:96]), attn_one[96:]], axis=0), "s").astype(F32)
+    leaving = jnp.concatenate([pick(attn_two, attn_one[:96]), attn_one[96:]], axis=0)
+    given = swap(leaving, "s").astype(F32)
     main = pick(attn_one[:96], attn_two).astype(F32) + given[:96]
     row = pick(attn_one[96], attn_one[98]).astype(F32) + pick(given[96], given[98])
     gains = pick(attn_one[97], attn_one[99]).astype(F32) + pick(given[97], given[99])
@@ -877,7 +879,7 @@
     grad_b_keyval = lax.dynamic_slice_in_dim(kv_bias_row, (lax.axis_index("z") * 4 + member) * 8, 8, 0)
 
     firsts, seconds = jnp.stack([out_one, grad_one]), jnp.stack([out_two, grad_two])
-    given = swap(after(pick(seconds, firsts), ffn_sum), "s")
+    given = swap(after(pick(seconds, firsts), leaving), "s")
     rows = jnp.stack([pick(firsts, given), pick(given, seconds)], axis=1)[:, None]
     section_out, input_grad = rows[0], rows[1]
 

time: 581 us -> 581 us (level)
  waiting for transfers between devices: 128 us -> 135 us
    ppermute x24, waiting for transfers between devices: 32.2 us -> 47.7 us  [shifted(): return lax.ppermute(value, axis, [(i, (i + steps) % 4) for i in range(4)])]
    all_to_all x11, waiting for transfers between devices: 73.6 us -> 61.5 us  [exchange(): return lax.all_to_all(value, axes, split_axis=0, concat_axis=0, tiled=True)]
    unnamed x118 -> x116, local copies, waits for them, and re-layouts: 21.8 us -> 20.3 us
  transfers between devices with their start and end apart: 62 -> 62, of which waited for: 29 -> 30; matrix products, arithmetic and copies ran while one was open for 4% -> 4% of each run, Pallas kernels for 16% -> 16%
where the time goes in v7:
time: 581 us; the launch traced here: 573 us
  blocking collectives  149 us (26%)
  waiting for transfers between devices  135 us (23%)
  starting transfers between devices  123 us (21%)
  Pallas kernels  106 us (18%)
  local copies, waits for them, and re-layouts  28.4 us (5%)
  between operations  16.8 us (3%)
  other arithmetic  14.5 us (2%)
    all_to_all x7, blocking collectives, exchange(): return lax.all_to_all(value, axes, split_axis=0, concat_axis=0, tiled=True)  124 us
    pallas_call x28, Pallas kernels, call(): pl.pallas_call(kernel, out_shape=out_shape, in_specs=in_specs, scratch_sh...  106 us
    all_to_all x11, waiting for transfers between devices, exchange(): return lax.all_to_all(value, axes, split_axis=0, concat_axis=0, tiled=True)  61.5 us
    all_to_all x11, starting transfers between devices, exchange(): return lax.all_to_all(value, axes, split_axis=0, concat_axis=0, tiled=True)  54.9 us
    ppermute x24, waiting for transfers between devices, shifted(): return lax.ppermute(value, axis, [(i, (i + steps) % 4) for i in range(4)])  47.7 us
    ppermute x24, starting transfers between devices, shifted(): return lax.ppermute(value, axis, [(i, (i + steps) % 4) for i in range(4)])  39.4 us
    all_gather x3, blocking collectives, gathered(): return lax.all_gather(piece, axes, axis=0, tiled=True)  24.8 us
    ppermute x17, starting transfers between devices, swap(): return lax.ppermute(value, axis, [(0, 1), (1, 0)])  24.3 us
  transfers between devices with their start and end apart: 62, of which 30 were waited for; matrix products, arithmetic and copies ran while one was open for 4% of the time, Pallas kernels for 16%

profile of v7, /device:TPU:1, one launch (start us, length us, event | category | flops | bytes accessed | tf_op | source)
XLA Modules:
  0.0 573.2 jit_solution(10930111360230470245)
XLA Ops:
  25.4 7.7 %all-to-all-start.1 = ((bf16[8,96,1792]{2,1,0:T(8,128)(2,1)}), bf16[8,96,1792]{2,1,0:T(8,128)(2,1)}, u32[]{:S(2)}, u32[]{:S(2)}) async-start(bf16[8,96,1792]{2,1,0:T(8,128)(2,1)} %shard_map.220), calls=%async_computation.1 | async-start | bytes 5505024 | tf_op jit(solution)/shard_map/all_to_all | solution.py:41
  47.1 19.3 %all-to-all-done.1.pieces = bf16[8,96,1792]{2,1,0:T(8,128)(2,1)} async-done(((bf16[8,96,1792]{2,1,0:T(8,128)(2,1)}), bf16[8,96,1792]{2,1,0:T(8,128)(2,1)}, u32[]{:S(2)}, u32[]{:S(2)}) %all-to-all-start.1) | async-done | bytes 2752544 | tf_op jit(solution)/shard_map/all_to_all | solution.py:41
  78.8 7.2 %collective-permute-done.11.refs_3_ = bf16[4,112,512]{2,1,0:T(8,128)(2,1)S(1)} collective-permute-done((bf16[4,112,512]{2,1,0:T(8,128)(2,1)S(1)}, bf16[4,112,512]{2,1,0:T(8,128)(2,1)S(1)}, u32[]{:S(2)}, u32[]{:S(2)}) %collective-permute-start.11) | collective-permute-done | bytes 458784 | tf_op jit(solution)/shard_map/ppermute | solution.py:447
  89.5 8.3 %collective-permute-start.13 = (bf16[4,96,384]{2,1,0:T(8,128)(2,1)S(1)}, bf16[4,96,384]{2,1,0:T(8,128)(2,1)S(1)}, u32[]{:S(2)}, u32[]{:S(2)}) collective-permute-start(bf16[4,96,384]{2,1,0:T(8,128)(2,1)S(1)} %pad_maximum_fusion.3.refs_0_), channel_id=1, source_target_pairs={{0,12},{4,0},{8,4},{12,8},{1,13},{5,1},{9,5},{13,9},{2,14},{6,2},{... | collective-permute-start | bytes 884744 | tf_op jit(solution)/shard_map/ppermute | solution.py:447
  149.3 27.6 %all_to_all.90 = bf16[8,32,1536]{2,1,0:T(8,128)(2,1)S(1)} all-to-all(bf16[8,32,1536]{2,1,0:T(8,128)(2,1)S(1)} %get-tuple-element.135), channel_id=1, replica_groups=mesh['s'=2,'y'=4,'z'=4,'x'=2,'c'=2] {'z','x'}, dimensions={0} | all-to-all | bytes 1572864 | tf_op jit(solution)/shard_map/all_to_all | solution.py:41
  176.9 7.3 %shard_map.227 = (bf16[256,1536]{1,0:T(8,128)(2,1)}, bf16[2,256,1152]{2,1,0:T(8,128)(2,1)}) custom-call(bf16[256,1536]{1,0:T(8,128)(2,1)S(1)} %bitcast.132, bf16[1536,1792]{1,0:T(8,128)(2,1)} %all-gather.4.cloned.1.call-done.own, bf16[1536,1792]{1,0:T(8,128)(2,1)} %collective-permute-done.16.other), custom_call_target="tpu_custom_call" | custom-call | flops 3019898880 | bytes 15000000 | tf_op jit(solution)/shard_map/pallas_call | solution.py:65
  190.6 9.6 %all-to-all-done.5.pieces = bf16[8,32,1536]{2,1,0:T(8,128)(2,1)S(1)} async-done(((bf16[8,32,1536]{2,1,0:T(8,128)(2,1)}), bf16[8,32,1536]{2,1,0:T(8,128)(2,1)S(1)}, u32[]{:S(2)}, u32[]{:S(2)}) %all-to-all-start.5) | async-done | bytes 786464 | tf_op jit(solution)/shard_map/all_to_all | solution.py:41
  200.3 10.0 %all_gather.19.xin = bf16[128,1536]{1,0:T(8,128)(2,1)S(1)} all-gather(bf16[32,1536]{1,0:T(8,128)(2,1)S(1)} %shard_map.228.xin), channel_id=1, replica_groups=mesh['s'=2,'y'=4,'z'=4,'x'=2,'c'=2] {'x','c'}, dimensions={0}, use_global_device_ids=true | all-gather | bytes 491520 | tf_op jit(solution)/shard_map/all_gather | solution.py:703
  212.7 17.3 %all_to_all.91 = bf16[16,128,128]{2,1,0:T(8,128)(2,1)S(1)} all-to-all(bf16[16,128,128]{2,1,0:T(8,128)(2,1)S(1)} %get-tuple-element.142), channel_id=1, replica_groups=mesh['s'=2,'y'=4,'z'=4,'x'=2,'c'=2] {'y','z'}, dimensions={0} | all-to-all | bytes 1048576 | tf_op jit(solution)/shard_map/all_to_all | solution.py:41
  251.4 16.1 %all_to_all.92 = bf16[8,32,1536]{2,1,0:T(8,128)(2,1)S(1)} all-to-all(bf16[8,32,1536]{2,1,0:T(8,128)(2,1)S(1)} %get-tuple-element.146), channel_id=1, replica_groups=mesh['s'=2,'y'=4,'z'=4,'x'=2,'c'=2] {'z','x'}, dimensions={0} | all-to-all | bytes 1572864 | tf_op jit(solution)/shard_map/all_to_all | solution.py:41
  269.5 15.2 %all_to_all.93 = bf16[8,32,1536]{2,1,0:T(8,128)(2,1)S(1)} all-to-all(bf16[8,32,1536]{2,1,0:T(8,128)(2,1)S(1)} %broadcast_in_dim.71), channel_id=1, replica_groups=mesh['s'=2,'y'=4,'z'=4,'x'=2,'c'=2] {'z','x'}, dimensions={0} | all-to-all | bytes 1572864 | tf_op jit(solution)/shard_map/all_to_all | solution.py:41
  287.1 10.8 %shard_map.232 = (bf16[8,64,1536]{2,1,0:T(8,128)(2,1)}, bf16[256,1792]{1,0:T(8,128)(2,1)}, bf16[256,1792]{1,0:T(8,128)(2,1)}) custom-call(bf16[256,1536]{1,0:T(8,128)(2,1)S(1)} %bitcast.147, bf16[256,1536]{1,0:T(8,128)(2,1)S(1)} %bitcast.150, bf16[1536,1792]{1,0:T(8,128)(2,1)} %all-gather.8.cloned.1.call-done.own, bf16[1536,1792]{1,0:T(8,128)(2,1)} %copy-done.53), custom_call_target="tpu_custom_call" | custom-call | flops 6039797760 | bytes 17000000 | tf_op jit(solution)/shard_map/pallas_call | solution.py:65
  309.6 8.2 %shard_map.233 = bf16[1536,1792]{1,0:T(8,128)(2,1)} custom-call(bf16[256,1536]{1,0:T(8,128)(2,1)S(1)} %bitcast.149, bf16[256,1536]{1,0:T(8,128)(2,1)S(1)} %collective-permute-done.19.tokens_other, bf16[256,1536]{1,0:T(8,128)(2,1)} %bitcast.152, bf16[256,1536]{1,0:T(8,128)(2,1)} %copy-done.55, bf16[256,1792]{1,0:T(8,128)(2,1)} %get-tuple-element.153.own, ...), custom_call_target="tpu_custom_call" | custom-call | flops 3019898880 | bytes 12000000 | tf_op jit(solution)/shard_map/pallas_call | solution.py:65
  324.7 7.9 %all_gather.22.grad_att = bf16[128,1536]{1,0:T(8,128)(2,1)S(1)} all-gather(bf16[32,1536]{1,0:T(8,128)(2,1)S(1)} %get-tuple-element.157), channel_id=1, replica_groups=mesh['s'=2,'y'=4,'z'=4,'x'=2,'c'=2] {'x','c'}, dimensions={0}, use_global_device_ids=true | all-gather | bytes 491520 | tf_op jit(solution)/shard_map/all_gather | solution.py:703
  334.5 7.1 %shard_map.235 = (bf16[128,384]{1,0:T(8,128)(2,1)S(1)}, f32[2048,128]{1,0:T(8,128)}, bf16[2048,128]{1,0:T(8,128)(2,1)S(1)}) custom-call(s32[2]{0:T(128)S(1)} %pad_add_fusion.flag, bf16[3,128,128]{2,1,0:T(8,128)(2,1)S(1)} %copy-done.20, bf16[2048,128]{1,0:T(8,128)(2,1)S(1)} %bitcast.129, bf16[2048,128]{1,0:T(8,128)(2,1)} %copy-done.7, ...), custom_call_target="tpu_custom_call" | custom-call | flops 1157627904 | bytes 5000000 | tf_op jit(solution)/shard_map/pallas_call | solution.py:65
  345.0 18.2 %all_to_all.94.pieces = bf16[16,128,128]{2,1,0:T(8,128)(2,1)S(1)} all-to-all(bf16[16,128,128]{2,1,0:T(8,128)(2,1)S(1)} %bitcast.161), channel_id=1, replica_groups=mesh['s'=2,'y'=4,'z'=4,'x'=2,'c'=2] {'y','z'}, dimensions={0} | all-to-all | bytes 1048576 | tf_op jit(solution)/shard_map/all_to_all | solution.py:41
  366.0 10.5 %all_to_all.95.pieces = bf16[4,32,1536]{2,1,0:T(8,128)(2,1)S(1)} all-to-all(bf16[4,32,1536]{2,1,0:T(8,128)(2,1)S(1)} %get-tuple-element.161), channel_id=1, replica_groups=mesh['s'=2,'y'=4,'z'=4,'x'=2,'c'=2] {'x','c'}, dimensions={0} | all-to-all | bytes 786432 | tf_op jit(solution)/shard_map/all_to_all | solution.py:41
  384.9 8.7 %all-to-all-done.13 = bf16[8,32,1536]{2,1,0:T(8,128)(2,1)S(1)} async-done(((bf16[8,32,1536]{2,1,0:T(8,128)(2,1)}), bf16[8,32,1536]{2,1,0:T(8,128)(2,1)S(1)}, u32[]{:S(2)}, u32[]{:S(2)}) %all-to-all-start.13) | async-done | bytes 786464 | tf_op jit(solution)/shard_map/all_to_all | solution.py:41
  393.7 8.5 %shard_map.239 = (bf16[256,1536]{1,0:T(8,128)(2,1)}, bf16[256,1792]{1,0:T(8,128)(2,1)}, bf16[256,1792]{1,0:T(8,128)(2,1)}) custom-call(bf16[256,1536]{1,0:T(8,128)(2,1)S(1)} %bitcast.135, bf16[1536,1792]{1,0:T(8,128)(2,1)} %all-gather.4.cloned.1.call-done.own, bf16[1536,1792]{1,0:T(8,128)(2,1)} %collective-permute-done.16.other, ...), custom_call_target="tpu_custom_call" | custom-call | flops 3019898880 | bytes 17000000 | tf_op jit(solution)/shard_map/pallas_call | solution.py:65
  411.2 8.3 %shard_map.240 = bf16[1536,1792]{1,0:T(8,128)(2,1)} custom-call(bf16[256,1536]{1,0:T(8,128)(2,1)S(1)} %bitcast.134, bf16[256,1536]{1,0:T(8,128)(2,1)S(1)} %copy-done.28, bf16[256,1536]{1,0:T(8,128)(2,1)} %bitcast.137, bf16[256,1536]{1,0:T(8,128)(2,1)} %collective-permute-done.24.grads_other, bf16[256,1792]{1,0:T(8,128)(2,1)} %get-tuple-element.170.own, ...), custom_call_target="tpu_custom_call" | custom-call | flops 3019898880 | bytes 12000000 | tf_op jit(solution)/shard_map/pallas_call | solution.py:65
  431.6 7.1 %shard_map.242 = (bf16[128,384]{1,0:T(8,128)(2,1)S(1)}, f32[2048,128]{1,0:T(8,128)}, bf16[2048,128]{1,0:T(8,128)(2,1)S(1)}) custom-call(s32[2]{0:T(128)S(1)} %pad_add_fusion.flag, bf16[3,128,128]{2,1,0:T(8,128)(2,1)S(1)} %copy-done.24, bf16[2048,128]{1,0:T(8,128)(2,1)S(1)} %bitcast.141, bf16[2048,128]{1,0:T(8,128)(2,1)} %copy-done.15, ...), custom_call_target="tpu_custom_call" | custom-call | flops 1157627904 | bytes 5000000 | tf_op jit(solution)/shard_map/pallas_call | solution.py:65
  442.1 19.2 %all_to_all.96.pieces = bf16[16,128,128]{2,1,0:T(8,128)(2,1)S(1)} all-to-all(bf16[16,128,128]{2,1,0:T(8,128)(2,1)S(1)} %bitcast.162), channel_id=1, replica_groups=mesh['s'=2,'y'=4,'z'=4,'x'=2,'c'=2] {'y','z'}, dimensions={0} | all-to-all | bytes 1048576 | tf_op jit(solution)/shard_map/all_to_all | solution.py:41
  483.0 9.6 %reduce-scatter.9.cloned.1.call-done = bf16[384,1792]{1,0:T(8,128)(2,1)} async-done(((bf16[1536,1792]{1,0:T(8,128)(2,1)}), bf16[384,1792]{1,0:T(8,128)(2,1)}) %reduce-scatter.9.cloned.1.call-update) | async-done | bytes 1376272 | tf_op jit(solution)/shard_map/reduce_scatter | solution.py:811
  527.9 13.6 %collective-permute-done.36 = bf16[96,384]{1,0:T(8,128)(2,1)S(1)} collective-permute-done((bf16[96,384]{1,0:T(8,128)(2,1)S(1)}, bf16[96,384]{1,0:T(8,128)(2,1)S(1)}, u32[]{:S(2)}, u32[]{:S(2)}) %collective-permute-start.36) | collective-permute-done | bytes 73760 | tf_op jit(solution)/shard_map/ppermute | solution.py:447
  (373 shorter events, 273.1 us)
Async XLA Ops:
  25.4 41.0 %all-to-all-start.1 = ((bf16[8,96,1792]{2,1,0:T(8,128)(2,1)}), bf16[8,96,1792]{2,1,0:T(8,128)(2,1)}, u32[]{:S(2)}, u32[]{:S(2)}) async-start(bf16[8,96,1792]{2,1,0:T(8,128)(2,1)} %shard_map.220), calls=%async_computation.1 | async-start | bytes 5505024 | tf_op jit(solution)/shard_map/all_to_all | solution.py:41
  33.1 105.5 %all-gather.4.cloned.1.call-start = ((), (), s32[]{:S(2)}) async-start(), calls=%async_computation.22 | async-start | bytes 6881280 | tf_op jit(solution)/shard_map/all_gather | solution.py:703
  75.9 21.9 %collective-permute-start.10 = (bf16[4,112,512]{2,1,0:T(8,128)(2,1)S(1)}, bf16[4,112,512]{2,1,0:T(8,128)(2,1)S(1)}, u32[]{:S(2)}, u32[]{:S(2)}) collective-permute-start(bf16[4,112,512]{2,1,0:T(8,128)(2,1)S(1)} %pad_maximum_fusion.1.refs_0_), channel_id=1, source_target_pairs={{0,8},{4,12},{8,0},{12,4},{1,9},{5,13},{9,1},{13,5},{2,10},{6,14},... | collective-permute-start | bytes 1376264 | tf_op jit(solution)/shard_map/ppermute | solution.py:447
  104.6 18.4 %all-to-all-start.2 = ((bf16[16,128,128]{2,1,0:T(8,128)(2,1)}), bf16[16,128,128]{2,1,0:T(8,128)(2,1)S(1)}, u32[]{:S(2)}, u32[]{:S(2)}) async-start(bf16[16,128,128]{2,1,0:T(8,128)(2,1)} %get-tuple-element.125), calls=%async_computation.2 | async-start | bytes 1048576 | tf_op jit(solution)/shard_map/all_to_all | solution.py:41
  109.9 100.3 %all-gather.6.cloned.1.call-start = ((), (), s32[]{:S(2)}) async-start(), calls=%async_computation.23 | async-start | bytes 2924544 | tf_op jit(solution)/shard_map/all_gather | solution.py:703
  142.5 125.0 %all-gather.8.cloned.1.call-start = ((), (), s32[]{:S(2)}) async-start(), calls=%async_computation.24 | async-start | bytes 6881280 | tf_op jit(solution)/shard_map/all_gather | solution.py:703
  267.5 17.2 %collective-permute-start.18 = (bf16[1536,1792]{1,0:T(8,128)(2,1)}, bf16[1536,1792]{1,0:T(8,128)(2,1)S(1)}, u32[]{:S(2)}, u32[]{:S(2)}) collective-permute-start(bf16[1536,1792]{1,0:T(8,128)(2,1)} %all-gather.8.cloned.1.call-done.own), channel_id=1, source_target_pairs={{0,1},{1,0},{2,3},{3,2},{4,5},{5,4},{6,7},{7,6},{8,9},{9,8},{10,11... | collective-permute-start | bytes 16515080 | tf_op jit(solution)/shard_map/ppermute | solution.py:37
  297.9 23.9 %all-to-all-start.10 = ((bf16[8,64,1536]{2,1,0:T(8,128)(2,1)}), bf16[8,64,1536]{2,1,0:T(8,128)(2,1)S(1)}, u32[]{:S(2)}, u32[]{:S(2)}) async-start(bf16[8,64,1536]{2,1,0:T(8,128)(2,1)} %get-tuple-element.152), calls=%async_computation.10 | async-start | bytes 3145728 | tf_op jit(solution)/shard_map/all_to_all | solution.py:41
  301.5 92.1 %reduce-scatter.5.cloned.1.call-start = ((), (), s32[]{:S(2)}) async-start(), calls=%async_computation.25 | async-start | bytes 6881280 | tf_op jit(solution)/shard_map/reduce_scatter | solution.py:811
  377.7 16.0 %all-to-all-start.13 = ((bf16[8,32,1536]{2,1,0:T(8,128)(2,1)}), bf16[8,32,1536]{2,1,0:T(8,128)(2,1)S(1)}, u32[]{:S(2)}, u32[]{:S(2)}) async-start(bf16[8,32,1536]{2,1,0:T(8,128)(2,1)} %get-tuple-element.163), calls=%async_computation.13 | async-start | bytes 1572864 | tf_op jit(solution)/shard_map/all_to_all | solution.py:41
  381.9 48.5 %reduce-scatter.7.cloned.1.call-start = ((), (), s32[]{:S(2)}) async-start(), calls=%async_computation.26 | async-start | bytes 3440640 | tf_op jit(solution)/shard_map/reduce_scatter | solution.py:838
  404.9 17.3 %all-to-all-start.14 = ((bf16[8,32,1536]{2,1,0:T(8,128)(2,1)}), bf16[8,32,1536]{2,1,0:T(8,128)(2,1)}, u32[]{:S(2)}, u32[]{:S(2)}) async-start(bf16[8,32,1536]{2,1,0:T(8,128)(2,1)} %bitcast.49), calls=%async_computation.14 | async-start | bytes 1572864 | tf_op jit(solution)/shard_map/all_to_all | solution.py:41
  409.1 83.5 %reduce-scatter.9.cloned.1.call-start = ((), (), s32[]{:S(2)}) async-start(), calls=%async_computation.27 | async-start | bytes 6881280 | tf_op jit(solution)/shard_map/reduce_scatter | solution.py:811
  472.0 23.7 %collective-permute-start.27 = (bf16[4,112,512]{2,1,0:T(8,128)(2,1)}, bf16[4,112,512]{2,1,0:T(8,128)(2,1)}, u32[]{:S(2)}, u32[]{:S(2)}) collective-permute-start(bf16[4,112,512]{2,1,0:T(8,128)(2,1)} %get-tuple-element.189), channel_id=1, source_target_pairs={{0,4},{4,8},{8,12},{12,0},{1,5},{5,9},{9,13},{13,1},{2,6},{6,10},{... | collective-permute-start | bytes 1376264 | tf_op jit(solution)/shard_map/ppermute | solution.py:447
  472.2 23.4 %collective-permute-start.28 = (bf16[4,112,512]{2,1,0:T(8,128)(2,1)}, bf16[4,112,512]{2,1,0:T(8,128)(2,1)}, u32[]{:S(2)}, u32[]{:S(2)}) collective-permute-start(bf16[4,112,512]{2,1,0:T(8,128)(2,1)} %get-tuple-element.190), channel_id=1, source_target_pairs={{0,8},{4,12},{8,0},{12,4},{1,9},{5,13},{9,1},{13,5},{2,10},{6,14},... | collective-permute-start | bytes 1376264 | tf_op jit(solution)/shard_map/ppermute | solution.py:447
  476.1 19.5 %collective-permute-start.29 = (bf16[4,112,512]{2,1,0:T(8,128)(2,1)}, bf16[4,112,512]{2,1,0:T(8,128)(2,1)}, u32[]{:S(2)}, u32[]{:S(2)}) collective-permute-start(bf16[4,112,512]{2,1,0:T(8,128)(2,1)} %get-tuple-element.191), channel_id=1, source_target_pairs={{0,12},{4,0},{8,4},{12,8},{1,13},{5,1},{9,5},{13,9},{2,14},{6,2},{... | collective-permute-start | bytes 1376264 | tf_op jit(solution)/shard_map/ppermute | solution.py:447
  477.4 18.3 %all-to-all-start.16 = ((bf16[4,32,1536]{2,1,0:T(8,128)(2,1)}), bf16[4,32,1536]{2,1,0:T(8,128)(2,1)S(1)}, u32[]{:S(2)}, u32[]{:S(2)}) async-start(bf16[4,32,1536]{2,1,0:T(8,128)(2,1)} %get-tuple-element.196), calls=%async_computation.16 | async-start | bytes 786432 | tf_op jit(solution)/shard_map/all_to_all | solution.py:41
  495.7 47.4 %all-to-all-start.17 = ((bf16[8,96,1792]{2,1,0:T(8,128)(2,1)}), bf16[8,96,1792]{2,1,0:T(8,128)(2,1)}, u32[]{:S(2)}, u32[]{:S(2)}) async-start(bf16[8,96,1792]{2,1,0:T(8,128)(2,1)} %bitcast.159), calls=%async_computation.21 | async-start | bytes 5505024 | tf_op jit(solution)/shard_map/all_to_all | solution.py:41
  502.3 42.1 %reduce-scatter.11.cloned.1.call-start = ((), (), s32[]{:S(2)}) async-start(), calls=%async_computation.28 | async-start | bytes 860160 | tf_op jit(solution)/shard_map/reduce_scatter | solution.py:852
  508.8 17.8 %collective-permute-start.30 = (bf16[112,512]{1,0:T(8,128)(2,1)S(1)}, bf16[112,512]{1,0:T(8,128)(2,1)S(1)}, u32[]{:S(2)}, u32[]{:S(2)}) collective-permute-start(bf16[112,512]{1,0:T(8,128)(2,1)S(1)} %get-tuple-element.268), channel_id=1, source_target_pairs={{0,16},{16,32},{32,48},{48,0},{1,17},{17,33},{33,49},{49,1},{2,18}... | collective-permute-start | bytes 344072 | tf_op jit(solution)/shard_map/ppermute | solution.py:447
  509.9 17.9 %collective-permute-start.31 = (bf16[112,512]{1,0:T(8,128)(2,1)S(1)}, bf16[112,512]{1,0:T(8,128)(2,1)S(1)}, u32[]{:S(2)}, u32[]{:S(2)}) collective-permute-start(bf16[112,512]{1,0:T(8,128)(2,1)S(1)} %get-tuple-element.270), channel_id=1, source_target_pairs={{0,32},{16,48},{32,0},{48,16},{1,33},{17,49},{33,1},{49,17},{2,34}... | collective-permute-start | bytes 344072 | tf_op jit(solution)/shard_map/ppermute | solution.py:447
  522.8 18.7 %collective-permute-start.36 = (bf16[96,384]{1,0:T(8,128)(2,1)S(1)}, bf16[96,384]{1,0:T(8,128)(2,1)S(1)}, u32[]{:S(2)}, u32[]{:S(2)}) collective-permute-start(bf16[96,384]{1,0:T(8,128)(2,1)S(1)} %get-tuple-element.281), channel_id=1, source_target_pairs={{0,4},{4,8},{8,12},{12,0},{1,5},{5,9},{9,13},{13,1},{2,6},{6,10},{... | collective-permute-start | bytes 221192 | tf_op jit(solution)/shard_map/ppermute | solution.py:447
  524.3 18.8 %collective-permute-start.37 = (bf16[96,384]{1,0:T(8,128)(2,1)S(1)}, bf16[96,384]{1,0:T(8,128)(2,1)S(1)}, u32[]{:S(2)}, u32[]{:S(2)}) collective-permute-start(bf16[96,384]{1,0:T(8,128)(2,1)S(1)} %get-tuple-element.280), channel_id=1, source_target_pairs={{0,8},{4,12},{8,0},{12,4},{1,9},{5,13},{9,1},{13,5},{2,10},{6,14},... | collective-permute-start | bytes 221192 | tf_op jit(solution)/shard_map/ppermute | solution.py:447
  526.7 16.4 %collective-permute-start.38 = (bf16[96,384]{1,0:T(8,128)(2,1)S(1)}, bf16[96,384]{1,0:T(8,128)(2,1)S(1)}, u32[]{:S(2)}, u32[]{:S(2)}) collective-permute-start(bf16[96,384]{1,0:T(8,128)(2,1)S(1)} %get-tuple-element.279), channel_id=1, source_target_pairs={{0,12},{4,0},{8,4},{12,8},{1,13},{5,1},{9,5},{13,9},{2,14},{6,2},{... | collective-permute-start | bytes 221192 | tf_op jit(solution)/shard_map/ppermute | solution.py:447
  (94 other events, 948.6 us)
Sparse Core Ops, SparseCore 0:
  69.9 64.6 all-gather.3
  322.0 61.0 reduce-scatter.4
  505.5 38.8 reduce-scatter.10
Sparse Core Ops, SparseCore 1:
  138.9 50.1 all-gather.5
  190.5 62.6 all-gather.7
  393.7 33.4 reduce-scatter.6
  430.5 62.0 reduce-scatter.8
